TPU v7x, 128 devices: a whole 4x4x4 slice. The times are simulated.
128 devices in a mesh: rep: 16 (over x, y_hi, core), tp: 8 (over z, y_lo).
Axes of the slice: x: 4, y: 4 (y_hi: 2, y_lo: 2; y = y_hi * 2 + y_lo), z: 4, core: 2. Of those that a mesh axis runs over, the one named last changes fastest.
Arguments:
- new_tokens: bfloat16 [4, 256, 8192], P(None, 'rep'), may hold values from -6 to 6
- norm_gain: bfloat16 [8192], replicated, may hold values from 0.099609375 to 1.8984375
- w_query: bfloat16 [8192, 8192], P('rep', 'tp'), may hold values from -0.0625 to 0.0625
- w_keyval: bfloat16 [8192, 2, 1024], P('rep', None, 'tp'), may hold values from -0.0625 to 0.0625
- w_output: bfloat16 [8192, 8192], P('tp', 'rep'), may hold values from -0.5 to 0.5
- kv_cache: bfloat16 [256, 2, 768, 1024], P('rep', None, None, 'tp'), may hold values from -200 to 200
- block_counts: int32 [256], P('rep'), may hold values from 1 to 6, 512 in all
- new_slot: int32 [256], P('rep'), may hold values from 0 to 255, as said below
Outputs:
- layer_out: bfloat16 [4, 256, 8192], P(None, 'rep', 'tp')
- cache_moved: bfloat16 [256, 2, 768, 1024], P('rep', None, None, 'tp')
Inputs may be any that keep to these rules, and one draw needn't show every extreme that they name: new_slot is a permutation of the 256 slots; the request in old slot o goes to new replica new_slot[o] // 16; the 16 requests of each old replica (aligned blocks of 16 old slots) go to 8 new replicas, exactly 2 to each.
All inputs are finite; a program needn't handle non-finite values. No bound on the sum of `block_counts` on one device may be relied on, other than what follows from the above.
Results may differ from a plain program's by a relative error of at most 0.019.
Values may be sent and summed in bfloat16 or wider, within the bound.
No kernel may reach another device: no remote copies, remote signals or barrier semaphores. Data moves between devices by JAX's collectives and lax.ppermute only.
A program may use at most 192 MiB of HBM per device.

v0:
```python
import jax
import jax.numpy as jnp
from jax import lax
from jax.sharding import PartitionSpec as P

HEADDIM = 128
BLOCK = 128
CAP = 2


def per_device(
    new_tokens, norm_gain, w_query, w_keyval, w_output, kv_cache, block_counts, new_slot
):
    rep_count = lax.axis_size("rep")
    rep_index = lax.axis_index("rep")
    num_steps, num_rows, feat_width = new_tokens.shape
    head_cols = w_query.shape[1]
    pair_cols = w_keyval.shape[2]
    kv_local = pair_cols // HEADDIM
    group = head_cols // pair_cols
    row_total = num_steps * num_rows
    inputs_f = new_tokens.astype(jnp.float32)
    inverse = lax.rsqrt(jnp.mean(inputs_f * inputs_f, axis=-1, keepdims=True) + 1e-05)
    normed = (inputs_f * inverse * norm_gain.astype(jnp.float32)).astype(jnp.bfloat16)
    normed = normed.reshape(row_total, feat_width)
    keyval_flat = w_keyval.reshape(w_keyval.shape[0], 2 * pair_cols)
    query_sum = jnp.dot(
        normed,
        lax.all_gather(w_query, "rep", axis=0, tiled=True),
        preferred_element_type=jnp.float32,
    )
    pair_sum = jnp.dot(
        normed,
        lax.all_gather(keyval_flat, "rep", axis=0, tiled=True),
        preferred_element_type=jnp.float32,
    )
    slot_table, length_table = (
        lax.all_gather(new_slot, "rep", axis=0, tiled=True),
        lax.all_gather(block_counts, "rep", axis=0, tiled=True),
    )
    grid_target = (slot_table // num_rows).reshape(rep_count, num_rows)
    same_target = grid_target[:, :, None] == grid_target[:, None, :]
    earlier = jnp.arange(num_rows)[None, :] < jnp.arange(num_rows)[:, None]
    position = jnp.sum(same_target & earlier[None], axis=-1)
    bucket = grid_target * CAP + position
    arrival = jnp.arange(rep_count, dtype=jnp.int32)[:, None] * CAP + position
    my_bucket = lax.dynamic_index_in_dim(bucket, rep_index, 0, keepdims=False)
    slot_hit = my_bucket[None, :] == jnp.arange(rep_count * CAP, dtype=jnp.int32)[:, None]
    source_row = jnp.sum(
        jnp.where(slot_hit, jnp.arange(num_rows, dtype=jnp.int32)[None, :], 0), axis=1
    )
    filled = jnp.any(slot_hit, axis=1)
    outgoing = jnp.where(
        filled[:, None, None, None], kv_cache[source_row], jnp.zeros((), jnp.bfloat16)
    )
    received = lax.all_to_all(outgoing, "rep", split_axis=0, concat_axis=0, tiled=True)
    my_slots = rep_index * num_rows + jnp.arange(num_rows, dtype=jnp.int32)
    slot_match = slot_table[None, :] == my_slots[:, None]
    pick_index = jnp.sum(jnp.where(slot_match, arrival.reshape(-1)[None, :], 0), axis=1)
    moved_blocks = jnp.sum(jnp.where(slot_match, length_table[None, :], 0), axis=1)
    span_len = received.shape[2]
    live = jnp.arange(span_len)[None, :] < (moved_blocks * BLOCK)[:, None]
    cache_moved = jnp.where(
        live[:, None, :, None], received[pick_index], jnp.zeros((), jnp.bfloat16)
    )
    query = query_sum.astype(jnp.bfloat16).reshape(num_steps, num_rows, kv_local, group, HEADDIM)
    fresh = pair_sum.astype(jnp.bfloat16).reshape(num_steps, num_rows, 2, kv_local, HEADDIM)
    old_keys = cache_moved[:, 0].reshape(num_rows, span_len, kv_local, HEADDIM)
    old_values = cache_moved[:, 1].reshape(num_rows, span_len, kv_local, HEADDIM)
    factor = 1.0 / HEADDIM**0.5
    cache_scores = (
        jnp.einsum("trkgd,rlkd->rkgtl", query, old_keys, preferred_element_type=jnp.float32)
        * factor
    )
    cache_scores = jnp.where(live[:, None, None, None, :], cache_scores, -1e30)
    fresh_scores = (
        jnp.einsum("trkgd,urkd->rkgtu", query, fresh[:, :, 0], preferred_element_type=jnp.float32)
        * factor
    )
    causal = jnp.arange(num_steps)[None, :] <= jnp.arange(num_steps)[:, None]
    fresh_scores = jnp.where(causal, fresh_scores, -1e30)
    peak = jnp.maximum(jnp.max(cache_scores, -1), jnp.max(fresh_scores, -1))
    cache_exp = jnp.exp(cache_scores - peak[..., None])
    fresh_exp = jnp.exp(fresh_scores - peak[..., None])
    total = jnp.sum(cache_exp, -1) + jnp.sum(fresh_exp, -1)
    cache_prob = (cache_exp / total[..., None]).astype(jnp.bfloat16)
    fresh_prob = (fresh_exp / total[..., None]).astype(jnp.bfloat16)
    mixed_heads = jnp.einsum(
        "rkgtl,rlkd->trkgd", cache_prob, old_values, preferred_element_type=jnp.float32
    )
    mixed_heads = mixed_heads + jnp.einsum(
        "rkgtu,urkd->trkgd", fresh_prob, fresh[:, :, 1], preferred_element_type=jnp.float32
    )
    attended = mixed_heads.astype(jnp.bfloat16).reshape(row_total, head_cols)
    partial_value = jnp.dot(
        attended,
        lax.all_gather(w_output, "rep", axis=1, tiled=True),
        preferred_element_type=jnp.float32,
    )
    head_total = lax.psum_scatter(
        partial_value.astype(jnp.bfloat16), "tp", scatter_dimension=1, tiled=True
    )
    layer_out = head_total.reshape(num_steps, num_rows, -1)
    return (layer_out, cache_moved)


def solution(mesh):
    placed = (
        P(None, "rep", None),
        P(),
        P("rep", "tp"),
        P("rep", None, "tp"),
        P("tp", "rep"),
        P("rep", None, None, "tp"),
        P("rep"),
        P("rep"),
    )
    return jax.shard_map(
        per_device,
        mesh=mesh,
        in_specs=placed,
        out_specs=(P(None, "rep", "tp"), P("rep", None, None, "tp")),
        check_vma=False,
    )
```

profile of v0, /device:TPU:17, one launch (start us, length us, event | category | flops | bytes accessed | tf_op | source)
XLA Modules:
  0.0 496.6 jit_solution(6567724023553185872)
XLA Ops:
  7.2 1.7 copy.58
  9.0 0.7 all-gather.4.cloned.1.call-update
  9.7 0.7 all-gather.8.cloned.1.call-update
  10.4 1.2 dynamic-slice
  12.3 0.9 dynamic-update-slice
  13.2 0.8 dynamic-update-slice.1
  14.0 10.3 %all-reduce.2 = (s32[256]{0:T(256)S(1)}, s32[256]{0:T(256)S(1)}) all-reduce(s32[256]{0:T(256)S(1)} %dynamic-update-slice, s32[256]{0:T(256)S(1)} %dynamic-update-slice.1), channel_id=1, replica_groups=mesh['rep'=16,'tp'=8] {'rep'}, use_global_device_ids=true, to_apply=%add | all-reduce | flops 512 | bytes 4096
  24.4 0.4 convert_reduce_fusion
  25.0 9.5 %gather_fusion = bf16[32,2,768,128]{3,2,1,0:T(8,128)(2,1)} fusion(bf16[16,2,768,128]{3,2,1,0:T(8,128)(2,1)} %param.13, s32[1024]{0:T(1024)S(1)} %pad_clamp_fusion.1), kind=kCustom, calls=%fused_computation | custom fusion | bytes 25165952 | tf_op jit(solution)/shard_map/gather | solution.py:54
  34.5 10.6 %broadcast_select_fusion = bf16[32,2,768,128]{3,2,1,0:T(8,128)(2,1)} fusion(bf16[32,2,768,128]{3,2,1,0:T(8,128)(2,1)} %gather_fusion, pred[32]{0:T(512)(128)(4,1)S(1)} %fusion.25), kind=kLoop, calls=%fused_computation.2 | loop fusion | flops 6291456 | bytes 25165856 | tf_op jit(solution)/shard_map/jit(_where)/select_n | solution.py:53
  45.2 9.4 %all-to-all-start = ((bf16[32,2,768,128]{3,2,1,0:T(8,128)(2,1)}), bf16[32,2,768,128]{3,2,1,0:T(8,128)(2,1)}, u32[]{:S(2)}, u32[]{:S(2)}) async-start(bf16[32,2,768,128]{3,2,1,0:T(8,128)(2,1)} %broadcast_select_fusion), calls=%async_computation | async-start | bytes 25165824 | tf_op jit(solution)/shard_map/all_to_all | solution.py:56
  54.6 0.2 reduce-scatter.2.cloned.1.call-start
  55.0 0.2 fusion.23
  55.2 0.3 fusion.2
  55.6 0.3 fusion.4
  55.9 41.5 %all-gather.6.cloned.1.call-done = bf16[8192,256]{1,0:T(8,128)(2,1)} async-done(((bf16[512,256]{1,0:T(8,128)(2,1)}), bf16[8192,256]{1,0:T(8,128)(2,1)}) %all-gather.6.cloned.1.call-update) | async-done | bytes 4194320 | tf_op jit(solution)/shard_map/all_gather | solution.py:34
  97.4 3.0 convolution_convert_fusion.2
  100.5 177.1 %all-to-all-done = bf16[32,2,768,128]{3,2,1,0:T(8,128)(2,1)} async-done(((bf16[32,2,768,128]{3,2,1,0:T(8,128)(2,1)}), bf16[32,2,768,128]{3,2,1,0:T(8,128)(2,1)}, u32[]{:S(2)}, u32[]{:S(2)}) %all-to-all-start) | async-done | bytes 12582944 | tf_op jit(solution)/shard_map/all_to_all | solution.py:56
  277.6 8.6 %gather_fusion.1 = bf16[16,2,768,128]{3,2,1,0:T(8,128)(2,1)} fusion(bf16[32,2,768,128]{3,2,1,0:T(8,128)(2,1)} %all-to-all-done, s32[1024]{0:T(1024)S(1)} %pad_clamp_fusion), kind=kCustom, calls=%fused_computation.1 | custom fusion | bytes 12582976 | tf_op jit(solution)/shard_map/gather | solution.py:64
  286.2 7.6 %copy_select_fusion = bf16[16,2,768,128]{3,2,0,1:T(8,128)(2,1)} fusion(bf16[16,2,768,128]{3,2,1,0:T(8,128)(2,1)} %gather_fusion.1, pred[16,768]{1,0:T(8,128)(4,1)S(1)} %iota_compare_fusion), kind=kLoop, calls=%fused_computation.4 | loop fusion | flops 3145728 | bytes 12595200 | tf_op jit(solution)/shard_map/jit(_where)/select_n | solution.py:63
  293.9 20.5 %all-gather.4.cloned.1.call-done = bf16[8192,1024]{1,0:T(8,128)(2,1)} async-done(((bf16[512,1024]{1,0:T(8,128)(2,1)}), bf16[8192,1024]{1,0:T(8,128)(2,1)}) %all-gather.4.cloned.1.call-update) | async-done | bytes 16777232 | tf_op jit(solution)/shard_map/all_gather | solution.py:29
  314.4 8.9 %fusion.10 = bf16[8,8,8,128]{3,1,2,0:T(8,128)(2,1)S(1)} fusion(bf16[64,8192]{1,0:T(8,128)(2,1)S(1)} %bitcast.113, bf16[8192,1024]{1,0:T(8,128)(2,1)} %all-gather.4.cloned.1.call-done), kind=kOutput, calls=%fused_computation.25 | convolution fusion | flops 1073807360 | bytes 17956864 | tf_op jit(solution)/shard_map/dot_general | solution.py:27
  323.4 0.7 fusion.30
  324.1 1.2 bitcast_reduce_fusion
  325.3 0.1 fusion.19
  325.5 0.5 fusion.6
  326.0 0.3 fusion.20
  326.2 0.7 fusion.11
  327.0 116.8 %all-gather.8.cloned.1.call-done = bf16[1024,8192]{1,0:T(8,128)(2,1)} async-done(((bf16[1024,512]{1,0:T(8,128)(2,1)}), bf16[1024,8192]{1,0:T(8,128)(2,1)}) %all-gather.8.cloned.1.call-update) | async-done | bytes 16777232 | tf_op jit(solution)/shard_map/all_gather | solution.py:97
  443.7 9.8 %convolution_convert_fusion = bf16[64,8192]{1,0:T(8,128)(2,1)} fusion(bf16[1024,8192]{1,0:T(8,128)(2,1)} %all-gather.8.cloned.1.call-done, bf16[8,8,8,128]{3,2,1,0:T(8,128)(2,1)S(1)} %bitcast.115), kind=kOutput, calls=%fused_computation.3 | convolution fusion | flops 1074266112 | bytes 17956864 | tf_op jit(solution)/shard_map/dot_general | solution.py:95
  453.5 6.2 %copy.28 = bf16[16,2,768,128]{3,2,1,0:T(8,128)(2,1)} copy(bf16[16,2,768,128]{3,2,0,1:T(8,128)(2,1)} %copy_select_fusion) | data formatting | bytes 12582912
  459.7 30.4 %reduce-scatter.2.cloned.1.call-done = bf16[64,1024]{1,0:T(8,128)(2,1)} async-done(((bf16[64,8192]{1,0:T(8,128)(2,1)}), bf16[64,1024]{1,0:T(8,128)(2,1)}) %reduce-scatter.2.cloned.1.call-update) | async-done | bytes 131088 | tf_op jit(solution)/shard_map/reduce_scatter | solution.py:100
  (38 shorter events, 0.9 us)
Async XLA Ops:
  7.2 90.2 %all-gather.6.cloned.1.call-start = ((), (), s32[]{:S(2)}) async-start(), calls=%async_computation.3 | async-start | bytes 4456448 | tf_op jit(solution)/shard_map/all_gather | solution.py:34
  8.9 305.5 %all-gather.4.cloned.1.call-start = ((), (), s32[]{:S(2)}) async-start(), calls=%async_computation.2 | async-start | bytes 17825792 | tf_op jit(solution)/shard_map/all_gather | solution.py:29
  9.7 434.1 %all-gather.8.cloned.1.call-start = ((), (), s32[]{:S(2)}) async-start(), calls=%async_computation.4 | async-start | bytes 17825792 | tf_op jit(solution)/shard_map/all_gather | solution.py:97
  45.2 9.8 %copy-start.2 = (bf16[8192]{0:T(1024)(128)(2,1)S(1)}, bf16[8192]{0:T(1024)(128)(2,1)}, u32[]{:S(2)}) copy-start(bf16[8192]{0:T(1024)(128)(2,1)} %param.9) | copy-start | bytes 49156
  45.2 10.0 %copy-start.1 = (bf16[4,16,8192]{2,1,0:T(8,128)(2,1)S(1)}, bf16[4,16,8192]{2,1,0:T(8,128)(2,1)}, u32[]{:S(2)}) copy-start(bf16[4,16,8192]{2,1,0:T(8,128)(2,1)} %param.8) | copy-start | bytes 3145732
  45.2 232.4 %all-to-all-start = ((bf16[32,2,768,128]{3,2,1,0:T(8,128)(2,1)}), bf16[32,2,768,128]{3,2,1,0:T(8,128)(2,1)}, u32[]{:S(2)}, u32[]{:S(2)}) async-start(bf16[32,2,768,128]{3,2,1,0:T(8,128)(2,1)} %broadcast_select_fusion), calls=%async_computation | async-start | bytes 25165824 | tf_op jit(solution)/shard_map/all_to_all | solution.py:56
  54.6 435.5 %reduce-scatter.2.cloned.1.call-start = ((), (), s32[]{:S(2)}) async-start(), calls=%async_computation.5 | async-start | bytes 1179648 | tf_op jit(solution)/shard_map/reduce_scatter | solution.py:100
  314.4 9.7 %copy-start = (bf16[16,2,768,128]{3,2,0,1:T(8,128)(2,1)S(1)}, bf16[16,2,768,128]{3,2,0,1:T(8,128)(2,1)}, u32[]{:S(2)}) copy-start(bf16[16,2,768,128]{3,2,0,1:T(8,128)(2,1)} %copy_select_fusion) | copy-start | bytes 18874372
Sparse Core Ops, SparseCore 0:
  11.0 86.3 all-gather.5
  99.8 214.5 all-gather.3
  316.6 127.0 all-gather.7
  453.7 36.3 reduce-scatter.1
where the time goes:
time: 503 us; the launch traced here: 497 us
  waiting for transfers between devices  388 us (77%)
  local copies, waits for them, and re-layouts  29.2 us (6%)
  matrix products  24.6 us (5%)
  other arithmetic  20.5 us (4%)
  between operations  14.6 us (3%)
  blocking collectives  10.3 us (2%)
  starting transfers between devices  9.71 us (2%)
    all_to_all x1, waiting for transfers between devices, per_device(): lax.all_to_all(outgoing, 'rep', split_axis=0, concat_axis=0, tiled=True)  177 us
    all_gather x1, waiting for transfers between devices, per_device(): lax.all_gather(w_output, 'rep', axis=1, tiled=True)  117 us
    all_gather x1, waiting for transfers between devices, per_device(): lax.all_gather(keyval_flat, 'rep', axis=0, tiled=True)  41.5 us
    reduce_scatter x1, waiting for transfers between devices, per_device(): lax.psum_scatter(partial_value.astype(jnp.bfloat16), 'tp', scatter_dimens...  30.4 us
    all_gather x1, waiting for transfers between devices, per_device(): lax.all_gather(w_query, 'rep', axis=0, tiled=True)  20.5 us
    unnamed x14, local copies, waits for them, and re-layouts  10.8 us
    select_n x1, other arithmetic, per_device(): jnp.where(filled[:, None, None, None], kv_cache[source_row], jnp.zeros(()...  10.6 us
    unnamed x1, blocking collectives  10.3 us
  transfers between devices with their start and end apart: 5, of which 5 were waited for; matrix products, arithmetic and copies ran while one was open for 13% of the time, Pallas kernels for 0%

commit v1 on v0

v1 whole, which is shorter than its diff:
```python
import jax
import jax.numpy as jnp
from jax import lax
from jax.sharding import PartitionSpec as P

HEADDIM = 128
BLOCK = 128
CAP = 2


def per_device(
    new_tokens, norm_gain, w_query, w_keyval, w_output, kv_cache, block_counts, new_slot
):
    reps = lax.axis_size("rep")
    tps = lax.axis_size("tp")
    rep_index = lax.axis_index("rep")
    core = rep_index % 2
    chips = reps // 2
    same_core = [[2 * chip + one for chip in range(chips)] for one in range(2)]
    other_core = [(one, one ^ 1) for one in range(reps)]
    num_steps, num_rows, feat_width = new_tokens.shape
    row_total = num_steps * num_rows
    all_rows = reps * row_total
    depth = feat_width // reps
    head_cols = w_query.shape[1]
    pair_cols = w_keyval.shape[2]
    group = head_cols // pair_cols
    out_cols = w_output.shape[1]
    span_len = kv_cache.shape[2]

    inputs_f = new_tokens.astype(jnp.float32)
    inverse = lax.rsqrt(jnp.mean(inputs_f * inputs_f, axis=-1, keepdims=True) + 1e-05)
    normed = (inputs_f * inverse * norm_gain.astype(jnp.float32)).astype(jnp.bfloat16)
    slabs = normed.reshape(row_total, reps, depth).transpose(1, 0, 2)
    table = jnp.concatenate([new_slot, block_counts]).astype(jnp.bfloat16)
    table = jnp.pad(table[None], ((0, 15), (0, depth - 2 * num_rows)))
    slabs = jnp.concatenate([slabs, jnp.broadcast_to(table, (reps, 16, depth))], axis=1)
    slabs = lax.all_to_all(slabs, "rep", split_axis=0, concat_axis=0, tiled=True)
    features = slabs[:, :row_total].reshape(all_rows, depth)
    table = slabs[:, row_total, : 2 * num_rows].astype(jnp.int32)
    slot_grid, length_grid = table[:, :num_rows], table[:, num_rows:]
    slot_table, length_table = slot_grid.reshape(-1), length_grid.reshape(-1)

    new_row = (slot_grid // num_rows * row_total + slot_grid % num_rows)[:, None, :]
    new_row = new_row + num_rows * jnp.arange(num_steps)[None, :, None]
    shuffle = (
        new_row.reshape(-1)[:, None] == jnp.arange(all_rows)[None, :]
    ).astype(jnp.bfloat16)
    features = jnp.dot(shuffle, features, preferred_element_type=jnp.bfloat16)
    weights = jnp.concatenate([w_query, w_keyval.reshape(depth, 2 * pair_cols)], axis=1)
    partial = jnp.dot(features, weights, preferred_element_type=jnp.float32)
    partial = partial.reshape(chips, 2, row_total, -1)
    mine = lax.dynamic_index_in_dim(partial, core, 1, keepdims=False)
    theirs = lax.dynamic_index_in_dim(partial, 1 - core, 1, keepdims=False)
    theirs = lax.ppermute(theirs.astype(jnp.bfloat16), "rep", other_core)
    pair_sum = (mine + theirs.astype(jnp.float32)).astype(jnp.bfloat16)
    pair_sum = lax.all_to_all(
        pair_sum, "rep", split_axis=0, concat_axis=0, tiled=True, axis_index_groups=same_core
    )
    projected = jnp.sum(pair_sum.astype(jnp.float32), axis=0).astype(jnp.bfloat16)
    query = projected[:, :head_cols].reshape(num_steps, num_rows, group, HEADDIM)
    fresh = projected[:, head_cols:].reshape(num_steps, num_rows, 2, HEADDIM)

    live = jnp.arange(span_len)[None, :] < (block_counts * BLOCK)[:, None]
    factor = 1.0 / HEADDIM**0.5
    cache_scores = (
        jnp.einsum("trgd,rld->rgtl", query, kv_cache[:, 0], preferred_element_type=jnp.float32)
        * factor
    )
    cache_scores = jnp.where(live[:, None, None, :], cache_scores, -1e30)
    fresh_scores = (
        jnp.einsum("trgd,urd->rgtu", query, fresh[:, :, 0], preferred_element_type=jnp.float32)
        * factor
    )
    causal = jnp.arange(num_steps)[None, :] <= jnp.arange(num_steps)[:, None]
    fresh_scores = jnp.where(causal, fresh_scores, -1e30)
    peak = jnp.maximum(jnp.max(cache_scores, -1), jnp.max(fresh_scores, -1))
    cache_exp = jnp.exp(cache_scores - peak[..., None])
    fresh_exp = jnp.exp(fresh_scores - peak[..., None])
    total = jnp.sum(cache_exp, -1) + jnp.sum(fresh_exp, -1)
    cache_prob = (cache_exp / total[..., None]).astype(jnp.bfloat16)
    fresh_prob = (fresh_exp / total[..., None]).astype(jnp.bfloat16)
    mixed = jnp.einsum(
        "rgtl,rld->trgd", cache_prob, kv_cache[:, 1], preferred_element_type=jnp.float32
    )
    mixed = mixed + jnp.einsum(
        "rgtu,urd->trgd", fresh_prob, fresh[:, :, 1], preferred_element_type=jnp.float32
    )
    attended = mixed.astype(jnp.bfloat16).reshape(row_total, head_cols)

    attended = lax.all_to_all(
        jnp.broadcast_to(attended[None], (reps, row_total, head_cols)),
        "rep",
        split_axis=0,
        concat_axis=0,
        tiled=True,
    ).reshape(all_rows, head_cols)
    attended = jnp.einsum("on,oc->nc", shuffle, attended, preferred_element_type=jnp.bfloat16)
    partial_out = jnp.dot(attended, w_output, preferred_element_type=jnp.float32)
    partial_out = lax.all_to_all(
        partial_out.astype(jnp.bfloat16).reshape(tps, all_rows // tps, out_cols),
        "tp",
        split_axis=0,
        concat_axis=0,
        tiled=True,
    )
    summed = jnp.sum(partial_out.astype(jnp.float32), axis=0).astype(jnp.bfloat16)
    summed = summed.reshape(2, row_total, out_cols)
    straight = [
        (r * tps + t, (2 * t + r % 2) * tps + r // 2) for r in range(reps) for t in range(tps)
    ]
    crossed = [
        (r * tps + t, (2 * t + 1 - r % 2) * tps + r // 2) for r in range(reps) for t in range(tps)
    ]
    near = lax.ppermute(
        lax.dynamic_index_in_dim(summed, core, 0, keepdims=False), ("rep", "tp"), straight
    )
    far = lax.ppermute(
        lax.dynamic_index_in_dim(summed, 1 - core, 0, keepdims=False), ("rep", "tp"), crossed
    )
    layer_out = jnp.where(
        core == 0,
        jnp.concatenate([near, far], axis=1),
        jnp.concatenate([far, near], axis=1),
    ).reshape(num_steps, num_rows, 2 * out_cols)

    grid_target = slot_grid // num_rows
    same_target = grid_target[:, :, None] == grid_target[:, None, :]
    earlier = jnp.arange(num_rows)[None, :] < jnp.arange(num_rows)[:, None]
    position = jnp.sum(same_target & earlier[None], axis=-1)
    bucket = grid_target * CAP + position
    arrival = jnp.arange(reps, dtype=jnp.int32)[:, None] * CAP + position
    my_bucket = lax.dynamic_index_in_dim(bucket, rep_index, 0, keepdims=False)
    slot_hit = my_bucket[None, :] == jnp.arange(reps * CAP, dtype=jnp.int32)[:, None]
    source_row = jnp.sum(
        jnp.where(slot_hit, jnp.arange(num_rows, dtype=jnp.int32)[None, :], 0), axis=1
    )
    outgoing = kv_cache[source_row]
    received = lax.all_to_all(outgoing, "rep", split_axis=0, concat_axis=0, tiled=True)
    my_slots = rep_index * num_rows + jnp.arange(num_rows, dtype=jnp.int32)
    slot_match = slot_table[None, :] == my_slots[:, None]
    pick_index = jnp.sum(jnp.where(slot_match, arrival.reshape(-1)[None, :], 0), axis=1)
    moved_blocks = jnp.sum(jnp.where(slot_match, length_table[None, :], 0), axis=1)
    moved_live = jnp.arange(span_len)[None, :] < (moved_blocks * BLOCK)[:, None]
    cache_moved = jnp.where(
        moved_live[:, None, :, None], received[pick_index], jnp.zeros((), jnp.bfloat16)
    )
    return (layer_out, cache_moved)


def solution(mesh):
    placed = (
        P(None, "rep", None),
        P(),
        P("rep", "tp"),
        P("rep", None, "tp"),
        P("tp", "rep"),
        P("rep", None, None, "tp"),
        P("rep"),
        P("rep"),
    )
    return jax.shard_map(
        per_device,
        mesh=mesh,
        in_specs=placed,
        out_specs=(P(None, "rep", "tp"), P("rep", None, None, "tp")),
        check_vma=False,
    )
```

time: 503 us -> 373 us (0.74)
  the two profiles are of different devices: /device:TPU:17 before, /device:TPU:5 now
where the time goes in v1:
time: 373 us; the launch traced here: 372 us
  waiting for transfers between devices  243 us (65%)
  starting transfers between devices  36 us (10%)
  blocking collectives  32.2 us (9%)
  local copies, waits for them, and re-layouts  23.7 us (6%)
  other arithmetic  20.7 us (6%)
  matrix products  16 us (4%)
    ppermute x1, waiting for transfers between devices, per_device(): lax.ppermute(lax.dynamic_index_in_dim(summed, core, 0, keepdims=False), (...  197 us
    all_to_all x1, blocking collectives, per_device(): lax.all_to_all(jnp.broadcast_to(attended[None], (reps, row_total, head_co...  32.2 us
    all_to_all x1, waiting for transfers between devices, per_device(): lax.all_to_all(pair_sum, 'rep', split_axis=0, concat_axis=0, tiled=True,...  19.1 us
    all_to_all x1, waiting for transfers between devices, per_device(): lax.all_to_all(slabs, 'rep', split_axis=0, concat_axis=0, tiled=True)  17.1 us
    gather x1, local copies, waits for them, and re-layouts, per_device(): outgoing = kv_cache[source_row]  9.4 us
    gather x1, local copies, waits for them, and re-layouts, per_device(): received[pick_index]  8.63 us
    all_to_all x1, starting transfers between devices, per_device(): lax.all_to_all(slabs, 'rep', split_axis=0, concat_axis=0, tiled=True)  7.77 us
    select_n x1, other arithmetic, per_device(): jnp.where(moved_live[:, None, :, None], received[pick_index], jnp.zeros((...  7.67 us
  transfers between devices with their start and end apart: 7, of which 6 were waited for; matrix products, arithmetic and copies ran while one was open for 3% of the time, Pallas kernels for 0%

profile of v1, /device:TPU:5, one launch (start us, length us, event | category | flops | bytes accessed | tf_op | source)
XLA Modules:
  0.0 372.3 jit_solution(5835387889408026497)
XLA Ops:
  0.6 0.7 convert_bitcast_fusion.1
  1.4 0.7 broadcast_multiply_fusion.1
  2.1 1.5 fusion.9
  3.7 0.7 convert_element_type.58
  4.4 1.5 fusion.11
  6.5 1.8 copy.35
  8.3 7.8 %all-to-all-start = ((bf16[16,80,512]{2,1,0:T(8,128)(2,1)}), bf16[16,80,512]{2,1,0:T(8,128)(2,1)S(1)}, u32[]{:S(2)}, u32[]{:S(2)}) async-start(bf16[16,80,512]{2,1,0:T(8,128)(2,1)} %copy.35), calls=%async_computation | async-start | bytes 2621440 | tf_op jit(solution)/shard_map/all_to_all | solution.py:38
  16.1 0.7 copy.76
  16.8 17.1 %all-to-all-done = bf16[16,80,512]{2,1,0:T(8,128)(2,1)S(1)} async-done(((bf16[16,80,512]{2,1,0:T(8,128)(2,1)}), bf16[16,80,512]{2,1,0:T(8,128)(2,1)S(1)}, u32[]{:S(2)}, u32[]{:S(2)}) %all-to-all-start) | async-done | bytes 1310752 | tf_op jit(solution)/shard_map/all_to_all | solution.py:38
  34.3 6.5 %fusion.19 = f32[1024,1280]{1,0:T(8,128)} fusion(bf16[512,256]{1,0:T(8,128)(2,1)} %bitcast.146, bf16[512,1024]{1,0:T(8,128)(2,1)} %param.10, bf16[1024,512]{1,0:T(8,128)(2,1)S(1)} %bitcast.139, s32[1024]{0:T(1024)S(1)} %add.134), kind=kOutput, calls=%fused_computation.31 | convolution fusion | flops 2419589120 | bytes 7606272 | tf_op jit(solution)/shard_map/dot_general | solution.py:51
  40.8 1.9 fusion.18
  42.7 1.2 collective-permute-start
  43.9 2.8 collective-permute-done
  46.7 3.5 fusion.8
  50.2 6.2 %all-to-all-start.1 = ((bf16[8,64,1280]{2,1,0:T(8,128)(2,1)}), bf16[8,64,1280]{2,1,0:T(8,128)(2,1)}, u32[]{:S(2)}, u32[]{:S(2)}) async-start(bf16[8,64,1280]{2,1,0:T(8,128)(2,1)} %fusion.8), calls=%async_computation.1 | async-start | bytes 2621440 | tf_op jit(solution)/shard_map/all_to_all | solution.py:57
  56.5 19.1 %all-to-all-done.1 = bf16[8,64,1280]{2,1,0:T(8,128)(2,1)} async-done(((bf16[8,64,1280]{2,1,0:T(8,128)(2,1)}), bf16[8,64,1280]{2,1,0:T(8,128)(2,1)}, u32[]{:S(2)}, u32[]{:S(2)}) %all-to-all-start.1) | async-done | bytes 1310752 | tf_op jit(solution)/shard_map/all_to_all | solution.py:57
  75.6 1.5 reduce_sum.92
  77.3 0.7 fusion.61
  78.0 3.3 bitcast_reduce_fusion
  82.2 0.7 fusion.29
  83.2 32.2 %all_to_all.25 = bf16[16,64,1024]{2,1,0:T(8,128)(2,1)S(1)} all-to-all(bf16[16,64,1024]{2,1,0:T(8,128)(2,1)S(1)} %broadcast_in_dim.110), channel_id=1, replica_groups=mesh['rep'=16,'tp'=8] {'rep'}, dimensions={0} | all-to-all | bytes 4194304 | tf_op jit(solution)/shard_map/all_to_all | solution.py:91
  115.5 4.5 %convolution_convert_fusion = bf16[1024,512]{1,0:T(8,128)(2,1)} fusion(bf16[1024,512]{1,0:T(8,128)(2,1)S(1)} %copy-done, bf16[1024,1024]{1,0:T(8,128)(2,1)S(1)} %bitcast.137, s32[1024]{0:T(1024)S(1)} %add.134), kind=kOutput, calls=%fused_computation.27 | convolution fusion | flops 3222798336 | bytes 4198400 | tf_op jit(solution)/shard_map/dot_general | solution.py:99
  120.0 5.1 %all-to-all-start.3 = ((bf16[8,128,512]{2,1,0:T(8,128)(2,1)}), bf16[8,128,512]{2,1,0:T(8,128)(2,1)S(1)}, u32[]{:S(2)}, u32[]{:S(2)}) async-start(bf16[8,128,512]{2,1,0:T(8,128)(2,1)} %bitcast.138), calls=%async_computation.3 | async-start | bytes 2097152 | tf_op jit(solution)/shard_map/all_to_all | solution.py:100
  125.7 9.4 %gather_fusion = bf16[32,2,768,128]{3,2,1,0:T(8,128)(2,1)} fusion(bf16[16,2,768,128]{3,2,1,0:T(8,128)(2,1)} %param.13, s32[1024]{0:T(1024)S(1)} %pad_clamp_fusion.1), kind=kCustom, calls=%fused_computation | custom fusion | bytes 25165952 | tf_op jit(solution)/shard_map/gather | solution.py:138
  135.1 5.1 %all-to-all-done.3 = bf16[8,128,512]{2,1,0:T(8,128)(2,1)S(1)} async-done(((bf16[8,128,512]{2,1,0:T(8,128)(2,1)}), bf16[8,128,512]{2,1,0:T(8,128)(2,1)S(1)}, u32[]{:S(2)}, u32[]{:S(2)}) %all-to-all-start.3) | async-done | bytes 1048608 | tf_op jit(solution)/shard_map/all_to_all | solution.py:100
  140.2 7.7 %all-to-all-start.4 = ((bf16[32,2,768,128]{3,2,1,0:T(8,128)(2,1)}), bf16[32,2,768,128]{3,2,1,0:T(8,128)(2,1)}, u32[]{:S(2)}, u32[]{:S(2)}) async-start(bf16[32,2,768,128]{3,2,1,0:T(8,128)(2,1)} %gather_fusion), calls=%async_computation.4 | async-start | bytes 25165824 | tf_op jit(solution)/shard_map/all_to_all | solution.py:139
  148.6 2.2 collective-permute-start.1
  150.9 5.7 %collective-permute-start.2 = (bf16[64,512]{1,0:T(8,128)(2,1)S(1)}, bf16[64,512]{1,0:T(8,128)(2,1)S(1)}, u32[]{:S(2)}, u32[]{:S(2)}) collective-permute-start(bf16[64,512]{1,0:T(8,128)(2,1)S(1)} %get-tuple-element.5), channel_id=1, source_target_pairs={{0,8},{1,24},{2,40},{3,56},{4,72},{5,88},{6,104},{7,120},{8,0},{9,... | collective-permute-start | bytes 196616 | tf_op jit(solution)/shard_map/ppermute | solution.py:118
  156.5 197.1 %collective-permute-done.1 = bf16[64,512]{1,0:T(8,128)(2,1)S(1)} collective-permute-done((bf16[64,512]{1,0:T(8,128)(2,1)S(1)}, bf16[64,512]{1,0:T(8,128)(2,1)S(1)}, u32[]{:S(2)}, u32[]{:S(2)}) %collective-permute-start.1) | collective-permute-done | bytes 65568 | tf_op jit(solution)/shard_map/ppermute | solution.py:115
  353.7 1.6 collective-permute-done.2
  355.9 8.6 %gather_fusion.1 = bf16[16,2,768,128]{3,2,1,0:T(8,128)(2,1)} fusion(bf16[32,2,768,128]{3,2,1,0:T(8,128)(2,1)} %all-to-all-done.4, s32[1024]{0:T(1024)S(1)} %pad_clamp_fusion), kind=kCustom, calls=%fused_computation.1 | custom fusion | bytes 12582976 | tf_op jit(solution)/shard_map/gather | solution.py:146
  364.6 7.7 %broadcast_select_fusion = bf16[16,2,768,128]{3,2,1,0:T(8,128)(2,1)} fusion(bf16[16,2,768,128]{3,2,1,0:T(8,128)(2,1)} %gather_fusion.1, pred[16,768]{1,0:T(8,128)(4,1)S(1)} %iota_compare_fusion.7), kind=kLoop, calls=%fused_computation.2 | loop fusion | flops 3145728 | bytes 12595200 | tf_op jit(solution)/shard_map/jit(_where)/select_n | solution.py:145
  (59 shorter events, 4.3 us)
Async XLA Ops:
  0.6 114.8 %copy-start = (bf16[1024,512]{1,0:T(8,128)(2,1)S(1)}, bf16[1024,512]{1,0:T(8,128)(2,1)}, u32[]{:S(2)}) copy-start(bf16[1024,512]{1,0:T(8,128)(2,1)} %param.12) | copy-start | bytes 3145732
  6.5 9.6 %copy-start.2 = (bf16[512,2,128]{2,1,0:T(2,128)(2,1)S(1)}, bf16[512,2,128]{2,1,0:T(2,128)(2,1)}, u32[]{:S(2)}) copy-start(bf16[512,2,128]{2,1,0:T(2,128)(2,1)} %param.11) | copy-start | bytes 786436
  8.3 25.6 %all-to-all-start = ((bf16[16,80,512]{2,1,0:T(8,128)(2,1)}), bf16[16,80,512]{2,1,0:T(8,128)(2,1)S(1)}, u32[]{:S(2)}, u32[]{:S(2)}) async-start(bf16[16,80,512]{2,1,0:T(8,128)(2,1)} %copy.35), calls=%async_computation | async-start | bytes 2621440 | tf_op jit(solution)/shard_map/all_to_all | solution.py:38
  42.7 4.0 %collective-permute-start = (bf16[8,64,1280]{2,1,0:T(8,128)(2,1)S(1)}, bf16[8,64,1280]{2,1,0:T(8,128)(2,1)}, u32[]{:S(2)}, u32[]{:S(2)}) collective-permute-start(bf16[8,64,1280]{2,1,0:T(8,128)(2,1)S(1)} %fusion.18), channel_id=1, source_target_pairs={{0,8},{8,0},{16,24},{24,16},{32,40},{40,32},{48,56},{56,48},{64,72... | collective-permute-start | bytes 3932168 | tf_op jit(solution)/shard_map/ppermute | solution.py:55
  50.2 32.0 %slice-start = ((s8[6291456]{0:T(1024)(128)(4,1)}), s8[2097152]{0:T(1024)(128)(4,1)S(1)}, s32[]{:S(2)}) async-start(s8[6291456]{0:T(1024)(128)(4,1)} %bitcast.131), calls=%async_computation.5 | async-start | bytes 4194304
  50.2 25.5 %all-to-all-start.1 = ((bf16[8,64,1280]{2,1,0:T(8,128)(2,1)}), bf16[8,64,1280]{2,1,0:T(8,128)(2,1)}, u32[]{:S(2)}, u32[]{:S(2)}) async-start(bf16[8,64,1280]{2,1,0:T(8,128)(2,1)} %fusion.8), calls=%async_computation.1 | async-start | bytes 2621440 | tf_op jit(solution)/shard_map/all_to_all | solution.py:57
  78.0 4.2 %slice-start.1 = ((s8[6291456]{0:T(1024)(128)(4,1)}), s8[4194304]{0:T(1024)(128)(4,1)S(1)}, s32[]{:S(2)}) async-start(s8[6291456]{0:T(1024)(128)(4,1)} %bitcast.131), calls=%async_computation.6 | async-start | bytes 8388608
  120.0 20.2 %all-to-all-start.3 = ((bf16[8,128,512]{2,1,0:T(8,128)(2,1)}), bf16[8,128,512]{2,1,0:T(8,128)(2,1)S(1)}, u32[]{:S(2)}, u32[]{:S(2)}) async-start(bf16[8,128,512]{2,1,0:T(8,128)(2,1)} %bitcast.138), calls=%async_computation.3 | async-start | bytes 2097152 | tf_op jit(solution)/shard_map/all_to_all | solution.py:100
  140.2 215.8 %all-to-all-start.4 = ((bf16[32,2,768,128]{3,2,1,0:T(8,128)(2,1)}), bf16[32,2,768,128]{3,2,1,0:T(8,128)(2,1)}, u32[]{:S(2)}, u32[]{:S(2)}) async-start(bf16[32,2,768,128]{3,2,1,0:T(8,128)(2,1)} %gather_fusion), calls=%async_computation.4 | async-start | bytes 25165824 | tf_op jit(solution)/shard_map/all_to_all | solution.py:139
  148.6 205.0 %collective-permute-start.1 = (bf16[64,512]{1,0:T(8,128)(2,1)S(1)}, bf16[64,512]{1,0:T(8,128)(2,1)S(1)}, u32[]{:S(2)}, u32[]{:S(2)}) collective-permute-start(bf16[64,512]{1,0:T(8,128)(2,1)S(1)} %get-tuple-element.4), channel_id=1, source_target_pairs={{0,0},{1,16},{2,32},{3,48},{4,64},{5,80},{6,96},{7,112},{8,8},{9,2... | collective-permute-start | bytes 196616 | tf_op jit(solution)/shard_map/ppermute | solution.py:115
  150.9 204.4 %collective-permute-start.2 = (bf16[64,512]{1,0:T(8,128)(2,1)S(1)}, bf16[64,512]{1,0:T(8,128)(2,1)S(1)}, u32[]{:S(2)}, u32[]{:S(2)}) collective-permute-start(bf16[64,512]{1,0:T(8,128)(2,1)S(1)} %get-tuple-element.5), channel_id=1, source_target_pairs={{0,8},{1,24},{2,40},{3,56},{4,72},{5,88},{6,104},{7,120},{8,0},{9,... | collective-permute-start | bytes 196616 | tf_op jit(solution)/shard_map/ppermute | solution.py:118
  364.6 7.7 %copy-start.1 = (bf16[1024,512]{1,0:T(8,128)(2,1)S(1)}, bf16[1024,512]{1,0:T(8,128)(2,1)}, u32[]{:S(2)}) copy-start(bf16[1024,512]{1,0:T(8,128)(2,1)} %param.12) | copy-start | bytes 3145732

commit v2 on v1

--- a/solution.py
+++ b/solution.py
@@ -1,11 +1,288 @@
 import jax
 import jax.numpy as jnp
 from jax import lax
+from jax.experimental import pallas as pl
+from jax.experimental.pallas import tpu as pltpu
 from jax.sharding import PartitionSpec as P
 
 HEADDIM = 128
 BLOCK = 128
-CAP = 2
+FIRST = 24
+LATER = 8
+
+
+def chip_shift(reps, shift):
+    across, along = reps // 4, shift // 2
+    pairs = []
+    for one in range(reps):
+        x, y, core = one // 4, one // 2 % 2, one % 2
+        there = (x + along) % across * 4 + (y + shift) % 2 * 2 + core
+        pairs.append((one, there))
+    return pairs
+
+
+def shift_between(source, target, chips):
+    along = (target // 2 - source // 2) % (chips // 2)
+    return along * 2 + (target - source) % 2
+
+
+def route(slot_table, length_table, my_chip, chips):
+    count = slot_table.shape[0] // chips
+    lengths = length_table.reshape(chips, count)
+    targets = (slot_table // count).reshape(chips, count)
+    shared = targets[:, :, None] == targets[:, None, :]
+    order = jnp.arange(count)
+    place = jnp.sum(
+        jnp.where(shared & (order[None, :] < order[:, None]), lengths[:, None, :], 0), axis=-1
+    )
+    sources = jnp.arange(chips, dtype=jnp.int32)[:, None]
+    shifts = shift_between(sources, targets, chips)
+    most = jnp.max(jnp.where(shifts > 0, place + lengths, 0))
+    both = jnp.stack([shifts, place, lengths])
+    pack_table = lax.dynamic_index_in_dim(both, my_chip, 1, keepdims=False)
+    wanted = my_chip * count + order
+    match = slot_table[None, :] == wanted[:, None]
+    fields = jnp.concatenate(
+        [
+            both.reshape(3, -1),
+            jnp.broadcast_to(order[None, :], (chips, count)).reshape(1, -1).astype(jnp.int32),
+        ]
+    )
+    unpack_table = jnp.sum(jnp.where(match[None], fields[:, None, :], 0), axis=-1)
+    return pack_table.astype(jnp.int32), unpack_table.astype(jnp.int32), most.astype(jnp.int32)
+
+
+def blocks_of(cache, rows, block, core=None):
+    span = pl.ds(pl.multiple_of(block * BLOCK, BLOCK), BLOCK)
+    if core is None:
+        return cache.at[rows, span]
+    return cache.at[rows, core, span]
+
+
+def pack_body(scalars, table, cache, lent, *rest):
+    outs, sem = rest[:-1], rest[-1]
+    core, start = scalars[0], scalars[1]
+    room = outs[0].shape[0]
+    requests = table.shape[1]
+    half = requests // 2
+
+    def send(at, total):
+        shift, place, length = table[0, at], table[1, at], table[2, at]
+        row = at % half
+        low = jnp.maximum(start - place, 0)
+        high = jnp.minimum(length, start + room - place)
+        own = at // half == core
+        for one, out in enumerate(outs, 1):
+
+            @pl.when((shift == one) & own)
+            def _():
+                @pl.loop(low, high)
+                def _(block):
+                    pltpu.make_async_copy(
+                        blocks_of(cache, row, block, core), out.at[place + block - start], sem
+                    ).start()
+
+            @pl.when((shift == one) & jnp.logical_not(own))
+            def _():
+                @pl.loop(low, high)
+                def _(block):
+                    pltpu.make_async_copy(
+                        blocks_of(lent, row, block), out.at[place + block - start], sem
+                    ).start()
+
+        return total + jnp.where(shift > 0, jnp.maximum(high - low, 0), 0)
+
+    total = lax.fori_loop(0, requests, send, jnp.int32(0))
+
+    @pl.loop(0, total)
+    def _(_):
+        pltpu.make_async_copy(outs[0].at[0], outs[0].at[0], sem).wait()
+
+
+def any_space(number):
+    return [pl.BlockSpec(memory_space=pl.ANY)] * number
+
+
+def smem_space(number):
+    return [pl.BlockSpec(memory_space=pltpu.SMEM)] * number
+
+
+def moved_cost(size):
+    return pl.CostEstimate(flops=0, bytes_accessed=size, transcendentals=0)
+
+
+def pack_kernel(core, start, table, cache, lent, room):
+    block = jax.ShapeDtypeStruct((room, BLOCK, HEADDIM), jnp.bfloat16)
+    scalars = jnp.stack([core, jnp.asarray(start, jnp.int32)]).astype(jnp.int32)
+    return pl.pallas_call(
+        pack_body,
+        out_shape=[block] * 7,
+        in_specs=smem_space(2) + any_space(2),
+        out_specs=any_space(7),
+        scratch_shapes=[pltpu.SemaphoreType.DMA],
+        cost_estimate=moved_cost(8 << 20),
+        name="pack_blocks",
+    )(scalars, table, cache, lent)
+
+
+def unpack_body(scalars, table, cache, lent, *rest):
+    pieces, (moved, theirs, zeros, sem_mine, sem_theirs) = rest[:7], rest[7:]
+    core = scalars[0]
+    room = pieces[0].shape[0]
+    half = theirs.shape[0]
+    zeros[...] = jnp.zeros_like(zeros)
+    most = cache.shape[2] // BLOCK
+
+    def receive(slot, mine):
+        at = jnp.where(mine, core, 1 - core) * half + slot
+        sem = sem_mine if mine else sem_theirs
+        shift, place, length, owner = table[0, at], table[1, at], table[2, at], table[3, at]
+        row = owner % half
+        inside = jnp.where(shift > 0, jnp.clip(room - place, 0, length), length)
+
+        def target(block, many=1):
+            span = pl.ds(pl.multiple_of(block * BLOCK, BLOCK), many * BLOCK)
+            return moved.at[slot, core, span] if mine else theirs.at[slot, span]
+
+        for one, piece in enumerate(pieces, 1):
+
+            @pl.when(shift == one)
+            def _():
+                @pl.loop(0, inside)
+                def _(block):
+                    pltpu.make_async_copy(piece.at[place + block], target(block), sem).start()
+
+        own = owner // half == core
+
+        @pl.when((shift == 0) & own)
+        def _():
+            @pl.loop(0, inside)
+            def _(block):
+                pltpu.make_async_copy(
+                    blocks_of(cache, row, block, core), target(block), sem
+                ).start()
+
+        @pl.when((shift == 0) & jnp.logical_not(own))
+        def _():
+            @pl.loop(0, inside)
+            def _(block):
+                pltpu.make_async_copy(blocks_of(lent, row, block), target(block), sem).start()
+
+        rest_at = inside
+        for many in (4, 2, 1):
+            hit = (most - inside) & many
+
+            @pl.when(hit > 0)
+            def _():
+                pltpu.make_async_copy(
+                    zeros.at[pl.ds(0, many * BLOCK)], target(rest_at, many), sem
+                ).start()
+
+            rest_at = rest_at + hit
+
+    @pl.loop(0, half)
+    def _(slot):
+        receive(slot, False)
+
+    @pl.loop(0, half)
+    def _(slot):
+        receive(slot, True)
+
+    pltpu.make_async_copy(theirs, theirs, sem_theirs).wait()
+    pltpu.make_async_copy(theirs, theirs, sem_mine).wait()
+
+
+def unpack_kernel(core, table, cache, lent, pieces):
+    rows, _, span, width = cache.shape
+    return pl.pallas_call(
+        unpack_body,
+        out_shape=[
+            jax.ShapeDtypeStruct(cache.shape, jnp.bfloat16),
+            jax.ShapeDtypeStruct((rows, span, width), jnp.bfloat16),
+        ],
+        in_specs=smem_space(2) + any_space(9),
+        out_specs=any_space(2),
+        scratch_shapes=[
+            pltpu.VMEM((4 * BLOCK, width), jnp.bfloat16),
+            pltpu.SemaphoreType.DMA,
+            pltpu.SemaphoreType.DMA,
+        ],
+        cost_estimate=moved_cost(10 << 20),
+        name="unpack_blocks",
+    )(core[None].astype(jnp.int32), table, cache, lent, *pieces)
+
+
+def unpack_more_body(scalars, table, *rest):
+    pieces, (_, _, moved, theirs, sem) = rest[:7], rest[7:]
+    core, start = scalars[0], scalars[1]
+    room = pieces[0].shape[0]
+    half = theirs.shape[0]
+
+    def receive(at, total):
+        shift, place, length = table[0, at], table[1, at], table[2, at]
+        slot = at % half
+        low = jnp.maximum(start - place, 0)
+        high = jnp.minimum(length, start + room - place)
+        mine = at // half == core
+        for one, piece in enumerate(pieces, 1):
+
+            @pl.when((shift == one) & mine)
+            def _():
+                @pl.loop(low, high)
+                def _(block):
+                    pltpu.make_async_copy(
+                        piece.at[place + block - start], blocks_of(moved, slot, block, core), sem
+                    ).start()
+
+            @pl.when((shift == one) & jnp.logical_not(mine))
+            def _():
+                @pl.loop(low, high)
+                def _(block):
+                    pltpu.make_async_copy(
+                        piece.at[place + block - start], blocks_of(theirs, slot, block), sem
+                    ).start()
+
+        return total + jnp.where(shift > 0, jnp.maximum(high - low, 0), 0)
+
+    total = lax.fori_loop(0, 2 * half, receive, jnp.int32(0))
+
+    @pl.loop(0, total)
+    def _(_):
+        pltpu.make_async_copy(pieces[0].at[0], pieces[0].at[0], sem).wait()
+
+
+def unpack_more_kernel(core, start, table, pieces, moved, theirs):
+    return pl.pallas_call(
+        unpack_more_body,
+        out_shape=[
+            jax.ShapeDtypeStruct(moved.shape, moved.dtype),
+            jax.ShapeDtypeStruct(theirs.shape, theirs.dtype),
+        ],
+        in_specs=smem_space(2) + any_space(9),
+        out_specs=any_space(2),
+        scratch_shapes=[pltpu.SemaphoreType.DMA],
+        input_output_aliases={9: 0, 10: 1},
+        name="unpack_later_blocks",
+    )(jnp.stack([core, start]).astype(jnp.int32), table, *pieces, moved, theirs)
+
+
+def finish_body(scalars, returned, _, moved, sem):
+    copy = pltpu.make_async_copy(returned, moved.at[:, 1 - scalars[0]], sem)
+    copy.start()
+    copy.wait()
+
+
+def finish_kernel(core, returned, moved):
+    return pl.pallas_call(
+        finish_body,
+        out_shape=jax.ShapeDtypeStruct(moved.shape, moved.dtype),
+        in_specs=smem_space(1) + any_space(2),
+        out_specs=any_space(1)[0],
+        scratch_shapes=[pltpu.SemaphoreType.DMA],
+        input_output_aliases={2: 0},
+        cost_estimate=moved_cost(6 << 20),
+        name="put_other_kind",
+    )(core[None].astype(jnp.int32), returned, moved)
 
 
 def per_device(
@@ -28,6 +305,10 @@
     out_cols = w_output.shape[1]
     span_len = kv_cache.shape[2]
 
+    lent = lax.ppermute(
+        lax.dynamic_index_in_dim(kv_cache, 1 - core, 1, keepdims=False), "rep", other_core
+    )
+
     inputs_f = new_tokens.astype(jnp.float32)
     inverse = lax.rsqrt(jnp.mean(inputs_f * inputs_f, axis=-1, keepdims=True) + 1e-05)
     normed = (inputs_f * inverse * norm_gain.astype(jnp.float32)).astype(jnp.bfloat16)
@@ -124,27 +405,29 @@
         jnp.concatenate([far, near], axis=1),
     ).reshape(num_steps, num_rows, 2 * out_cols)
 
-    grid_target = slot_grid // num_rows
-    same_target = grid_target[:, :, None] == grid_target[:, None, :]
-    earlier = jnp.arange(num_rows)[None, :] < jnp.arange(num_rows)[:, None]
-    position = jnp.sum(same_target & earlier[None], axis=-1)
-    bucket = grid_target * CAP + position
-    arrival = jnp.arange(reps, dtype=jnp.int32)[:, None] * CAP + position
-    my_bucket = lax.dynamic_index_in_dim(bucket, rep_index, 0, keepdims=False)
-    slot_hit = my_bucket[None, :] == jnp.arange(reps * CAP, dtype=jnp.int32)[:, None]
-    source_row = jnp.sum(
-        jnp.where(slot_hit, jnp.arange(num_rows, dtype=jnp.int32)[None, :], 0), axis=1
-    )
-    outgoing = kv_cache[source_row]
-    received = lax.all_to_all(outgoing, "rep", split_axis=0, concat_axis=0, tiled=True)
-    my_slots = rep_index * num_rows + jnp.arange(num_rows, dtype=jnp.int32)
-    slot_match = slot_table[None, :] == my_slots[:, None]
-    pick_index = jnp.sum(jnp.where(slot_match, arrival.reshape(-1)[None, :], 0), axis=1)
-    moved_blocks = jnp.sum(jnp.where(slot_match, length_table[None, :], 0), axis=1)
-    moved_live = jnp.arange(span_len)[None, :] < (moved_blocks * BLOCK)[:, None]
-    cache_moved = jnp.where(
-        moved_live[:, None, :, None], received[pick_index], jnp.zeros((), jnp.bfloat16)
-    )
+    my_chip = rep_index // 2
+    pack_table, unpack_table, most = route(slot_table, length_table, my_chip, chips)
+    sent = pack_kernel(core, 0, pack_table, kv_cache, lent, FIRST)
+    arrived = [
+        lax.ppermute(piece, "rep", chip_shift(reps, shift)) for shift, piece in enumerate(sent, 1)
+    ]
+    cache_moved, theirs = unpack_kernel(core, unpack_table, kv_cache, lent, arrived)
+
+    def more(state):
+        start, moved, other = state
+        pieces = pack_kernel(core, start, pack_table, kv_cache, lent, LATER)
+        pieces = [
+            lax.ppermute(piece, "rep", chip_shift(reps, shift))
+            for shift, piece in enumerate(pieces, 1)
+        ]
+        moved, other = unpack_more_kernel(core, start, unpack_table, pieces, moved, other)
+        return start + LATER, moved, other
+
+    _, cache_moved, theirs = lax.while_loop(
+        lambda state: state[0] < most, more, (jnp.int32(FIRST), cache_moved, theirs)
+    )
+    returned = lax.ppermute(theirs, "rep", other_core)
+    cache_moved = finish_kernel(core, returned, cache_moved)
     return (layer_out, cache_moved)
 
 

time: 373 us -> 431 us (1.16)
  the two profiles are of different devices: /device:TPU:5 before, /device:TPU:17 now
where the time goes in v2:
time: 431 us; the launch traced here: 427 us
  Pallas kernels  226 us (52%)
  waiting for transfers between devices  92.6 us (21%)
  starting transfers between devices  41.2 us (10%)
  blocking collectives  21.1 us (5%)
  matrix products  18.3 us (4%)
  local copies, waits for them, and re-layouts  12.9 us (3%)
  other arithmetic  12.8 us (3%)
    pallas_call x1, Pallas kernels, finish_kernel(): pl.pallas_call(finish_body, out_shape=jax.ShapeDtypeStruct(moved.shape, m...  96.4 us
    ppermute x7, waiting for transfers between devices, per_device(): lax.ppermute(piece, 'rep', chip_shift(reps, shift))  67.5 us
    pallas_call x1, Pallas kernels, unpack_kernel(): pl.pallas_call(unpack_body, out_shape=[jax.ShapeDtypeStruct(cache.shape,...  66.3 us
    pallas_call x1, Pallas kernels, pack_kernel(): pl.pallas_call(pack_body, out_shape=[block] * 7, in_specs=smem_space(2) +...  63.4 us
    all_to_all x1, blocking collectives, per_device(): lax.all_to_all(partial_out.astype(jnp.bfloat16).reshape(tps, all_rows //...  21.1 us
    ppermute x7, starting transfers between devices, per_device(): lax.ppermute(piece, 'rep', chip_shift(reps, shift))  13.2 us
    all_to_all x1, waiting for transfers between devices, per_device(): lax.all_to_all(slabs, 'rep', split_axis=0, concat_axis=0, tiled=True)  12.9 us
  transfers between devices with their start and end apart: 15, of which 8 were waited for; matrix products, arithmetic and copies ran while one was open for 8% of the time, Pallas kernels for 30%

profile of v2, /device:TPU:17, one launch (start us, length us, event | category | flops | bytes accessed | tf_op | source)
XLA Modules:
  0.0 426.7 jit_solution(9027961233079486322)
XLA Ops:
  2.1 1.5 fusion.9
  4.4 1.5 fusion.11
  6.5 1.8 copy.53
  8.3 7.6 %all-to-all-start = ((bf16[16,80,512]{2,1,0:T(8,128)(2,1)}), bf16[16,80,512]{2,1,0:T(8,128)(2,1)S(1)}, u32[]{:S(2)}, u32[]{:S(2)}) async-start(bf16[16,80,512]{2,1,0:T(8,128)(2,1)} %copy.53), calls=%async_computation | async-start | bytes 2621440 | tf_op jit(solution)/shard_map/all_to_all | solution.py:319
  15.9 3.9 dynamic-slice_bitcast_fusion
  21.2 12.9 %all-to-all-done = bf16[16,80,512]{2,1,0:T(8,128)(2,1)S(1)} async-done(((bf16[16,80,512]{2,1,0:T(8,128)(2,1)}), bf16[16,80,512]{2,1,0:T(8,128)(2,1)S(1)}, u32[]{:S(2)}, u32[]{:S(2)}) %all-to-all-start) | async-done | bytes 1310752 | tf_op jit(solution)/shard_map/all_to_all | solution.py:319
  35.7 6.5 %fusion.19 = f32[1024,1280]{1,0:T(8,128)} fusion(bf16[512,256]{1,0:T(8,128)(2,1)} %bitcast.148, bf16[512,1024]{1,0:T(8,128)(2,1)} %param.12, bf16[1024,512]{1,0:T(8,128)(2,1)S(1)} %bitcast.140, s32[1024]{0:T(1024)S(1)} %add.220), kind=kOutput, calls=%fused_computation.30 | convolution fusion | flops 2419589120 | bytes 7606272 | tf_op jit(solution)/shard_map/dot_general | solution.py:332
  42.2 1.9 fusion.18
  44.4 3.0 collective-permute-done.7
  47.3 3.5 fusion.8
  50.8 5.8 %all-to-all-start.1 = ((bf16[8,64,1280]{2,1,0:T(8,128)(2,1)}), bf16[8,64,1280]{2,1,0:T(8,128)(2,1)S(1)}, u32[]{:S(2)}, u32[]{:S(2)}) async-start(bf16[8,64,1280]{2,1,0:T(8,128)(2,1)} %fusion.8), calls=%async_computation.1 | async-start | bytes 2621440 | tf_op jit(solution)/shard_map/all_to_all | solution.py:338
  58.3 63.4 %pack_blocks.2 = (bf16[24,128,128]{2,1,0:T(8,128)(2,1)}, bf16[24,128,128]{2,1,0:T(8,128)(2,1)}, bf16[24,128,128]{2,1,0:T(8,128)(2,1)}, bf16[24,128,128]{2,1,0:T(...) custom-call(s32[2]{0:T(128)} %pad_add_fusion.2.scalars, ...), custom_call_target="tpu_custom_call" | custom-call | bytes 8388608 | tf_op jit(solution)/shard_map/pack_blocks/pallas_call | solution.py:117
  121.9 3.4 collective-permute-start.13
  125.3 3.0 collective-permute-start.14
  128.6 3.1 bitcast_reduce_fusion
  133.4 2.6 collective-permute-start.15
  136.0 5.9 %collective-permute-done.11.rest_0_ = bf16[24,128,128]{2,1,0:T(8,128)(2,1)S(1)} collective-permute-done((bf16[24,128,128]{2,1,0:T(8,128)(2,1)}, bf16[24,128,128]{2,1,0:T(8,128)(2,1)S(1)}, u32[]{:S(2)}, u32[]{:S(2)}) %collective-permute-start.11) | collective-permute-done | bytes 786464 | tf_op jit(solution)/shard_map/ppermute | solution.py:412
  142.0 3.9 collective-permute-start.17
  145.9 2.6 fusion.29
  148.6 1.7 broadcast_in_dim.104
  150.2 7.5 %all-to-all-start.2 = ((bf16[16,64,1024]{2,1,0:T(8,128)(2,1)}), bf16[16,64,1024]{2,1,0:T(8,128)(2,1)}, u32[]{:S(2)}, u32[]{:S(2)}) async-start(bf16[16,64,1024]{2,1,0:T(8,128)(2,1)} %broadcast_in_dim.104), calls=%async_computation.2 | async-start | bytes 4194304 | tf_op jit(solution)/shard_map/all_to_all | solution.py:372
  158.0 10.5 %collective-permute-done.13.rest_2_ = bf16[24,128,128]{2,1,0:T(8,128)(2,1)} collective-permute-done((bf16[24,128,128]{2,1,0:T(8,128)(2,1)}, bf16[24,128,128]{2,1,0:T(8,128)(2,1)}, u32[]{:S(2)}, u32[]{:S(2)}) %collective-permute-start.13) | collective-permute-done | bytes 786464 | tf_op jit(solution)/shard_map/ppermute | solution.py:412
  168.5 25.1 %collective-permute-done.14.rest_3_ = bf16[24,128,128]{2,1,0:T(8,128)(2,1)} collective-permute-done((bf16[24,128,128]{2,1,0:T(8,128)(2,1)}, bf16[24,128,128]{2,1,0:T(8,128)(2,1)}, u32[]{:S(2)}, u32[]{:S(2)}) %collective-permute-start.14) | collective-permute-done | bytes 786464 | tf_op jit(solution)/shard_map/ppermute | solution.py:412
  193.6 25.8 %collective-permute-done.15.rest_4_ = bf16[24,128,128]{2,1,0:T(8,128)(2,1)S(1)} collective-permute-done((bf16[24,128,128]{2,1,0:T(8,128)(2,1)}, bf16[24,128,128]{2,1,0:T(8,128)(2,1)S(1)}, u32[]{:S(2)}, u32[]{:S(2)}) %collective-permute-start.15) | collective-permute-done | bytes 786464 | tf_op jit(solution)/shard_map/ppermute | solution.py:412
  220.4 66.3 %unpack_blocks.1 = (bf16[16,2,768,128]{3,2,1,0:T(8,128)(2,1)}, bf16[16,768,128]{2,1,0:T(8,128)(2,1)}) custom-call(s32[1]{0:T(128)} %bitcast.33.scalars, s32[4,32]{1,0:T(4,128)S(1)} %select_reduce_fusion.table, bf16[16,2,768,128]{3,2,1,0:T(8,128)(2,1)} %cache.3, bf16[16,768,128]{2,1,0:T(8,128)(2,1)} %collective-permute-done.10.lent, ...), custom_call_target="tpu_custom_call" | custom-call | bytes 10485760 | tf_op jit(solution)/shard_map/unpack_blocks/pallas_call | solution.py:197
  287.3 1.7 collective-permute-start.18
  289.0 5.1 %convolution_convert_fusion = bf16[1024,512]{1,0:T(8,128)(2,1)S(1)} fusion(bf16[1024,512]{1,0:T(8,128)(2,1)S(1)} %copy-done, bf16[1024,1024]{1,0:T(8,128)(2,1)} %bitcast.26, s32[1024]{0:T(1024)S(1)} %add.220), kind=kOutput, calls=%fused_computation.26 | convolution fusion | flops 3222798336 | bytes 4198400 | tf_op jit(solution)/shard_map/dot_general | solution.py:380
  294.1 21.1 %all_to_all.20 = bf16[8,128,512]{2,1,0:T(8,128)(2,1)S(1)} all-to-all(bf16[8,128,512]{2,1,0:T(8,128)(2,1)S(1)} %bitcast.141), channel_id=1, replica_groups=mesh['rep'=16,'tp'=8] {'tp'}, dimensions={0} | all-to-all | bytes 2097152 | tf_op jit(solution)/shard_map/all_to_all | solution.py:381
  315.4 1.9 collective-permute-start.8
  317.3 2.8 collective-permute-start.9
  321.0 8.4 %collective-permute-done.9 = bf16[64,512]{1,0:T(8,128)(2,1)S(1)} collective-permute-done((bf16[64,512]{1,0:T(8,128)(2,1)S(1)}, bf16[64,512]{1,0:T(8,128)(2,1)S(1)}, u32[]{:S(2)}, u32[]{:S(2)}) %collective-permute-start.9) | collective-permute-done | bytes 65568 | tf_op jit(solution)/shard_map/ppermute | solution.py:399
  330.1 96.4 %put_other_kind.1 = bf16[16,2,768,128]{3,2,1,0:T(8,128)(2,1)} custom-call(s32[1]{0:T(128)} %bitcast.33.scalars, bf16[16,768,128]{2,1,0:T(8,128)(2,1)} %collective-permute-done.18.returned, bf16[16,2,768,128]{3,2,1,0:T(8,128)(2,1)} %get-tuple-element.79._), custom_call_target="tpu_custom_call", output_to_operand_aliasing={{}: (2, {})} | custom-call | bytes 6291456 | tf_op jit(solution)/shard_map/put_other_kind/pallas_call | solution.py:276
  (89 shorter events, 13.3 us)
Async XLA Ops:
  0.6 288.4 %copy-start = (bf16[1024,512]{1,0:T(8,128)(2,1)S(1)}, bf16[1024,512]{1,0:T(8,128)(2,1)}, u32[]{:S(2)}) copy-start(bf16[1024,512]{1,0:T(8,128)(2,1)} %param.14) | copy-start | bytes 3145732
  8.3 25.8 %all-to-all-start = ((bf16[16,80,512]{2,1,0:T(8,128)(2,1)}), bf16[16,80,512]{2,1,0:T(8,128)(2,1)S(1)}, u32[]{:S(2)}, u32[]{:S(2)}) async-start(bf16[16,80,512]{2,1,0:T(8,128)(2,1)} %copy.53), calls=%async_computation | async-start | bytes 2621440 | tf_op jit(solution)/shard_map/all_to_all | solution.py:319
  15.9 4.5 %copy-start.10 = (bf16[512,2,128]{2,1,0:T(2,128)(2,1)S(1)}, bf16[512,2,128]{2,1,0:T(2,128)(2,1)}, u32[]{:S(2)}) copy-start(bf16[512,2,128]{2,1,0:T(2,128)(2,1)} %param.13) | copy-start | bytes 786436
  19.8 38.5 %collective-permute-start.10 = (bf16[16,768,128]{2,1,0:T(8,128)(2,1)}, bf16[16,768,128]{2,1,0:T(8,128)(2,1)}, u32[]{:S(2)}, u32[]{:S(2)}) collective-permute-start(bf16[16,768,128]{2,1,0:T(8,128)(2,1)} %dynamic-slice_bitcast_fusion), channel_id=1, source_target_pairs={{0,8},{8,0},{16,24},{24,16},{32,40},{40,32},{48,56},{56,48},{64,72... | collective-permute-start | bytes 9437192 | tf_op jit(solution)/shard_map/ppermute | solution.py:308
  44.1 3.2 collective-permute-start.7
  50.8 77.5 %all-to-all-start.1 = ((bf16[8,64,1280]{2,1,0:T(8,128)(2,1)}), bf16[8,64,1280]{2,1,0:T(8,128)(2,1)S(1)}, u32[]{:S(2)}, u32[]{:S(2)}) async-start(bf16[8,64,1280]{2,1,0:T(8,128)(2,1)} %fusion.8), calls=%async_computation.1 | async-start | bytes 2621440 | tf_op jit(solution)/shard_map/all_to_all | solution.py:338
  121.7 20.2 %collective-permute-start.11 = (bf16[24,128,128]{2,1,0:T(8,128)(2,1)}, bf16[24,128,128]{2,1,0:T(8,128)(2,1)S(1)}, u32[]{:S(2)}, u32[]{:S(2)}) collective-permute-start(bf16[24,128,128]{2,1,0:T(8,128)(2,1)} %get-tuple-element.69), channel_id=1, source_target_pairs={{0,16},{8,24},{16,0},{24,8},{32,48},{40,56},{48,32},{56,40},{64,80... | collective-permute-start | bytes 2359304 | tf_op jit(solution)/shard_map/ppermute | solution.py:412
  121.8 20.2 %collective-permute-start.12 = (bf16[24,128,128]{2,1,0:T(8,128)(2,1)}, bf16[24,128,128]{2,1,0:T(8,128)(2,1)}, u32[]{:S(2)}, u32[]{:S(2)}) collective-permute-start(bf16[24,128,128]{2,1,0:T(8,128)(2,1)} %get-tuple-element.70), channel_id=1, source_target_pairs={{0,32},{8,40},{16,48},{24,56},{32,64},{40,72},{48,80},{56,88},{64,... | collective-permute-start | bytes 2359304 | tf_op jit(solution)/shard_map/ppermute | solution.py:412
  121.9 46.6 %collective-permute-start.13 = (bf16[24,128,128]{2,1,0:T(8,128)(2,1)}, bf16[24,128,128]{2,1,0:T(8,128)(2,1)}, u32[]{:S(2)}, u32[]{:S(2)}) collective-permute-start(bf16[24,128,128]{2,1,0:T(8,128)(2,1)} %get-tuple-element.71), channel_id=1, source_target_pairs={{0,48},{8,56},{16,32},{24,40},{32,80},{40,88},{48,64},{56,72},{64,... | collective-permute-start | bytes 2359304 | tf_op jit(solution)/shard_map/ppermute | solution.py:412
  125.3 68.3 %collective-permute-start.14 = (bf16[24,128,128]{2,1,0:T(8,128)(2,1)}, bf16[24,128,128]{2,1,0:T(8,128)(2,1)}, u32[]{:S(2)}, u32[]{:S(2)}) collective-permute-start(bf16[24,128,128]{2,1,0:T(8,128)(2,1)} %get-tuple-element.72), channel_id=1, source_target_pairs={{0,64},{8,72},{16,80},{24,88},{32,96},{40,104},{48,112},{56,120},{... | collective-permute-start | bytes 2359304 | tf_op jit(solution)/shard_map/ppermute | solution.py:412
  133.4 86.1 %collective-permute-start.15 = (bf16[24,128,128]{2,1,0:T(8,128)(2,1)}, bf16[24,128,128]{2,1,0:T(8,128)(2,1)S(1)}, u32[]{:S(2)}, u32[]{:S(2)}) collective-permute-start(bf16[24,128,128]{2,1,0:T(8,128)(2,1)} %get-tuple-element.73), channel_id=1, source_target_pairs={{0,80},{8,88},{16,64},{24,72},{32,112},{40,120},{48,96},{56,104},{... | collective-permute-start | bytes 2359304 | tf_op jit(solution)/shard_map/ppermute | solution.py:412
  142.0 6.6 %copy-start.8 = (bf16[24,128,128]{2,1,0:T(8,128)(2,1)}, bf16[24,128,128]{2,1,0:T(8,128)(2,1)S(1)}, u32[]{:S(2)}) copy-start(bf16[24,128,128]{2,1,0:T(8,128)(2,1)S(1)} %collective-permute-done.11.rest_0_) | copy-start | bytes 2359300
  142.0 77.5 %collective-permute-start.16 = (bf16[24,128,128]{2,1,0:T(8,128)(2,1)}, bf16[24,128,128]{2,1,0:T(8,128)(2,1)}, u32[]{:S(2)}, u32[]{:S(2)}) collective-permute-start(bf16[24,128,128]{2,1,0:T(8,128)(2,1)} %get-tuple-element.74), channel_id=1, source_target_pairs={{0,96},{8,104},{16,112},{24,120},{32,0},{40,8},{48,16},{56,24},{64... | collective-permute-start | bytes 2359304 | tf_op jit(solution)/shard_map/ppermute | solution.py:412
  142.0 77.5 %collective-permute-start.17 = (bf16[24,128,128]{2,1,0:T(8,128)(2,1)}, bf16[24,128,128]{2,1,0:T(8,128)(2,1)}, u32[]{:S(2)}, u32[]{:S(2)}) collective-permute-start(bf16[24,128,128]{2,1,0:T(8,128)(2,1)} %get-tuple-element.75), channel_id=1, source_target_pairs={{0,112},{8,120},{16,96},{24,104},{32,16},{40,24},{48,0},{56,8},{64... | collective-permute-start | bytes 2359304 | tf_op jit(solution)/shard_map/ppermute | solution.py:412
  150.2 138.8 %all-to-all-start.2 = ((bf16[16,64,1024]{2,1,0:T(8,128)(2,1)}), bf16[16,64,1024]{2,1,0:T(8,128)(2,1)}, u32[]{:S(2)}, u32[]{:S(2)}) async-start(bf16[16,64,1024]{2,1,0:T(8,128)(2,1)} %broadcast_in_dim.104), calls=%async_computation.2 | async-start | bytes 4194304 | tf_op jit(solution)/shard_map/all_to_all | solution.py:372
  219.5 0.9 copy-start.9
  287.3 42.8 %collective-permute-start.18 = (bf16[16,768,128]{2,1,0:T(8,128)(2,1)}, bf16[16,768,128]{2,1,0:T(8,128)(2,1)}, u32[]{:S(2)}, u32[]{:S(2)}) collective-permute-start(bf16[16,768,128]{2,1,0:T(8,128)(2,1)} %get-tuple-element.78), channel_id=1, source_target_pairs={{0,8},{8,0},{16,24},{24,16},{32,40},{40,32},{48,56},{56,48},{64,72... | collective-permute-start | bytes 9437192 | tf_op jit(solution)/shard_map/ppermute | solution.py:429
  315.4 5.6 %collective-permute-start.8 = (bf16[64,512]{1,0:T(8,128)(2,1)S(1)}, bf16[64,512]{1,0:T(8,128)(2,1)S(1)}, u32[]{:S(2)}, u32[]{:S(2)}) collective-permute-start(bf16[64,512]{1,0:T(8,128)(2,1)S(1)} %get-tuple-element.98), channel_id=1, source_target_pairs={{0,0},{1,16},{2,32},{3,48},{4,64},{5,80},{6,96},{7,112},{8,8},{9,2... | collective-permute-start | bytes 196616 | tf_op jit(solution)/shard_map/ppermute | solution.py:396
  317.3 12.1 %collective-permute-start.9 = (bf16[64,512]{1,0:T(8,128)(2,1)S(1)}, bf16[64,512]{1,0:T(8,128)(2,1)S(1)}, u32[]{:S(2)}, u32[]{:S(2)}) collective-permute-start(bf16[64,512]{1,0:T(8,128)(2,1)S(1)} %get-tuple-element.99), channel_id=1, source_target_pairs={{0,8},{1,24},{2,40},{3,56},{4,72},{5,88},{6,104},{7,120},{8,0},{9,... | collective-permute-start | bytes 196616 | tf_op jit(solution)/shard_map/ppermute | solution.py:399

commit v3 on v2

--- a/solution.py
+++ b/solution.py
@@ -9,6 +9,7 @@
 BLOCK = 128
 FIRST = 24
 LATER = 8
+VMEM_LIMIT = 32 << 20
 
 
 def chip_shift(reps, shift):
@@ -60,7 +61,7 @@
 
 
 def pack_body(scalars, table, cache, lent, *rest):
-    outs, sem = rest[:-1], rest[-1]
+    outs, held, sem, out_sem = rest[:7], rest[7], rest[8], rest[9]
     core, start = scalars[0], scalars[1]
     room = outs[0].shape[0]
     requests = table.shape[1]
@@ -72,23 +73,23 @@
         low = jnp.maximum(start - place, 0)
         high = jnp.minimum(length, start + room - place)
         own = at // half == core
-        for one, out in enumerate(outs, 1):
-
-            @pl.when((shift == one) & own)
-            def _():
-                @pl.loop(low, high)
-                def _(block):
-                    pltpu.make_async_copy(
-                        blocks_of(cache, row, block, core), out.at[place + block - start], sem
-                    ).start()
-
-            @pl.when((shift == one) & jnp.logical_not(own))
-            def _():
-                @pl.loop(low, high)
-                def _(block):
-                    pltpu.make_async_copy(
-                        blocks_of(lent, row, block), out.at[place + block - start], sem
-                    ).start()
+        line = shift - 1
+
+        @pl.when((shift > 0) & own)
+        def _():
+            @pl.loop(low, high)
+            def _(block):
+                pltpu.make_async_copy(
+                    blocks_of(cache, row, block, core), held.at[line, place + block - start], sem
+                ).start()
+
+        @pl.when((shift > 0) & jnp.logical_not(own))
+        def _():
+            @pl.loop(low, high)
+            def _(block):
+                pltpu.make_async_copy(
+                    blocks_of(lent, row, block), held.at[line, place + block - start], sem
+                ).start()
 
         return total + jnp.where(shift > 0, jnp.maximum(high - low, 0), 0)
 
@@ -96,7 +97,16 @@
 
     @pl.loop(0, total)
     def _(_):
-        pltpu.make_async_copy(outs[0].at[0], outs[0].at[0], sem).wait()
+        pltpu.make_async_copy(held.at[0, 0], held.at[0, 0], sem).wait()
+
+    copies = [
+        pltpu.make_async_copy(held.at[line], out, out_sem.at[line])
+        for line, out in enumerate(outs)
+    ]
+    for copy in copies:
+        copy.start()
+    for copy in copies:
+        copy.wait()
 
 
 def any_space(number):
@@ -119,77 +129,63 @@
         out_shape=[block] * 7,
         in_specs=smem_space(2) + any_space(2),
         out_specs=any_space(7),
-        scratch_shapes=[pltpu.SemaphoreType.DMA],
+        scratch_shapes=[
+            pltpu.VMEM((7,) + block.shape, jnp.bfloat16),
+            pltpu.SemaphoreType.DMA,
+            pltpu.SemaphoreType.DMA((7,)),
+        ],
+        compiler_params=pltpu.CompilerParams(vmem_limit_bytes=VMEM_LIMIT),
         cost_estimate=moved_cost(8 << 20),
         name="pack_blocks",
     )(scalars, table, cache, lent)
 
 
 def unpack_body(scalars, table, cache, lent, *rest):
-    pieces, (moved, theirs, zeros, sem_mine, sem_theirs) = rest[:7], rest[7:]
+    pieces, (moved, theirs, held, sem, out_sem) = rest[:7], rest[7:]
     core = scalars[0]
     room = pieces[0].shape[0]
     half = theirs.shape[0]
-    zeros[...] = jnp.zeros_like(zeros)
     most = cache.shape[2] // BLOCK
 
-    def receive(slot, mine):
-        at = jnp.where(mine, core, 1 - core) * half + slot
-        sem = sem_mine if mine else sem_theirs
+    def receive(at, total):
         shift, place, length, owner = table[0, at], table[1, at], table[2, at], table[3, at]
         row = owner % half
         inside = jnp.where(shift > 0, jnp.clip(room - place, 0, length), length)
-
-        def target(block, many=1):
-            span = pl.ds(pl.multiple_of(block * BLOCK, BLOCK), many * BLOCK)
-            return moved.at[slot, core, span] if mine else theirs.at[slot, span]
-
-        for one, piece in enumerate(pieces, 1):
-
-            @pl.when(shift == one)
+        own = owner // half == core
+
+        def fetch(condition, source):
+            @pl.when(condition)
             def _():
                 @pl.loop(0, inside)
                 def _(block):
-                    pltpu.make_async_copy(piece.at[place + block], target(block), sem).start()
-
-        own = owner // half == core
-
-        @pl.when((shift == 0) & own)
-        def _():
-            @pl.loop(0, inside)
-            def _(block):
-                pltpu.make_async_copy(
-                    blocks_of(cache, row, block, core), target(block), sem
-                ).start()
-
-        @pl.when((shift == 0) & jnp.logical_not(own))
-        def _():
-            @pl.loop(0, inside)
-            def _(block):
-                pltpu.make_async_copy(blocks_of(lent, row, block), target(block), sem).start()
-
-        rest_at = inside
-        for many in (4, 2, 1):
-            hit = (most - inside) & many
-
-            @pl.when(hit > 0)
-            def _():
-                pltpu.make_async_copy(
-                    zeros.at[pl.ds(0, many * BLOCK)], target(rest_at, many), sem
-                ).start()
-
-            rest_at = rest_at + hit
-
-    @pl.loop(0, half)
-    def _(slot):
-        receive(slot, False)
-
-    @pl.loop(0, half)
-    def _(slot):
-        receive(slot, True)
-
-    pltpu.make_async_copy(theirs, theirs, sem_theirs).wait()
-    pltpu.make_async_copy(theirs, theirs, sem_mine).wait()
+                    pltpu.make_async_copy(source(block), blocks_of(held, at, block), sem).start()
+
+        for one, piece in enumerate(pieces, 1):
+            fetch(shift == one, lambda block, piece=piece: piece.at[place + block])
+        fetch((shift == 0) & own, lambda block: blocks_of(cache, row, block, core))
+        fetch((shift == 0) & jnp.logical_not(own), lambda block: blocks_of(lent, row, block))
+
+        @pl.loop(inside, most)
+        def _(block):
+            span = pl.ds(pl.multiple_of(block * BLOCK, BLOCK), BLOCK)
+            held[at, span] = jnp.zeros((BLOCK, HEADDIM), held.dtype)
+
+        return total + inside
+
+    total = lax.fori_loop(0, 2 * half, receive, jnp.int32(0))
+
+    @pl.loop(0, total)
+    def _(_):
+        pltpu.make_async_copy(pieces[0].at[0], pieces[0].at[0], sem).wait()
+
+    copies = [
+        pltpu.make_async_copy(held.at[pl.ds((1 - core) * half, half)], theirs, out_sem.at[0]),
+        pltpu.make_async_copy(held.at[pl.ds(core * half, half)], moved.at[:, core], out_sem.at[1]),
+    ]
+    for copy in copies:
+        copy.start()
+    for copy in copies:
+        copy.wait()
 
 
 def unpack_kernel(core, table, cache, lent, pieces):
@@ -203,20 +199,28 @@
         in_specs=smem_space(2) + any_space(9),
         out_specs=any_space(2),
         scratch_shapes=[
-            pltpu.VMEM((4 * BLOCK, width), jnp.bfloat16),
+            pltpu.VMEM((2 * rows, span, width), jnp.bfloat16),
             pltpu.SemaphoreType.DMA,
-            pltpu.SemaphoreType.DMA,
-        ],
+            pltpu.SemaphoreType.DMA((2,)),
+        ],
+        compiler_params=pltpu.CompilerParams(vmem_limit_bytes=VMEM_LIMIT),
         cost_estimate=moved_cost(10 << 20),
         name="unpack_blocks",
     )(core[None].astype(jnp.int32), table, cache, lent, *pieces)
 
 
 def unpack_more_body(scalars, table, *rest):
-    pieces, (_, _, moved, theirs, sem) = rest[:7], rest[7:]
+    pieces, (_, _, moved, theirs, held, sem) = rest[:7], rest[7:]
     core, start = scalars[0], scalars[1]
     room = pieces[0].shape[0]
     half = theirs.shape[0]
+    fetches = [
+        pltpu.make_async_copy(piece, held.at[line], sem) for line, piece in enumerate(pieces)
+    ]
+    for fetch in fetches:
+        fetch.start()
+    for fetch in fetches:
+        fetch.wait()
 
     def receive(at, total):
         shift, place, length = table[0, at], table[1, at], table[2, at]
@@ -224,23 +228,23 @@
         low = jnp.maximum(start - place, 0)
         high = jnp.minimum(length, start + room - place)
         mine = at // half == core
-        for one, piece in enumerate(pieces, 1):
-
-            @pl.when((shift == one) & mine)
-            def _():
-                @pl.loop(low, high)
-                def _(block):
-                    pltpu.make_async_copy(
-                        piece.at[place + block - start], blocks_of(moved, slot, block, core), sem
-                    ).start()
-
-            @pl.when((shift == one) & jnp.logical_not(mine))
-            def _():
-                @pl.loop(low, high)
-                def _(block):
-                    pltpu.make_async_copy(
-                        piece.at[place + block - start], blocks_of(theirs, slot, block), sem
-                    ).start()
+        line = shift - 1
+
+        @pl.when((shift > 0) & mine)
+        def _():
+            @pl.loop(low, high)
+            def _(block):
+                pltpu.make_async_copy(
+                    held.at[line, place + block - start], blocks_of(moved, slot, block, core), sem
+                ).start()
+
+        @pl.when((shift > 0) & jnp.logical_not(mine))
+        def _():
+            @pl.loop(low, high)
+            def _(block):
+                pltpu.make_async_copy(
+                    held.at[line, place + block - start], blocks_of(theirs, slot, block), sem
+                ).start()
 
         return total + jnp.where(shift > 0, jnp.maximum(high - low, 0), 0)
 
@@ -248,7 +252,7 @@
 
     @pl.loop(0, total)
     def _(_):
-        pltpu.make_async_copy(pieces[0].at[0], pieces[0].at[0], sem).wait()
+        pltpu.make_async_copy(held.at[0, 0], held.at[0, 0], sem).wait()
 
 
 def unpack_more_kernel(core, start, table, pieces, moved, theirs):
@@ -260,16 +264,35 @@
         ],
         in_specs=smem_space(2) + any_space(9),
         out_specs=any_space(2),
-        scratch_shapes=[pltpu.SemaphoreType.DMA],
+        scratch_shapes=[
+            pltpu.VMEM((7,) + pieces[0].shape, jnp.bfloat16),
+            pltpu.SemaphoreType.DMA,
+        ],
+        compiler_params=pltpu.CompilerParams(vmem_limit_bytes=VMEM_LIMIT),
         input_output_aliases={9: 0, 10: 1},
         name="unpack_later_blocks",
     )(jnp.stack([core, start]).astype(jnp.int32), table, *pieces, moved, theirs)
 
 
-def finish_body(scalars, returned, _, moved, sem):
-    copy = pltpu.make_async_copy(returned, moved.at[:, 1 - scalars[0]], sem)
-    copy.start()
-    copy.wait()
+def finish_body(scalars, returned, _, moved, held, in_sem, out_sem):
+    parts = in_sem.shape[0]
+    rows = returned.shape[0] // parts
+    spans = [pl.ds(part * rows, rows) for part in range(parts)]
+    fetches = [
+        pltpu.make_async_copy(returned.at[span], held.at[span], in_sem.at[part])
+        for part, span in enumerate(spans)
+    ]
+    stores = [
+        pltpu.make_async_copy(held.at[span], moved.at[span, 1 - scalars[0]], out_sem.at[part])
+        for part, span in enumerate(spans)
+    ]
+    for fetch in fetches:
+        fetch.start()
+    for fetch, store in zip(fetches, stores):
+        fetch.wait()
+        store.start()
+    for store in stores:
+        store.wait()
 
 
 def finish_kernel(core, returned, moved):
@@ -278,7 +301,12 @@
         out_shape=jax.ShapeDtypeStruct(moved.shape, moved.dtype),
         in_specs=smem_space(1) + any_space(2),
         out_specs=any_space(1)[0],
-        scratch_shapes=[pltpu.SemaphoreType.DMA],
+        scratch_shapes=[
+            pltpu.VMEM(returned.shape, returned.dtype),
+            pltpu.SemaphoreType.DMA((4,)),
+            pltpu.SemaphoreType.DMA((4,)),
+        ],
+        compiler_params=pltpu.CompilerParams(vmem_limit_bytes=VMEM_LIMIT),
         input_output_aliases={2: 0},
         cost_estimate=moved_cost(6 << 20),
         name="put_other_kind",

time: 431 us -> 238 us (0.55)
  Pallas kernels: 226 us -> 16.6 us
  waiting for transfers between devices: 92.6 us -> 103 us
    pallas_call x1, Pallas kernels: 96.4 us -> 2.86 us  [finish_kernel(): pl.pallas_call(finish_body, out_shape=jax.ShapeDtypeStruct(moved.shape, m...]
    pallas_call x1, Pallas kernels: 63.4 us -> 5.37 us  [pack_kernel(): pl.pallas_call(pack_body, out_shape=[block] * 7, in_specs=smem_space(2) +...]
    pallas_call x1, Pallas kernels: 66.3 us -> 8.42 us  [unpack_kernel(): pl.pallas_call(unpack_body, out_shape=[jax.ShapeDtypeStruct(cache.shape,...]
    all_to_all x1, waiting for transfers between devices: 0.01 us -> 10.8 us  [per_device(): lax.all_to_all(jnp.broadcast_to(attended[None], (reps, row_total, head_co...]
    ppermute x7, waiting for transfers between devices: 67.5 us -> 61.5 us  [per_device(): lax.ppermute(piece, 'rep', chip_shift(reps, shift))]
  transfers between devices with their start and end apart: 15 -> 15, of which waited for: 8 -> 10; matrix products, arithmetic and copies ran while one was open for 8% -> 18% of each run, Pallas kernels for 30% -> 6%
where the time goes in v3:
time: 238 us; the launch traced here: 235 us
  waiting for transfers between devices  103 us (43%)
  starting transfers between devices  43.4 us (18%)
  blocking collectives  19.8 us (8%)
  matrix products  18.3 us (8%)
  Pallas kernels  16.6 us (7%)
  local copies, waits for them, and re-layouts  16.2 us (7%)
  other arithmetic  16.1 us (7%)
    ppermute x7, waiting for transfers between devices, per_device(): lax.ppermute(piece, 'rep', chip_shift(reps, shift))  61.5 us
    all_to_all x1, blocking collectives, per_device(): lax.all_to_all(partial_out.astype(jnp.bfloat16).reshape(tps, all_rows //...  19.8 us
    ppermute x7, starting transfers between devices, per_device(): lax.ppermute(piece, 'rep', chip_shift(reps, shift))  13.3 us
    all_to_all x1, waiting for transfers between devices, per_device(): lax.all_to_all(slabs, 'rep', split_axis=0, concat_axis=0, tiled=True)  12.9 us
    all_to_all x1, waiting for transfers between devices, per_device(): lax.all_to_all(jnp.broadcast_to(attended[None], (reps, row_total, head_co...  10.8 us
    ppermute x1, waiting for transfers between devices, per_device(): lax.ppermute(lax.dynamic_index_in_dim(summed, 1 - core, 0, keepdims=False...  10.5 us
    pallas_call x1, Pallas kernels, unpack_kernel(): pl.pallas_call(unpack_body, out_shape=[jax.ShapeDtypeStruct(cache.shape,...  8.42 us
    all_to_all x1, starting transfers between devices, per_device(): lax.all_to_all(jnp.broadcast_to(attended[None], (reps, row_total, head_co...  7.6 us
  transfers between devices with their start and end apart: 15, of which 10 were waited for; matrix products, arithmetic and copies ran while one was open for 18% of the time, Pallas kernels for 6%

profile of v3, /device:TPU:17, one launch (start us, length us, event | category | flops | bytes accessed | tf_op | source)
XLA Modules:
  0.0 235.0 jit_solution(17003009880015010213)
XLA Ops:
  6.5 1.8 copy.53
  8.3 7.6 %all-to-all-start = ((bf16[16,80,512]{2,1,0:T(8,128)(2,1)}), bf16[16,80,512]{2,1,0:T(8,128)(2,1)S(1)}, u32[]{:S(2)}, u32[]{:S(2)}) async-start(bf16[16,80,512]{2,1,0:T(8,128)(2,1)} %copy.53), calls=%async_computation | async-start | bytes 2621440 | tf_op jit(solution)/shard_map/all_to_all | solution.py:347
  15.9 3.9 %dynamic-slice_bitcast_fusion = bf16[16,768,128]{2,1,0:T(8,128)(2,1)} fusion(bf16[16,2,768,128]{3,2,1,0:T(8,128)(2,1)} %cache.3, s32[]{:T(128)S(6)} %select_n.197), kind=kLoop, calls=%fused_computation.8 | loop fusion | bytes 6291460 | tf_op jit(solution)/shard_map/jit(dynamic_index_in_dim)/squeeze | solution.py:337
  21.2 12.9 %all-to-all-done = bf16[16,80,512]{2,1,0:T(8,128)(2,1)S(1)} async-done(((bf16[16,80,512]{2,1,0:T(8,128)(2,1)}), bf16[16,80,512]{2,1,0:T(8,128)(2,1)S(1)}, u32[]{:S(2)}, u32[]{:S(2)}) %all-to-all-start) | async-done | bytes 1310752 | tf_op jit(solution)/shard_map/all_to_all | solution.py:347
  35.8 6.5 %fusion.19 = f32[1024,1280]{1,0:T(8,128)} fusion(bf16[512,256]{1,0:T(8,128)(2,1)} %bitcast.148, bf16[512,1024]{1,0:T(8,128)(2,1)} %param.12, bf16[1024,512]{1,0:T(8,128)(2,1)S(1)} %bitcast.140, s32[1024]{0:T(1024)S(1)} %add.220), kind=kOutput, calls=%fused_computation.30 | convolution fusion | flops 2419589120 | bytes 7606272 | tf_op jit(solution)/shard_map/dot_general | solution.py:360
  42.3 1.9 fusion.18
  44.5 3.0 %collective-permute-done.7 = bf16[8,64,1280]{2,1,0:T(8,128)(2,1)} collective-permute-done((bf16[8,64,1280]{2,1,0:T(8,128)(2,1)S(1)}, bf16[8,64,1280]{2,1,0:T(8,128)(2,1)}, u32[]{:S(2)}, u32[]{:S(2)}) %collective-permute-start.7) | collective-permute-done | bytes 1310752 | tf_op jit(solution)/shard_map/ppermute | solution.py:364
  47.4 3.6 %fusion.8 = bf16[8,64,1280]{2,1,0:T(8,128)(2,1)} fusion(bf16[8,64,1280]{2,1,0:T(8,128)(2,1)} %collective-permute-done.7, f32[8,2,64,1280]{3,2,1,0:T(8,128)} %bitcast.139, s32[]{:T(128)S(6)} %select_n.196), kind=kLoop, calls=%fused_computation.14 | loop fusion | flops 1966080 | bytes 5242884 | tf_op jit(solution)/shard_map/convert_element_type | solution.py:365
  51.0 6.5 %all-to-all-start.1 = ((bf16[8,64,1280]{2,1,0:T(8,128)(2,1)}), bf16[8,64,1280]{2,1,0:T(8,128)(2,1)}, u32[]{:S(2)}, u32[]{:S(2)}) async-start(bf16[8,64,1280]{2,1,0:T(8,128)(2,1)} %fusion.8), calls=%async_computation.1 | async-start | bytes 2621440 | tf_op jit(solution)/shard_map/all_to_all | solution.py:366
  60.9 5.4 %pack_blocks.2 = (bf16[24,128,128]{2,1,0:T(8,128)(2,1)}, bf16[24,128,128]{2,1,0:T(8,128)(2,1)}, bf16[24,128,128]{2,1,0:T(8,128)(2,1)}, bf16[24,128,128]{2,1,0:T(...) custom-call(s32[2]{0:T(128)S(1)} %pad_add_fusion.2.scalars, ...), custom_call_target="tpu_custom_call" | custom-call | bytes 8388608 | tf_op jit(solution)/shard_map/pack_blocks/pallas_call | solution.py:127
  67.8 3.6 %collective-permute-start.13 = (bf16[24,128,128]{2,1,0:T(8,128)(2,1)}, bf16[24,128,128]{2,1,0:T(8,128)(2,1)S(1)}, u32[]{:S(2)}, u32[]{:S(2)}) collective-permute-start(bf16[24,128,128]{2,1,0:T(8,128)(2,1)} %get-tuple-element.71), channel_id=1, source_target_pairs={{0,48},{8,56},{16,32},{24,40},{32,80},{40,88},{48,64},{56,72},{64,... | collective-permute-start | bytes 2359304 | tf_op jit(solution)/shard_map/ppermute | solution.py:440
  72.9 4.0 %all-to-all-done.1 = bf16[8,64,1280]{2,1,0:T(8,128)(2,1)} async-done(((bf16[8,64,1280]{2,1,0:T(8,128)(2,1)}), bf16[8,64,1280]{2,1,0:T(8,128)(2,1)}, u32[]{:S(2)}, u32[]{:S(2)}) %all-to-all-start.1) | async-done | bytes 1310752 | tf_op jit(solution)/shard_map/all_to_all | solution.py:366
  76.9 2.2 reduce_sum.72
  82.8 3.1 %bitcast_reduce_fusion = (f32[16,8,4]{1,2,0:T(4,128)S(1)}, f32[16,4,8,768]{3,2,1,0:T(8,128)S(1)}) fusion(bf16[16,2,768,128]{3,2,1,0:T(8,128)(2,1)} %cache.3, pred[16,768]{1,0:T(8,128)(4,1)S(1)} %iota_compare_fusion.7, bf16[4,16,8,128]{3,2,1,0:T(8,128)(2,1)S(1)} %bitcast.142), kind=kOutput, calls=%fused_computation.22 | convolution fusion | flops 101842432 | bytes 4864000 | tf_op jit(solution)/shard_map/trgd,rld->rgtl/dot_general | solution.py:376
  87.6 2.0 collective-permute-start.15
  90.4 1.9 collective-permute-start.16
  92.8 2.7 %collective-permute-start.17 = (bf16[24,128,128]{2,1,0:T(8,128)(2,1)}, bf16[24,128,128]{2,1,0:T(8,128)(2,1)}, u32[]{:S(2)}, u32[]{:S(2)}) collective-permute-start(bf16[24,128,128]{2,1,0:T(8,128)(2,1)} %get-tuple-element.75), channel_id=1, source_target_pairs={{0,112},{8,120},{16,96},{24,104},{32,16},{40,24},{48,0},{56,8},{64... | collective-permute-start | bytes 2359304 | tf_op jit(solution)/shard_map/ppermute | solution.py:440
  95.5 2.6 %fusion.29 = bf16[4,16,8,128]{3,2,0,1:T(8,128)(2,1)S(1)} fusion(f32[4,16,8,128]{3,2,0,1:T(8,128)S(1)} %convolution_bitcast_fusion, bf16[16,2,768,128]{3,2,1,0:T(8,128)(2,1)} %cache.3, f32[16,4,8,768]{3,2,1,0:T(8,128)S(1)} %get-tuple-element.109, f32[16,8,4]{1,2,0:T(4,128)S(1)} %add.224, f32[16,8,4]{1,2,0:T(4,128)S(1)} %max.7), kind=kOutput, calls=%fused_computation.37 | convolution fusion | flops 101974016 | bytes 5115904 | tf_op jit(solution)/shard_map/rgtl,rld->trgd/dot_general | solution.py:392
  98.2 1.6 broadcast_in_dim.104
  99.8 7.6 %all-to-all-start.2 = ((bf16[16,64,1024]{2,1,0:T(8,128)(2,1)}), bf16[16,64,1024]{2,1,0:T(8,128)(2,1)}, u32[]{:S(2)}, u32[]{:S(2)}) async-start(bf16[16,64,1024]{2,1,0:T(8,128)(2,1)} %broadcast_in_dim.104), calls=%async_computation.2 | async-start | bytes 4194304 | tf_op jit(solution)/shard_map/all_to_all | solution.py:400
  107.7 14.3 %collective-permute-done.13.rest_2_ = bf16[24,128,128]{2,1,0:T(8,128)(2,1)S(1)} collective-permute-done((bf16[24,128,128]{2,1,0:T(8,128)(2,1)}, bf16[24,128,128]{2,1,0:T(8,128)(2,1)S(1)}, u32[]{:S(2)}, u32[]{:S(2)}) %collective-permute-start.13) | collective-permute-done | bytes 786464 | tf_op jit(solution)/shard_map/ppermute | solution.py:440
  122.0 20.9 %collective-permute-done.14.rest_3_ = bf16[24,128,128]{2,1,0:T(8,128)(2,1)} collective-permute-done((bf16[24,128,128]{2,1,0:T(8,128)(2,1)}, bf16[24,128,128]{2,1,0:T(8,128)(2,1)}, u32[]{:S(2)}, u32[]{:S(2)}) %collective-permute-start.14) | collective-permute-done | bytes 786464 | tf_op jit(solution)/shard_map/ppermute | solution.py:440
  142.9 25.1 %collective-permute-done.15.rest_4_ = bf16[24,128,128]{2,1,0:T(8,128)(2,1)} collective-permute-done((bf16[24,128,128]{2,1,0:T(8,128)(2,1)}, bf16[24,128,128]{2,1,0:T(8,128)(2,1)}, u32[]{:S(2)}, u32[]{:S(2)}) %collective-permute-start.15) | collective-permute-done | bytes 786464 | tf_op jit(solution)/shard_map/ppermute | solution.py:440
  168.0 8.4 %unpack_blocks.1 = (bf16[16,2,768,128]{3,2,1,0:T(8,128)(2,1)}, bf16[16,768,128]{2,1,0:T(8,128)(2,1)}) custom-call(s32[1]{0:T(128)} %bitcast.33.scalars, s32[4,32]{1,0:T(4,128)S(1)} %select_reduce_fusion.table, bf16[16,2,768,128]{3,2,1,0:T(8,128)(2,1)} %cache.3, bf16[16,768,128]{2,1,0:T(8,128)(2,1)} %collective-permute-done.10.lent, ...), custom_call_target="tpu_custom_call" | custom-call | bytes 10485760 | tf_op jit(solution)/shard_map/unpack_blocks/pallas_call | solution.py:193
  177.1 1.7 collective-permute-start.18
  178.8 10.8 %all-to-all-done.2 = bf16[16,64,1024]{2,1,0:T(8,128)(2,1)} async-done(((bf16[16,64,1024]{2,1,0:T(8,128)(2,1)}), bf16[16,64,1024]{2,1,0:T(8,128)(2,1)}, u32[]{:S(2)}, u32[]{:S(2)}) %all-to-all-start.2) | async-done | bytes 2097184 | tf_op jit(solution)/shard_map/all_to_all | solution.py:400
  189.6 5.1 %convolution_convert_fusion = bf16[1024,512]{1,0:T(8,128)(2,1)S(1)} fusion(bf16[1024,512]{1,0:T(8,128)(2,1)S(1)} %copy-done, bf16[1024,1024]{1,0:T(8,128)(2,1)} %bitcast.26, s32[1024]{0:T(1024)S(1)} %copy-done.5), kind=kOutput, calls=%fused_computation.26 | convolution fusion | flops 3222798336 | bytes 4198400 | tf_op jit(solution)/shard_map/dot_general | solution.py:408
  194.7 19.8 %all_to_all.20 = bf16[8,128,512]{2,1,0:T(8,128)(2,1)S(1)} all-to-all(bf16[8,128,512]{2,1,0:T(8,128)(2,1)S(1)} %bitcast.141), channel_id=1, replica_groups=mesh['rep'=16,'tp'=8] {'tp'}, dimensions={0} | all-to-all | bytes 2097152 | tf_op jit(solution)/shard_map/all_to_all | solution.py:409
  214.7 2.6 %collective-permute-start.8 = (bf16[64,512]{1,0:T(8,128)(2,1)S(1)}, bf16[64,512]{1,0:T(8,128)(2,1)S(1)}, u32[]{:S(2)}, u32[]{:S(2)}) collective-permute-start(bf16[64,512]{1,0:T(8,128)(2,1)S(1)} %get-tuple-element.98), channel_id=1, source_target_pairs={{0,0},{1,16},{2,32},{3,48},{4,64},{5,80},{6,96},{7,112},{8,8},{9,2... | collective-permute-start | bytes 196616 | tf_op jit(solution)/shard_map/ppermute | solution.py:424
  217.3 3.4 %collective-permute-start.9 = (bf16[64,512]{1,0:T(8,128)(2,1)S(1)}, bf16[64,512]{1,0:T(8,128)(2,1)S(1)}, u32[]{:S(2)}, u32[]{:S(2)}) collective-permute-start(bf16[64,512]{1,0:T(8,128)(2,1)S(1)} %get-tuple-element.99), channel_id=1, source_target_pairs={{0,8},{1,24},{2,40},{3,56},{4,72},{5,88},{6,104},{7,120},{8,0},{9,... | collective-permute-start | bytes 196616 | tf_op jit(solution)/shard_map/ppermute | solution.py:427
  220.7 10.5 %collective-permute-done.9 = bf16[64,512]{1,0:T(8,128)(2,1)S(1)} collective-permute-done((bf16[64,512]{1,0:T(8,128)(2,1)S(1)}, bf16[64,512]{1,0:T(8,128)(2,1)S(1)}, u32[]{:S(2)}, u32[]{:S(2)}) %collective-permute-start.9) | collective-permute-done | bytes 65568 | tf_op jit(solution)/shard_map/ppermute | solution.py:427
  231.9 2.9 %put_other_kind.1 = bf16[16,2,768,128]{3,2,1,0:T(8,128)(2,1)} custom-call(s32[1]{0:T(128)} %bitcast.33.scalars, bf16[16,768,128]{2,1,0:T(8,128)(2,1)} %collective-permute-done.18.returned, bf16[16,2,768,128]{3,2,1,0:T(8,128)(2,1)} %get-tuple-element.79._), custom_call_target="tpu_custom_call", output_to_operand_aliasing={{}: (2, {})} | custom-call | bytes 6291456 | tf_op jit(solution)/shard_map/put_other_kind/pallas_call | solution.py:299
  (99 shorter events, 23.9 us)
Async XLA Ops:
  0.6 188.9 %copy-start = (bf16[1024,512]{1,0:T(8,128)(2,1)S(1)}, bf16[1024,512]{1,0:T(8,128)(2,1)}, u32[]{:S(2)}) copy-start(bf16[1024,512]{1,0:T(8,128)(2,1)} %param.14) | copy-start | bytes 3145732
  8.3 25.8 %all-to-all-start = ((bf16[16,80,512]{2,1,0:T(8,128)(2,1)}), bf16[16,80,512]{2,1,0:T(8,128)(2,1)S(1)}, u32[]{:S(2)}, u32[]{:S(2)}) async-start(bf16[16,80,512]{2,1,0:T(8,128)(2,1)} %copy.53), calls=%async_computation | async-start | bytes 2621440 | tf_op jit(solution)/shard_map/all_to_all | solution.py:347
  15.9 4.5 %copy-start.2 = (bf16[512,2,128]{2,1,0:T(2,128)(2,1)S(1)}, bf16[512,2,128]{2,1,0:T(2,128)(2,1)}, u32[]{:S(2)}) copy-start(bf16[512,2,128]{2,1,0:T(2,128)(2,1)} %param.13) | copy-start | bytes 786436
  19.8 41.0 %collective-permute-start.10 = (bf16[16,768,128]{2,1,0:T(8,128)(2,1)}, bf16[16,768,128]{2,1,0:T(8,128)(2,1)}, u32[]{:S(2)}, u32[]{:S(2)}) collective-permute-start(bf16[16,768,128]{2,1,0:T(8,128)(2,1)} %dynamic-slice_bitcast_fusion), channel_id=1, source_target_pairs={{0,8},{8,0},{16,24},{24,16},{32,40},{40,32},{48,56},{56,48},{64,72... | collective-permute-start | bytes 9437192 | tf_op jit(solution)/shard_map/ppermute | solution.py:336
  35.7 6.6 %copy-start.4 = (s32[1024]{0:T(1024)}, s32[1024]{0:T(1024)S(1)}, u32[]{:S(2)}) copy-start(s32[1024]{0:T(1024)S(1)} %add.220) | copy-start | bytes 12292
  44.2 3.2 %collective-permute-start.7 = (bf16[8,64,1280]{2,1,0:T(8,128)(2,1)S(1)}, bf16[8,64,1280]{2,1,0:T(8,128)(2,1)}, u32[]{:S(2)}, u32[]{:S(2)}) collective-permute-start(bf16[8,64,1280]{2,1,0:T(8,128)(2,1)S(1)} %fusion.18), channel_id=1, source_target_pairs={{0,8},{8,0},{16,24},{24,16},{32,40},{40,32},{48,56},{56,48},{64,72... | collective-permute-start | bytes 3932168 | tf_op jit(solution)/shard_map/ppermute | solution.py:364
  51.0 25.9 %all-to-all-start.1 = ((bf16[8,64,1280]{2,1,0:T(8,128)(2,1)}), bf16[8,64,1280]{2,1,0:T(8,128)(2,1)}, u32[]{:S(2)}, u32[]{:S(2)}) async-start(bf16[8,64,1280]{2,1,0:T(8,128)(2,1)} %fusion.8), calls=%async_computation.1 | async-start | bytes 2621440 | tf_op jit(solution)/shard_map/all_to_all | solution.py:366
  66.2 24.1 %collective-permute-start.11 = (bf16[24,128,128]{2,1,0:T(8,128)(2,1)}, bf16[24,128,128]{2,1,0:T(8,128)(2,1)S(1)}, u32[]{:S(2)}, u32[]{:S(2)}) collective-permute-start(bf16[24,128,128]{2,1,0:T(8,128)(2,1)} %get-tuple-element.69), channel_id=1, source_target_pairs={{0,16},{8,24},{16,0},{24,8},{32,48},{40,56},{48,32},{56,40},{64,80... | collective-permute-start | bytes 2359304 | tf_op jit(solution)/shard_map/ppermute | solution.py:440
  66.4 26.4 %collective-permute-start.12 = (bf16[24,128,128]{2,1,0:T(8,128)(2,1)}, bf16[24,128,128]{2,1,0:T(8,128)(2,1)S(1)}, u32[]{:S(2)}, u32[]{:S(2)}) collective-permute-start(bf16[24,128,128]{2,1,0:T(8,128)(2,1)} %get-tuple-element.70), channel_id=1, source_target_pairs={{0,32},{8,40},{16,48},{24,56},{32,64},{40,72},{48,80},{56,88},{64,... | collective-permute-start | bytes 2359304 | tf_op jit(solution)/shard_map/ppermute | solution.py:440
  67.8 54.2 %collective-permute-start.13 = (bf16[24,128,128]{2,1,0:T(8,128)(2,1)}, bf16[24,128,128]{2,1,0:T(8,128)(2,1)S(1)}, u32[]{:S(2)}, u32[]{:S(2)}) collective-permute-start(bf16[24,128,128]{2,1,0:T(8,128)(2,1)} %get-tuple-element.71), channel_id=1, source_target_pairs={{0,48},{8,56},{16,32},{24,40},{32,80},{40,88},{48,64},{56,72},{64,... | collective-permute-start | bytes 2359304 | tf_op jit(solution)/shard_map/ppermute | solution.py:440
  71.3 71.5 %collective-permute-start.14 = (bf16[24,128,128]{2,1,0:T(8,128)(2,1)}, bf16[24,128,128]{2,1,0:T(8,128)(2,1)}, u32[]{:S(2)}, u32[]{:S(2)}) collective-permute-start(bf16[24,128,128]{2,1,0:T(8,128)(2,1)} %get-tuple-element.72), channel_id=1, source_target_pairs={{0,64},{8,72},{16,80},{24,88},{32,96},{40,104},{48,112},{56,120},{... | collective-permute-start | bytes 2359304 | tf_op jit(solution)/shard_map/ppermute | solution.py:440
  82.8 3.1 %copy-start.1 = (bf16[4,16,2,128]{3,2,1,0:T(2,128)(2,1)S(1)}, bf16[4,16,2,128]{3,2,1,0:T(2,128)(2,1)}, u32[]{:S(2)}) copy-start(bf16[4,16,2,128]{3,2,1,0:T(2,128)(2,1)} %reshape.724) | copy-start | bytes 98308
  82.8 3.2 %copy-start.8 = (pred[4,4]{1,0:T(4,128)(4,1)S(1)}, pred[4,4]{1,0:T(4,128)(4,1)}, u32[]{:S(2)}) copy-start(pred[4,4]{1,0:T(4,128)(4,1)} %iota_compare_fusion.11) | copy-start | bytes 52
  87.6 80.4 %collective-permute-start.15 = (bf16[24,128,128]{2,1,0:T(8,128)(2,1)}, bf16[24,128,128]{2,1,0:T(8,128)(2,1)}, u32[]{:S(2)}, u32[]{:S(2)}) collective-permute-start(bf16[24,128,128]{2,1,0:T(8,128)(2,1)} %get-tuple-element.73), channel_id=1, source_target_pairs={{0,80},{8,88},{16,64},{24,72},{32,112},{40,120},{48,96},{56,104},{... | collective-permute-start | bytes 2359304 | tf_op jit(solution)/shard_map/ppermute | solution.py:440
  90.4 77.6 %collective-permute-start.16 = (bf16[24,128,128]{2,1,0:T(8,128)(2,1)}, bf16[24,128,128]{2,1,0:T(8,128)(2,1)}, u32[]{:S(2)}, u32[]{:S(2)}) collective-permute-start(bf16[24,128,128]{2,1,0:T(8,128)(2,1)} %get-tuple-element.74), channel_id=1, source_target_pairs={{0,96},{8,104},{16,112},{24,120},{32,0},{40,8},{48,16},{56,24},{64... | collective-permute-start | bytes 2359304 | tf_op jit(solution)/shard_map/ppermute | solution.py:440
  92.8 75.2 %collective-permute-start.17 = (bf16[24,128,128]{2,1,0:T(8,128)(2,1)}, bf16[24,128,128]{2,1,0:T(8,128)(2,1)}, u32[]{:S(2)}, u32[]{:S(2)}) collective-permute-start(bf16[24,128,128]{2,1,0:T(8,128)(2,1)} %get-tuple-element.75), channel_id=1, source_target_pairs={{0,112},{8,120},{16,96},{24,104},{32,16},{40,24},{48,0},{56,8},{64... | collective-permute-start | bytes 2359304 | tf_op jit(solution)/shard_map/ppermute | solution.py:440
  99.8 7.6 %copy-start.6 = (s32[256]{0:T(256)S(1)}, s32[256]{0:T(256)}, u32[]{:S(2)}) copy-start(s32[256]{0:T(256)} %eq.59) | copy-start | bytes 3076
  99.8 7.6 %copy-start.7 = (s32[32]{0:T(128)S(1)}, s32[32]{0:T(128)}, u32[]{:S(2)}) copy-start(s32[32]{0:T(128)} %iota_add_fusion) | copy-start | bytes 388
  99.8 7.7 %copy-start.3 = (s32[4,256]{1,0:T(4,128)S(1)}, s32[4,256]{1,0:T(4,128)}, u32[]{:S(2)}) copy-start(s32[4,256]{1,0:T(4,128)} %pad_add_fusion.1) | copy-start | bytes 12292
  99.8 89.8 %all-to-all-start.2 = ((bf16[16,64,1024]{2,1,0:T(8,128)(2,1)}), bf16[16,64,1024]{2,1,0:T(8,128)(2,1)}, u32[]{:S(2)}, u32[]{:S(2)}) async-start(bf16[16,64,1024]{2,1,0:T(8,128)(2,1)} %broadcast_in_dim.104), calls=%async_computation.2 | async-start | bytes 4194304 | tf_op jit(solution)/shard_map/all_to_all | solution.py:400
  176.4 13.1 %copy-start.5 = (s32[1024]{0:T(1024)S(1)}, s32[1024]{0:T(1024)}, u32[]{:S(2)}) copy-start(s32[1024]{0:T(1024)} %copy-done.4) | copy-start | bytes 12292
  177.1 54.9 %collective-permute-start.18 = (bf16[16,768,128]{2,1,0:T(8,128)(2,1)}, bf16[16,768,128]{2,1,0:T(8,128)(2,1)}, u32[]{:S(2)}, u32[]{:S(2)}) collective-permute-start(bf16[16,768,128]{2,1,0:T(8,128)(2,1)} %get-tuple-element.78), channel_id=1, source_target_pairs={{0,8},{8,0},{16,24},{24,16},{32,40},{40,32},{48,56},{56,48},{64,72... | collective-permute-start | bytes 9437192 | tf_op jit(solution)/shard_map/ppermute | solution.py:457
  214.7 6.0 %collective-permute-start.8 = (bf16[64,512]{1,0:T(8,128)(2,1)S(1)}, bf16[64,512]{1,0:T(8,128)(2,1)S(1)}, u32[]{:S(2)}, u32[]{:S(2)}) collective-permute-start(bf16[64,512]{1,0:T(8,128)(2,1)S(1)} %get-tuple-element.98), channel_id=1, source_target_pairs={{0,0},{1,16},{2,32},{3,48},{4,64},{5,80},{6,96},{7,112},{8,8},{9,2... | collective-permute-start | bytes 196616 | tf_op jit(solution)/shard_map/ppermute | solution.py:424
  217.3 14.0 %collective-permute-start.9 = (bf16[64,512]{1,0:T(8,128)(2,1)S(1)}, bf16[64,512]{1,0:T(8,128)(2,1)S(1)}, u32[]{:S(2)}, u32[]{:S(2)}) collective-permute-start(bf16[64,512]{1,0:T(8,128)(2,1)S(1)} %get-tuple-element.99), channel_id=1, source_target_pairs={{0,8},{1,24},{2,40},{3,56},{4,72},{5,88},{6,104},{7,120},{8,0},{9,... | collective-permute-start | bytes 196616 | tf_op jit(solution)/shard_map/ppermute | solution.py:427

commit v4 on v1

v4 whole, which is shorter than its diff:
```python
import jax
import jax.numpy as jnp
from jax import lax
from jax.experimental import pallas as pl
from jax.experimental.pallas import tpu as pltpu
from jax.sharding import PartitionSpec as P

HEADDIM = 128
BLOCK = 128
ROOM = 38
LATER = 4
VMEM_LIMIT = 56 << 20


def line_pairs(reps, line, along_first):
    across, pairs = reps // 4, []
    for one in range(reps):
        x, y, core = one // 4, one // 2 % 2, one % 2
        if core == along_first:
            pairs.append((one, (x + (1, 3, 2)[line]) % across * 4 + y * 2 + core))
        elif line < 2:
            pairs.append((one, x * 4 + (1 - y) * 2 + core))
    return pairs


def places(key, lengths):
    order = jnp.arange(key.shape[0])
    before = (key[:, None] == key[None, :]) & (order[None, :] < order[:, None])
    return jnp.sum(jnp.where(before, lengths[None, :], 0), axis=-1)


def x_leg(source, target, key, lengths):
    along = (target // 2 - source // 2) % 4
    moves = along > 0
    place = places(key, jnp.where(moves, lengths, 0))
    line = jnp.where(along == 1, 0, jnp.where(along == 3, 1, 2))
    return moves, line * ROOM + place, jnp.where(moves, ROOM - place, lengths)


def y_leg(source, target, key, lengths):
    moves = target % 2 != source % 2
    place = places(key, jnp.where(moves, lengths, 0))
    return moves, place, jnp.where(moves, 2 * ROOM - place, lengths)


def first_leg(core, source, target, lengths):
    x = x_leg(source, target, source * 4 + target // 2, lengths)
    y = y_leg(source, target, source * 2 + target % 2, lengths)
    return [jnp.where(core == 0, one, other) for one, other in zip(x, y)]


def second_leg(core, source, target, lengths):
    x = x_leg(source, target, source // 2 * 8 + target, lengths)
    y = y_leg(source, target, source % 2 * 8 + target, lengths)
    return [jnp.where(core == 0, one, other) for one, other in zip(y, x)]


def pick(match, fields):
    return jnp.sum(jnp.where(match[None], jnp.stack(fields)[:, None, :], 0), axis=-1).astype(
        jnp.int32
    )


def blocks_of(cache, rows, block, core=None):
    span = pl.ds(pl.multiple_of(block * BLOCK, BLOCK), BLOCK)
    if core is None:
        return cache.at[rows, span]
    return cache.at[rows, core, span]


def fetch_blocks(entry, core, cache, lent, legs, put, sem):
    place, at, count = entry

    def fetch(condition, source):
        @pl.when(condition)
        def _():
            @pl.loop(0, count)
            def _(block):
                pltpu.make_async_copy(source(block), put(block), sem).start()

    fetch(place == 1, lambda block: blocks_of(cache, at, block, core))
    fetch(place == 2, lambda block: blocks_of(lent, at, block))
    for number, lines in enumerate(legs, 3):

        @pl.when(place == number)
        def _():
            @pl.loop(0, count)
            def _(block):
                spot = at + block
                for one, line in enumerate(lines):

                    @pl.when(spot // ROOM == one)
                    def _():
                        pltpu.make_async_copy(
                            line.at[spot - one * ROOM], put(block), sem
                        ).start()

    return jnp.where(place > 0, jnp.maximum(count, 0), 0)


def wait_blocks(total, example, sem):
    @pl.loop(0, total)
    def _(_):
        pltpu.make_async_copy(example, example, sem).wait()


def pack_body(core, table, cache, lent, *rest):
    lines, (out, held, sem, out_sem) = rest[:-6], (rest[-6:-3],) + rest[-3:]

    def send(at, total):
        to = table[2, at]
        entry = (table[0, at], table[1, at], table[3, at])
        return total + fetch_blocks(
            entry, core[0], cache, lent, [lines], lambda block: held.at[to + block], sem
        )

    total = lax.fori_loop(0, table.shape[1], send, jnp.int32(0))
    wait_blocks(total, held.at[0], sem)
    copies = [
        pltpu.make_async_copy(held.at[pl.ds(line * ROOM, ROOM)], one, out_sem.at[line])
        for line, one in enumerate(out)
    ]
    for copy in copies:
        copy.start()
    for copy in copies:
        copy.wait()


def any_space(number):
    return [pl.BlockSpec(memory_space=pl.ANY)] * number


def smem_space(number):
    return [pl.BlockSpec(memory_space=pltpu.SMEM)] * number


def moved_cost(size):
    return pl.CostEstimate(flops=0, bytes_accessed=size, transcendentals=0)


def pack_kernel(core, table, cache, lent, lines):
    line = jax.ShapeDtypeStruct((ROOM, BLOCK, HEADDIM), jnp.bfloat16)
    return pl.pallas_call(
        pack_body,
        out_shape=[line] * 3,
        in_specs=smem_space(2) + any_space(2 + len(lines)),
        out_specs=any_space(3),
        scratch_shapes=[
            pltpu.VMEM((3 * ROOM, BLOCK, HEADDIM), jnp.bfloat16),
            pltpu.SemaphoreType.DMA,
            pltpu.SemaphoreType.DMA((3,)),
        ],
        compiler_params=pltpu.CompilerParams(vmem_limit_bytes=VMEM_LIMIT),
        cost_estimate=moved_cost(8 << 20),
        name="pack_blocks",
    )(core[None].astype(jnp.int32), table, cache, lent, *lines)


def unpack_body(scalars, table, cache, lent, *rest):
    first, second, rest = rest[:3], rest[3:6], rest[6:]
    _, moved, theirs, held, sem, out_sem = rest
    core = scalars[0]
    half = theirs.shape[0]
    most = cache.shape[2] // BLOCK

    def receive(at, total):
        count = table[2, at]
        entry = (table[0, at], table[1, at], count)

        @pl.loop(count, most)
        def _(block):
            span = pl.ds(pl.multiple_of(block * BLOCK, BLOCK), BLOCK)
            held[at, span] = jnp.zeros((BLOCK, HEADDIM), held.dtype)

        return total + fetch_blocks(
            entry, core, cache, lent, [first, second], lambda block: blocks_of(held, at, block), sem
        )

    total = lax.fori_loop(0, 2 * half, receive, jnp.int32(0))
    wait_blocks(total, first[0].at[0], sem)
    copies = [
        pltpu.make_async_copy(held.at[pl.ds((1 - core) * half, half)], theirs, out_sem.at[0]),
        pltpu.make_async_copy(held.at[pl.ds(core * half, half)], moved.at[:, core], out_sem.at[1]),
    ]
    for copy in copies:
        copy.start()
    for copy in copies:
        copy.wait()


def unpack_kernel(core, table, cache, lent, first, second, after):
    rows, _, span, width = cache.shape
    return pl.pallas_call(
        unpack_body,
        out_shape=[
            jax.ShapeDtypeStruct(cache.shape, jnp.bfloat16),
            jax.ShapeDtypeStruct((rows, span, width), jnp.bfloat16),
        ],
        in_specs=smem_space(2) + any_space(9),
        out_specs=any_space(2),
        scratch_shapes=[
            pltpu.VMEM((2 * rows, span, width), jnp.bfloat16),
            pltpu.SemaphoreType.DMA,
            pltpu.SemaphoreType.DMA((2,)),
        ],
        compiler_params=pltpu.CompilerParams(vmem_limit_bytes=VMEM_LIMIT),
        cost_estimate=moved_cost(10 << 20),
        name="unpack_blocks",
    )(core[None].astype(jnp.int32), table, cache, lent, *first, *second, after)


def pack_more_body(scalars, table, cache, lent, out, held, sem):
    core, start = scalars[0], scalars[1]
    room = out.shape[1]
    requests = table.shape[1]
    half = requests // 2

    def send(at, total):
        line, place, skip, left = (table[field, at] for field in range(4))
        low = jnp.maximum(start - place, 0)
        count = jnp.maximum(jnp.minimum(left, start + room - place) - low, 0)

        def fetch(condition, source):
            @pl.when(condition)
            def _():
                @pl.loop(0, count)
                def _(block):
                    pltpu.make_async_copy(
                        source(skip + low + block), held.at[line, place + low + block - start], sem
                    ).start()

        row = at % half
        fetch(at // half == core, lambda block: blocks_of(cache, row, block, core))
        fetch(at // half != core, lambda block: blocks_of(lent, row, block))
        return total + count

    total = lax.fori_loop(0, requests, send, jnp.int32(0))
    wait_blocks(total, held.at[0, 0], sem)
    copy = pltpu.make_async_copy(held, out, sem)
    copy.start()
    copy.wait()


def pack_more_kernel(core, start, table, cache, lent, chips):
    lines = jax.ShapeDtypeStruct((chips, LATER, BLOCK, HEADDIM), jnp.bfloat16)
    return pl.pallas_call(
        pack_more_body,
        out_shape=lines,
        in_specs=smem_space(2) + any_space(2),
        out_specs=any_space(1)[0],
        scratch_shapes=[pltpu.VMEM(lines.shape, lines.dtype), pltpu.SemaphoreType.DMA],
        compiler_params=pltpu.CompilerParams(vmem_limit_bytes=VMEM_LIMIT),
        name="pack_later_blocks",
    )(jnp.stack([core, start]).astype(jnp.int32), table, cache, lent)


def unpack_more_body(scalars, table, pieces, _moved, _theirs, moved, theirs, held, sem):
    core, start = scalars[0], scalars[1]
    room = pieces.shape[1]
    half = theirs.shape[0]
    copy = pltpu.make_async_copy(pieces, held, sem)
    copy.start()
    copy.wait()

    def receive(at, total):
        line, place, skip, left = (table[field, at] for field in range(4))
        slot = at % half
        low = jnp.maximum(start - place, 0)
        count = jnp.maximum(jnp.minimum(left, start + room - place) - low, 0)

        def put(condition, target):
            @pl.when(condition)
            def _():
                @pl.loop(0, count)
                def _(block):
                    pltpu.make_async_copy(
                        held.at[line, place + low + block - start], target(skip + low + block), sem
                    ).start()

        put(at // half == core, lambda block: blocks_of(moved, slot, block, core))
        put(at // half != core, lambda block: blocks_of(theirs, slot, block))
        return total + count

    total = lax.fori_loop(0, 2 * half, receive, jnp.int32(0))
    wait_blocks(total, held.at[0, 0], sem)


def unpack_more_kernel(core, start, table, pieces, moved, theirs):
    return pl.pallas_call(
        unpack_more_body,
        out_shape=[
            jax.ShapeDtypeStruct(moved.shape, moved.dtype),
            jax.ShapeDtypeStruct(theirs.shape, theirs.dtype),
        ],
        in_specs=smem_space(2) + any_space(3),
        out_specs=any_space(2),
        scratch_shapes=[pltpu.VMEM(pieces.shape, pieces.dtype), pltpu.SemaphoreType.DMA],
        input_output_aliases={3: 0, 4: 1},
        compiler_params=pltpu.CompilerParams(vmem_limit_bytes=VMEM_LIMIT),
        name="unpack_later_blocks",
    )(jnp.stack([core, start]).astype(jnp.int32), table, pieces, moved, theirs)


def finish_body(scalars, returned, _, moved, held, in_sem, out_sem):
    parts = in_sem.shape[0]
    rows = returned.shape[0] // parts
    spans = [pl.ds(part * rows, rows) for part in range(parts)]
    fetches = [
        pltpu.make_async_copy(returned.at[span], held.at[span], in_sem.at[part])
        for part, span in enumerate(spans)
    ]
    stores = [
        pltpu.make_async_copy(held.at[span], moved.at[span, 1 - scalars[0]], out_sem.at[part])
        for part, span in enumerate(spans)
    ]
    for fetch in fetches:
        fetch.start()
    for fetch, store in zip(fetches, stores):
        fetch.wait()
        store.start()
    for store in stores:
        store.wait()


def finish_kernel(core, returned, moved):
    return pl.pallas_call(
        finish_body,
        out_shape=jax.ShapeDtypeStruct(moved.shape, moved.dtype),
        in_specs=smem_space(1) + any_space(2),
        out_specs=any_space(1)[0],
        scratch_shapes=[
            pltpu.VMEM(returned.shape, returned.dtype),
            pltpu.SemaphoreType.DMA((4,)),
            pltpu.SemaphoreType.DMA((4,)),
        ],
        compiler_params=pltpu.CompilerParams(vmem_limit_bytes=VMEM_LIMIT),
        input_output_aliases={2: 0},
        cost_estimate=moved_cost(6 << 20),
        name="put_other_kind",
    )(core[None].astype(jnp.int32), returned, moved)


def norm_body(tokens, gain, table, out):
    rows, width = tokens.shape
    reps, _, depth = out.shape
    chunk = 1024
    total = jnp.zeros((rows, 1), jnp.float32)
    for at in range(0, width, chunk):
        part = tokens[:, at : at + chunk].astype(jnp.float32)
        total = total + jnp.sum(part * part, axis=-1, keepdims=True)
    inverse = lax.rsqrt(total * (1.0 / width) + 1e-05)
    for rep in range(reps):
        span = slice(rep * depth, (rep + 1) * depth)
        part = tokens[:, span].astype(jnp.float32) * inverse * gain[:, span].astype(jnp.float32)
        out[rep, :rows] = part.astype(jnp.bfloat16)
        out[rep, rows:] = table[...]


def norm_kernel(tokens, gain, table, reps):
    rows, width = tokens.shape
    return pl.pallas_call(
        norm_body,
        out_shape=jax.ShapeDtypeStruct((reps, rows + 16, width // reps), jnp.bfloat16),
        compiler_params=pltpu.CompilerParams(vmem_limit_bytes=VMEM_LIMIT),
        cost_estimate=moved_cost(4 << 20),
        name="norm_rows",
    )(tokens, gain, table)


def project_body(core, slabs, w_query, w_keyval, _, mine, theirs, held):
    reps, rows, depth = slabs.shape
    count = 16
    steps = (rows - count) // count
    requests = reps * count
    owners = slabs[:, rows - count :, :requests].reshape(requests, requests).astype(jnp.float32)
    number = lax.broadcasted_iota(jnp.int32, (requests, requests), 1).astype(jnp.float32)
    shuffle = jnp.where(owners == number, 1.0, 0.0).astype(jnp.bfloat16)
    query_cols = w_query.shape[1]
    for step in range(steps):
        span = slice(step * count, (step + 1) * count)
        features = slabs[:, span].reshape(requests, depth)
        features = jnp.dot(shuffle, features, preferred_element_type=jnp.float32)
        features = features.astype(jnp.bfloat16)
        for weight, at in ((w_query, 0), (w_keyval, query_cols)):
            product = jnp.dot(features, weight[...], preferred_element_type=jnp.float32)
            width = product.shape[1]
            held[:, :, at : at + width] = product.astype(jnp.bfloat16).reshape(reps, count, width)
        for one in range(2):

            @pl.when(core[0] == one)
            def _():
                for chip in range(reps // 2):
                    mine[chip, span] = held[2 * chip + one]
                    theirs[chip, span] = held[2 * chip + 1 - one]


def project_kernel(core, slabs, w_query, w_keyval, after):
    reps, rows, _ = slabs.shape
    width = w_query.shape[1] + w_keyval.shape[1]
    half = jax.ShapeDtypeStruct((reps // 2, rows - 16, width), jnp.bfloat16)
    vmem = pl.BlockSpec(memory_space=pltpu.VMEM)
    return pl.pallas_call(
        project_body,
        out_shape=[half, half],
        in_specs=smem_space(1) + [vmem] * 3 + any_space(1),
        out_specs=[vmem] * 2,
        scratch_shapes=[pltpu.VMEM((reps, 16, width), jnp.bfloat16)],
        compiler_params=pltpu.CompilerParams(vmem_limit_bytes=VMEM_LIMIT),
        cost_estimate=moved_cost(6 << 20),
        name="project_rows",
    )(core[None].astype(jnp.int32), slabs, w_query, w_keyval, after)


def attend_body(counts, sums, cache, *rest):
    out, queries, keys, values, mixed = rest[-5:]
    at = pl.program_id(0)
    together, _, span, width = cache.shape
    rows = sums.shape[1]
    per_step = 16
    steps = rows // per_step
    heads = (sums.shape[2] - 2 * width) // width

    @pl.when(at == 0)
    def _():
        for head in range(heads + 2):
            cols = slice(head * width, (head + 1) * width)
            total = jnp.sum(sums[:, :, cols].astype(jnp.float32), axis=0)
            total = total.astype(jnp.bfloat16).astype(jnp.float32)
            if head < heads:
                queries[head * rows : (head + 1) * rows] = total
            elif head == heads:
                keys[...] = total
            else:
                values[...] = total

    many = heads * steps
    flat = (((1,), (1,)), ((), ()))
    factor = 1.0 / width**0.5
    for one in range(together):
        request = at * together + one
        live = counts[request] * BLOCK
        query = queries[pl.ds(request, many, stride=per_step)].astype(jnp.bfloat16)
        key = keys[pl.ds(request, steps, stride=per_step)].astype(jnp.bfloat16)
        value = values[pl.ds(request, steps, stride=per_step)].astype(jnp.bfloat16)
        old = lax.dot_general(query, cache[one, 0], flat, preferred_element_type=jnp.float32)
        place = lax.broadcasted_iota(jnp.int32, (many, span), 1)
        old = jnp.where(place < live, old * factor, -1e30)
        new = lax.dot_general(query, key, flat, preferred_element_type=jnp.float32)
        later = lax.broadcasted_iota(jnp.int32, (many, steps), 1)
        step = lax.broadcasted_iota(jnp.int32, (many, steps), 0) % steps
        new = jnp.where(later <= step, new * factor, -1e30)
        peak = jnp.maximum(
            jnp.max(old, axis=-1, keepdims=True), jnp.max(new, axis=-1, keepdims=True)
        )
        old = jnp.exp(old - peak)
        new = jnp.exp(new - peak)
        total = jnp.sum(old, axis=-1, keepdims=True) + jnp.sum(new, axis=-1, keepdims=True)
        old = (old / total).astype(jnp.bfloat16)
        new = (new / total).astype(jnp.bfloat16)
        result = jnp.dot(old, cache[one, 1], preferred_element_type=jnp.float32)
        result = result + jnp.dot(new, value, preferred_element_type=jnp.float32)
        mixed[pl.ds(request, many, stride=per_step)] = result

    @pl.when(at == pl.num_programs(0) - 1)
    def _():
        for head in range(heads):
            cols = slice(head * width, (head + 1) * width)
            out[:, cols] = mixed[head * rows : (head + 1) * rows].astype(jnp.bfloat16)


def attend_kernel(counts, sums, cache, after):
    requests, kinds, span, width = cache.shape
    rows = sums.shape[1]
    cols = sums.shape[2] - 2 * width
    heads = cols // width
    together = 4
    return pl.pallas_call(
        attend_body,
        out_shape=jax.ShapeDtypeStruct((rows, cols), jnp.bfloat16),
        grid=(requests // together,),
        in_specs=smem_space(1)
        + [
            pl.BlockSpec(sums.shape, lambda at: (0, 0, 0)),
            pl.BlockSpec((together, kinds, span, width), lambda at: (at, 0, 0, 0)),
        ]
        + any_space(len(after)),
        out_specs=pl.BlockSpec((rows, cols), lambda at: (0, 0)),
        scratch_shapes=[
            pltpu.VMEM((heads * rows, width), jnp.float32),
            pltpu.VMEM((rows, width), jnp.float32),
            pltpu.VMEM((rows, width), jnp.float32),
            pltpu.VMEM((heads * rows, width), jnp.float32),
        ],
        compiler_params=pltpu.CompilerParams(vmem_limit_bytes=VMEM_LIMIT),
        cost_estimate=moved_cost(16 << 20),
        name="attend_old_place",
    )(counts, sums, cache, *after)


def output_body(core, slabs, near, far, weight, *rest):
    out = rest[-1]
    reps, rows, half = near.shape
    count = 16
    steps = rows // count
    requests = reps * count
    owners = slabs[:, rows:, :requests].reshape(requests, requests).astype(jnp.float32)
    number = lax.broadcasted_iota(jnp.int32, (requests, requests), 1).astype(jnp.float32)
    shuffle = jnp.where(owners == number, 1.0, 0.0).astype(jnp.bfloat16)
    first = pl.multiple_of(core[0] * half, half)
    second = pl.multiple_of((1 - core[0]) * half, half)
    for step in range(steps):
        span = slice(step * count, (step + 1) * count)
        product = jnp.dot(
            near[:, span].reshape(requests, half),
            weight[pl.ds(first, half)],
            preferred_element_type=jnp.float32,
        )
        product = product + jnp.dot(
            far[:, span].reshape(requests, half),
            weight[pl.ds(second, half)],
            preferred_element_type=jnp.float32,
        )
        product = lax.dot_general(
            shuffle,
            product.astype(jnp.bfloat16),
            (((0,), (0,)), ((), ())),
            preferred_element_type=jnp.float32,
        )
        out[:, span] = product.astype(jnp.bfloat16).reshape(reps, count, -1)


def output_kernel(core, slabs, near, far, weight, after):
    reps, rows, _ = near.shape
    vmem = pl.BlockSpec(memory_space=pltpu.VMEM)
    return pl.pallas_call(
        output_body,
        out_shape=jax.ShapeDtypeStruct((reps, rows, weight.shape[1]), jnp.bfloat16),
        in_specs=smem_space(1) + [vmem] * 4 + any_space(len(after)),
        out_specs=vmem,
        compiler_params=pltpu.CompilerParams(vmem_limit_bytes=VMEM_LIMIT),
        cost_estimate=moved_cost(6 << 20),
        name="output_rows",
    )(core[None].astype(jnp.int32), slabs, near, far, weight, *after)


def per_device(
    new_tokens, norm_gain, w_query, w_keyval, w_output, kv_cache, block_counts, new_slot
):
    reps = lax.axis_size("rep")
    tps = lax.axis_size("tp")
    rep_index = lax.axis_index("rep")
    core = rep_index % 2
    chips = reps // 2
    same_core = [[2 * chip + one for chip in range(chips)] for one in range(2)]
    other_core = [(one, one ^ 1) for one in range(reps)]
    num_steps, num_rows, feat_width = new_tokens.shape
    row_total = num_steps * num_rows
    all_rows = reps * row_total
    depth = feat_width // reps
    head_cols = w_query.shape[1]
    pair_cols = w_keyval.shape[2]
    out_cols = w_output.shape[1]

    own_table = jnp.stack([new_slot, block_counts])
    other_table = lax.ppermute(own_table, "rep", other_core)
    lent = lax.ppermute(
        lax.dynamic_index_in_dim(kv_cache, 1 - core, 1, keepdims=False), "rep", other_core
    )

    column = lax.broadcasted_iota(jnp.int32, (num_rows, depth), 1)
    table = jnp.where(column < depth // 2, new_slot[:, None], block_counts[:, None])
    slabs = norm_kernel(
        new_tokens.reshape(row_total, feat_width), norm_gain[None], table.astype(jnp.bfloat16), reps
    )
    slabs = lax.all_to_all(slabs, "rep", split_axis=0, concat_axis=0, tiled=True)
    slot_table = slabs[:, row_total:, 0].astype(jnp.int32).reshape(-1)
    length_table = slabs[:, row_total:, depth // 2].astype(jnp.int32).reshape(-1)

    my_chip = rep_index // 2
    pair_table = jnp.where(
        core == 0,
        jnp.concatenate([own_table, other_table], axis=1),
        jnp.concatenate([other_table, own_table], axis=1),
    )
    chip_rows = 2 * num_rows
    pair_slots, pair_lengths = pair_table[0], pair_table[1]
    moves, spot, fits = first_leg(
        core, jnp.broadcast_to(my_chip, (chip_rows,)), pair_slots // chip_rows, pair_lengths
    )
    order = jnp.arange(chip_rows, dtype=jnp.int32)
    at_home = jnp.where(order // num_rows == core, 1, 2)
    pack_table = jnp.stack(
        [
            jnp.where(moves, at_home, 0),
            order % num_rows,
            spot,
            jnp.clip(fits, 0, pair_lengths),
        ]
    ).astype(jnp.int32)
    sent = pack_kernel(core, pack_table, kv_cache, lent, [])
    leg_one = [
        lax.ppermute(piece, "rep", line_pairs(reps, line, 0)) for line, piece in enumerate(sent)
    ]

    every = jnp.arange(reps * num_rows, dtype=jnp.int32)
    source, target = every // chip_rows, slot_table // chip_rows
    plans = []
    for one in range(2):
        moves_one, spot_one, fits_one = first_leg(one, source, target, length_table)
        moves_two, spot_two, fits_two = second_leg(one, source, target, length_table)
        done = jnp.clip(jnp.minimum(fits_one, fits_two), 0, length_table)
        missed = length_table - done
        late_place = places(source * chips + target, missed)
        plans.append((moves_one, spot_one, moves_two, spot_two, done, missed, late_place))
    most = jnp.maximum(*[jnp.max(jnp.where(plan[5] > 0, plan[6] + plan[5], 0)) for plan in plans])
    moves_one, spot_one, moves_two, spot_two, done, missed, late_place = [
        jnp.where(core == 0, one, other) for one, other in zip(*plans)
    ]
    between = jnp.where(core == 0, target // 2 * 2 + source % 2, source // 2 * 2 + target % 2)
    home = jnp.where(every // num_rows % 2 == core, 1, 2)
    from_home = every % num_rows
    passing = jnp.where(moves_two & (between == my_chip), 1, 0)
    wanted = jnp.arange(2 * chip_rows, dtype=jnp.int32)
    across_chip = my_chip // 2 * 2 + 1 - my_chip % 2
    passing_match = jnp.where(
        core == 0,
        (slot_table[None, :] == (across_chip * chip_rows + wanted)[:, None])
        & (wanted < chip_rows)[:, None],
        every[None, :] == (my_chip // 2 * 2 * chip_rows + wanted)[:, None],
    )
    passing_table = pick(
        passing_match,
        [
            passing * jnp.where(moves_one, 3, home),
            jnp.where(moves_one, spot_one, from_home),
            spot_two,
            done,
        ],
    )
    leg_two = [
        lax.ppermute(piece, "rep", line_pairs(reps, line, 1))
        for line, piece in enumerate(pack_kernel(core, passing_table, kv_cache, lent, leg_one))
    ]

    mine, theirs = project_kernel(
        core, slabs, w_query, w_keyval.reshape(depth, 2 * pair_cols), sent[0]
    )
    theirs = lax.ppermute(theirs, "rep", other_core)
    pair_sum = (mine.astype(jnp.float32) + theirs.astype(jnp.float32)).astype(jnp.bfloat16)
    pair_sum = lax.all_to_all(
        pair_sum, "rep", split_axis=0, concat_axis=0, tiled=True, axis_index_groups=same_core
    )

    attended = attend_kernel(block_counts, pair_sum, kv_cache, leg_one)

    halves = attended.reshape(row_total, 2, head_cols // 2)
    kept = lax.dynamic_index_in_dim(halves, core, 1, keepdims=False)
    given = lax.dynamic_index_in_dim(halves, 1 - core, 1, keepdims=False)
    given = lax.ppermute(given, "rep", other_core)
    kept = jnp.where(core == 0, jnp.stack([kept, given]), jnp.stack([given, kept]))
    near = lax.all_to_all(
        jnp.broadcast_to(kept[None], (chips,) + kept.shape),
        "rep",
        split_axis=0,
        concat_axis=0,
        tiled=True,
        axis_index_groups=same_core,
    ).reshape(reps, row_total, head_cols // 2)
    near, *_ = lax.optimization_barrier((near, *leg_two))
    far = lax.ppermute(near, "rep", other_core)

    partial_out = output_kernel(core, slabs, near, far, w_output, [])
    exchanged = lax.all_to_all(
        partial_out.reshape(tps, all_rows // tps, out_cols),
        "tp",
        split_axis=0,
        concat_axis=0,
        tiled=True,
    )
    first, exchanged = lax.optimization_barrier((jnp.int32(0), exchanged))
    summed = jnp.sum(exchanged.astype(jnp.float32), axis=0).astype(jnp.bfloat16)
    summed = summed.reshape(2, row_total, out_cols)
    straight = [
        (r * tps + t, (2 * t + r % 2) * tps + r // 2) for r in range(reps) for t in range(tps)
    ]
    crossed = [
        (r * tps + t, (2 * t + 1 - r % 2) * tps + r // 2) for r in range(reps) for t in range(tps)
    ]
    left = lax.ppermute(
        lax.dynamic_index_in_dim(summed, core, 0, keepdims=False), ("rep", "tp"), straight
    )
    right = lax.ppermute(
        lax.dynamic_index_in_dim(summed, 1 - core, 0, keepdims=False), ("rep", "tp"), crossed
    )
    layer_out = jnp.where(
        core == 0,
        jnp.concatenate([left, right], axis=1),
        jnp.concatenate([right, left], axis=1),
    ).reshape(num_steps, num_rows, 2 * out_cols)

    arrive_match = slot_table[None, :] == (my_chip * chip_rows + order)[:, None]
    unpack_table = pick(
        arrive_match,
        [
            jnp.where(moves_two, 4, jnp.where(moves_one, 3, home)),
            jnp.where(moves_two, spot_two, jnp.where(moves_one, spot_one, from_home)),
            done,
        ],
    )
    cache_moved, held = unpack_kernel(
        core, unpack_table, kv_cache, lent, leg_one, leg_two, partial_out
    )

    late_fields = [late_place, done, missed]
    late_pack = pick(
        every[None, :] == (my_chip * chip_rows + order)[:, None], [target] + late_fields
    )
    late_unpack = pick(arrive_match, [source] + late_fields)

    def more(state):
        start, moved, other = state
        pieces = lax.all_to_all(
            pack_more_kernel(core, start, late_pack, kv_cache, lent, chips),
            "rep",
            split_axis=0,
            concat_axis=0,
            tiled=True,
            axis_index_groups=same_core,
        )
        moved, other = unpack_more_kernel(core, start, late_unpack, pieces, moved, other)
        return start + LATER, moved, other

    _, cache_moved, held = lax.while_loop(
        lambda state: state[0] < most, more, (first, cache_moved, held)
    )
    returned = lax.ppermute(held, "rep", other_core)
    cache_moved = finish_kernel(core, returned, cache_moved)
    return (layer_out, cache_moved)


def solution(mesh):
    placed = (
        P(None, "rep", None),
        P(),
        P("rep", "tp"),
        P("rep", None, "tp"),
        P("tp", "rep"),
        P("rep", None, None, "tp"),
        P("rep"),
        P("rep"),
    )
    return jax.shard_map(
        per_device,
        mesh=mesh,
        in_specs=placed,
        out_specs=(P(None, "rep", "tp"), P("rep", None, None, "tp")),
        check_vma=False,
    )
```

time: 373 us -> 197 us (0.53)
  the two profiles are of different devices: /device:TPU:5 before, /device:TPU:17 now
where the time goes in v4:
time: 197 us; the launch traced here: 195 us
  waiting for transfers between devices  71 us (36%)
  Pallas kernels  45.2 us (23%)
  starting transfers between devices  44.4 us (23%)
  other arithmetic  17 us (9%)
  local copies, waits for them, and re-layouts  15.5 us (8%)
  between operations  2.34 us (1%)
    ppermute x3, waiting for transfers between devices, per_device(): lax.ppermute(piece, 'rep', line_pairs(reps, line, 0))  22.4 us
    all_to_all x1, waiting for transfers between devices, per_device(): lax.all_to_all(slabs, 'rep', split_axis=0, concat_axis=0, tiled=True)  17.3 us
    pallas_call x2, Pallas kernels, pack_kernel(): pl.pallas_call(pack_body, out_shape=[line] * 3, in_specs=smem_space(2) +...  10.9 us
    all_to_all x1, waiting for transfers between devices, per_device(): lax.all_to_all(jnp.broadcast_to(kept[None], (chips,) + kept.shape), 'rep'...  10.9 us
    pallas_call x1, Pallas kernels, attend_kernel(): pl.pallas_call(attend_body, out_shape=jax.ShapeDtypeStruct((rows, cols),...  9.83 us
    ppermute x1, waiting for transfers between devices, per_device(): lax.ppermute(lax.dynamic_index_in_dim(summed, 1 - core, 0, keepdims=False...  8.49 us
    pallas_call x1, Pallas kernels, unpack_kernel(): pl.pallas_call(unpack_body, out_shape=[jax.ShapeDtypeStruct(cache.shape,...  7.38 us
    all_to_all x1, starting transfers between devices, per_device(): lax.all_to_all(slabs, 'rep', split_axis=0, concat_axis=0, tiled=True)  7.33 us
  transfers between devices with their start and end apart: 18, of which 8 were waited for; matrix products, arithmetic and copies ran while one was open for 14% of the time, Pallas kernels for 13%

profile of v4, /device:TPU:17, one launch (start us, length us, event | category | flops | bytes accessed | tf_op | source)
XLA Modules:
  0.0 195.5 jit_solution(11182928105974378355)
XLA Ops:
  0.7 3.9 %dynamic-slice_bitcast_fusion = bf16[16,768,128]{2,1,0:T(8,128)(2,1)} fusion(bf16[16,2,768,128]{3,2,1,0:T(8,128)(2,1)} %cache.7, s32[]{:T(128)S(6)} %select_n.1293), kind=kLoop, calls=%fused_computation.1 | loop fusion | bytes 6291460 | tf_op jit(solution)/shard_map/jit(dynamic_index_in_dim)/squeeze | solution.py:567
  7.5 2.8 %norm_rows.1 = bf16[16,80,512]{2,1,0:T(8,128)(2,1)} custom-call(bf16[64,8192]{1,0:T(8,128)(2,1)} %bitcast.69, bf16[1,8192]{1,0:T(2,128)(2,1)} %broadcast_in_dim.309.gain, bf16[16,512]{1,0:T(8,128)(2,1)} %select_convert_fusion.table), custom_call_target="tpu_custom_call" | custom-call | bytes 4194304 | tf_op jit(solution)/shard_map/norm_rows/pallas_call | solution.py:361
  10.5 7.3 %all-to-all-start.1 = ((bf16[16,80,512]{2,1,0:T(8,128)(2,1)}), bf16[16,80,512]{2,1,0:T(8,128)(2,1)}, u32[]{:S(2)}, u32[]{:S(2)}) async-start(bf16[16,80,512]{2,1,0:T(8,128)(2,1)} %norm_rows.1), calls=%async_computation.1 | async-start | bytes 2621440 | tf_op jit(solution)/shard_map/all_to_all | solution.py:575
  18.9 17.3 %all-to-all-done.1.slabs = bf16[16,80,512]{2,1,0:T(8,128)(2,1)} async-done(((bf16[16,80,512]{2,1,0:T(8,128)(2,1)}), bf16[16,80,512]{2,1,0:T(8,128)(2,1)}, u32[]{:S(2)}, u32[]{:S(2)}) %all-to-all-start.1) | async-done | bytes 1310752 | tf_op jit(solution)/shard_map/all_to_all | solution.py:575
  37.8 5.0 %pack_blocks.2 = (bf16[38,128,128]{2,1,0:T(8,128)(2,1)}, bf16[38,128,128]{2,1,0:T(8,128)(2,1)}, bf16[38,128,128]{2,1,0:T(8,128)(2,1)}) custom-call(s32[1]{0:T(128)} %bitcast.2.core.scalars, s32[4,32]{1,0:T(4,128)} %pad_add_fusion.9.table, bf16[16,2,768,128]{3,2,1,0:T(8,128)(2,1)} %cache.7, bf16[16,768,128]{2,1,0:T(8,128)(2,1)S(1)} %collective-permute-done.1.lent), custom_call_target="tpu_custom_call" | custom-call | bytes 8388608 | tf_op jit(solution)/shard_map/pack_blocks/pallas_call | solution.py:143
  42.8 6.1 %project_rows.1 = (bf16[8,64,1280]{2,1,0:T(8,128)(2,1)}, bf16[8,64,1280]{2,1,0:T(8,128)(2,1)}) custom-call(s32[1]{0:T(128)} %bitcast.2.core.scalars, bf16[16,80,512]{2,1,0:T(8,128)(2,1)} %all-to-all-done.1.slabs, bf16[512,1024]{1,0:T(8,128)(2,1)} %w_query.1, bf16[512,256]{1,0:T(8,128)(2,1)} %bitcast.70, bf16[38,128,128]{2,1,0:T(8,128)(2,1)} %get-tuple-element.66._), custom_call_target="tpu_custom_call" | custom-call | bytes 6291456 | tf_op jit(solution)/shard_map/project_rows/pallas_call | solution.py:402
  50.5 2.4 %collective-permute-start.3 = (bf16[38,128,128]{2,1,0:T(8,128)(2,1)}, bf16[38,128,128]{2,1,0:T(8,128)(2,1)}, u32[]{:S(2)}, u32[]{:S(2)}) collective-permute-start(bf16[38,128,128]{2,1,0:T(8,128)(2,1)} %get-tuple-element.66._), channel_id=1, source_target_pairs={{0,32},{8,24},{16,48},{24,8},{32,64},{40,56},{48,80},{56,40},{64,9... | collective-permute-start | bytes 3735560 | tf_op jit(solution)/shard_map/ppermute | solution.py:602
  53.6 1.7 collective-permute-start.5
  55.3 3.1 %add_convert_fusion = bf16[8,64,1280]{2,1,0:T(8,128)(2,1)} fusion(bf16[8,64,1280]{2,1,0:T(8,128)(2,1)} %collective-permute-done.2, bf16[8,64,1280]{2,1,0:T(8,128)(2,1)} %get-tuple-element.67), kind=kLoop, calls=%fused_computation.2 | loop fusion | flops 2621440 | bytes 3932160 | tf_op jit(solution)/shard_map/convert_element_type | solution.py:649
  58.3 6.4 %all-to-all-start.2 = ((bf16[8,64,1280]{2,1,0:T(8,128)(2,1)}), bf16[8,64,1280]{2,1,0:T(8,128)(2,1)}, u32[]{:S(2)}, u32[]{:S(2)}) async-start(bf16[8,64,1280]{2,1,0:T(8,128)(2,1)} %add_convert_fusion), calls=%async_computation.2 | async-start | bytes 2621440 | tf_op jit(solution)/shard_map/all_to_all | solution.py:650
  66.8 22.4 %collective-permute-done.4.rest_1_ = bf16[38,128,128]{2,1,0:T(8,128)(2,1)} collective-permute-done((bf16[38,128,128]{2,1,0:T(8,128)(2,1)}, bf16[38,128,128]{2,1,0:T(8,128)(2,1)}, u32[]{:S(2)}, u32[]{:S(2)}) %collective-permute-start.4) | collective-permute-done | bytes 1245216 | tf_op jit(solution)/shard_map/ppermute | solution.py:602
  89.1 5.9 %pack_blocks.3 = (bf16[38,128,128]{2,1,0:T(8,128)(2,1)}, bf16[38,128,128]{2,1,0:T(8,128)(2,1)}, bf16[38,128,128]{2,1,0:T(8,128)(2,1)}) custom-call(s32[1]{0:T(128)} %bitcast.2.core.scalars, s32[4,64]{1,0:T(4,128)} %select_reduce_fusion.2.table, bf16[16,2,768,128]{3,2,1,0:T(8,128)(2,1)} %cache.7, bf16[16,768,128]{2,1,0:T(8,128)(2,1)S(1)} %collective-permute-done.1.lent, ...), custom_call_target="tpu_custom_call" | custom-call | bytes 8388608 | tf_op jit(solution)/shard_map/pack_blocks/pallas_call | solution.py:143
  95.7 2.1 %collective-permute-start.8 = (bf16[38,128,128]{2,1,0:T(8,128)(2,1)}, bf16[38,128,128]{2,1,0:T(8,128)(2,1)}, u32[]{:S(2)}, u32[]{:S(2)}) collective-permute-start(bf16[38,128,128]{2,1,0:T(8,128)(2,1)} %get-tuple-element.72), channel_id=1, source_target_pairs={{0,16},{8,104},{16,0},{24,120},{32,48},{40,8},{48,32},{56,24},{64,... | collective-permute-start | bytes 3735560 | tf_op jit(solution)/shard_map/ppermute | solution.py:641
  97.8 3.7 %collective-permute-start.9 = (bf16[38,128,128]{2,1,0:T(8,128)(2,1)}, bf16[38,128,128]{2,1,0:T(8,128)(2,1)}, u32[]{:S(2)}, u32[]{:S(2)}) collective-permute-start(bf16[38,128,128]{2,1,0:T(8,128)(2,1)} %get-tuple-element.73), channel_id=1, source_target_pairs={{8,72},{24,88},{40,104},{56,120},{72,8},{88,24},{104,40},{120,56},... | collective-permute-start | bytes 3735560 | tf_op jit(solution)/shard_map/ppermute | solution.py:641
  101.6 9.8 %attend_old_place.1 = bf16[64,1024]{1,0:T(8,128)(2,1)} custom-call(s32[16]{0:T(128)} %counts.1, bf16[8,64,1280]{2,1,0:T(8,128)(2,1)} %all-to-all-done.2.sums, bf16[16,2,768,128]{3,2,1,0:T(8,128)(2,1)} %cache.7, bf16[38,128,128]{2,1,0:T(8,128)(2,1)} %collective-permute-done.3.rest_0_, bf16[38,128,128]{2,1,0:T(8,128)(2,1)} %collective-permute-done.4.rest_1_, ...), custom_call_target="tpu_custom_call" | custom-call | bytes 16777216 | tf_op jit(solution)/shard_map/attend_old_place/pallas_call | solution.py:477
  115.1 6.5 %all-to-all-start.3 = ((bf16[8,2,64,512]{3,2,1,0:T(8,128)(2,1)}), bf16[8,2,64,512]{3,2,1,0:T(8,128)(2,1)}, u32[]{:S(2)}, u32[]{:S(2)}) async-start(bf16[8,2,64,512]{3,2,1,0:T(8,128)(2,1)} %broadcast_in_dim.319), calls=%async_computation.3 | async-start | bytes 2097152 | tf_op jit(solution)/shard_map/all_to_all | solution.py:661
  121.6 4.7 %collective-permute-done.9.rest_5_ = bf16[38,128,128]{2,1,0:T(8,128)(2,1)} collective-permute-done((bf16[38,128,128]{2,1,0:T(8,128)(2,1)}, bf16[38,128,128]{2,1,0:T(8,128)(2,1)}, u32[]{:S(2)}, u32[]{:S(2)}) %collective-permute-start.9) | collective-permute-done | bytes 1245216 | tf_op jit(solution)/shard_map/ppermute | solution.py:641
  126.3 10.9 %all-to-all-done.3 = bf16[8,2,64,512]{3,2,1,0:T(8,128)(2,1)} async-done(((bf16[8,2,64,512]{3,2,1,0:T(8,128)(2,1)}), bf16[8,2,64,512]{3,2,1,0:T(8,128)(2,1)}, u32[]{:S(2)}, u32[]{:S(2)}) %all-to-all-start.3) | async-done | bytes 1048608 | tf_op jit(solution)/shard_map/all_to_all | solution.py:661
  137.1 1.7 collective-permute-start.10
  140.6 1.5 sub.415
  143.7 1.5 sub.413
  145.2 5.3 %output_rows.1.rest_6_ = bf16[16,64,512]{2,1,0:T(8,128)(2,1)} custom-call(s32[1]{0:T(128)} %bitcast.2.core.scalars, bf16[16,80,512]{2,1,0:T(8,128)(2,1)} %all-to-all-done.1.slabs, bf16[16,64,512]{2,1,0:T(8,128)(2,1)} %bitcast.17.near, bf16[16,64,512]{2,1,0:T(8,128)(2,1)} %collective-permute-done.10.far, bf16[1024,512]{1,0:T(8,128)(2,1)} %weight.1), custom_call_target="tpu_custom_call" | custom-call | bytes 6291456 | tf_op jit(solution)/shard_map/output_rows/pallas_call | solution.py:535
  150.6 5.8 %all-to-all-start.4 = ((bf16[8,128,512]{2,1,0:T(8,128)(2,1)}), bf16[8,128,512]{2,1,0:T(8,128)(2,1)}, u32[]{:S(2)}, u32[]{:S(2)}) async-start(bf16[8,128,512]{2,1,0:T(8,128)(2,1)} %bitcast.68), calls=%async_computation.4 | async-start | bytes 2097152 | tf_op jit(solution)/shard_map/all_to_all | solution.py:673
  156.3 2.2 %select_reduce_fusion.9 = (s32[]{:T(128)}, s32[]{:T(128)}) fusion(s32[16,16,1]{2,1,0:T(8,128)S(1)} %reduce_sum.174, s32[16,16,1]{2,1,0:T(8,128)} %sub.415, s32[16,16,1]{2,1,0:T(8,128)S(1)} %sub.414, bf16[16,80,512]{2,1,0:T(8,128)(2,1)} %all-to-all-done.1.slabs, s32[16,16,1]{2,1,0:T(8,128)S(1)} %reduce_sum.173, s32[16,16,1]{2,1,0:T(8,128)} %sub.413, ...), kind=kLoop, calls=%fused_computation.68 | loop fusion | flops 27134 | bytes 7176 | tf_op jit(solution)/shard_map/reduce_max | solution.py:615
  162.1 7.4 %unpack_blocks.1 = (bf16[16,2,768,128]{3,2,1,0:T(8,128)(2,1)}, bf16[16,768,128]{2,1,0:T(8,128)(2,1)}) custom-call(s32[1]{0:T(128)} %bitcast.2.core.scalars, s32[3,32]{1,0:T(4,128)} %select_reduce_fusion.11.table, bf16[16,2,768,128]{3,2,1,0:T(8,128)(2,1)} %cache.7, bf16[16,768,128]{2,1,0:T(8,128)(2,1)S(1)} %collective-permute-done.1.lent, ...), custom_call_target="tpu_custom_call" | custom-call | bytes 10485760 | tf_op jit(solution)/shard_map/unpack_blocks/pallas_call | solution.py:193
  169.5 2.5 %all-to-all-done.4 = bf16[8,128,512]{2,1,0:T(8,128)(2,1)} async-done(((bf16[8,128,512]{2,1,0:T(8,128)(2,1)}), bf16[8,128,512]{2,1,0:T(8,128)(2,1)}, u32[]{:S(2)}, u32[]{:S(2)}) %all-to-all-start.4) | async-done | bytes 1048608 | tf_op jit(solution)/shard_map/all_to_all | solution.py:673
  174.6 1.9 collective-permute-start.11
  176.5 1.7 collective-permute-start.12
  178.2 3.4 %collective-permute-done.11 = bf16[64,512]{1,0:T(8,128)(2,1)S(1)} collective-permute-done((bf16[64,512]{1,0:T(8,128)(2,1)S(1)}, bf16[64,512]{1,0:T(8,128)(2,1)S(1)}, u32[]{:S(2)}, u32[]{:S(2)}) %collective-permute-start.11) | collective-permute-done | bytes 65568 | tf_op jit(solution)/shard_map/ppermute | solution.py:689
  181.6 8.5 %collective-permute-done.12 = bf16[64,512]{1,0:T(8,128)(2,1)S(1)} collective-permute-done((bf16[64,512]{1,0:T(8,128)(2,1)S(1)}, bf16[64,512]{1,0:T(8,128)(2,1)S(1)}, u32[]{:S(2)}, u32[]{:S(2)}) %collective-permute-start.12) | collective-permute-done | bytes 65568 | tf_op jit(solution)/shard_map/ppermute | solution.py:692
  190.8 1.7 copy-done
  192.4 2.9 %put_other_kind.1 = bf16[16,2,768,128]{3,2,1,0:T(8,128)(2,1)} custom-call(s32[1]{0:T(128)} %bitcast.2.core.scalars, bf16[16,768,128]{2,1,0:T(8,128)(2,1)} %copy-done, bf16[16,2,768,128]{3,2,1,0:T(8,128)(2,1)} %get-tuple-element.80._), custom_call_target="tpu_custom_call", output_to_operand_aliasing={{}: (2, {})} | custom-call | bytes 6291456 | tf_op jit(solution)/shard_map/put_other_kind/pallas_call | solution.py:326
  (84 shorter events, 23.1 us)
Async XLA Ops:
  0.6 4.6 %copy-start.3 = (s32[16]{0:T(128)S(1)}, s32[16]{0:T(128)}, u32[]{:S(2)}) copy-start(s32[16]{0:T(128)} %counts.1) | copy-start | bytes 196
  0.7 4.6 %copy-start.4 = (s32[16]{0:T(128)S(1)}, s32[16]{0:T(128)}, u32[]{:S(2)}) copy-start(s32[16]{0:T(128)} %param.17) | copy-start | bytes 196
  0.7 4.8 %copy-start.2 = (bf16[8192]{0:T(1024)(128)(2,1)S(1)}, bf16[8192]{0:T(1024)(128)(2,1)}, u32[]{:S(2)}) copy-start(bf16[8192]{0:T(1024)(128)(2,1)} %param.11) | copy-start | bytes 49156
  0.7 5.4 %copy-start.1 = (bf16[512,2,128]{2,1,0:T(2,128)(2,1)S(1)}, bf16[512,2,128]{2,1,0:T(2,128)(2,1)}, u32[]{:S(2)}) copy-start(bf16[512,2,128]{2,1,0:T(2,128)(2,1)} %param.13) | copy-start | bytes 786436
  4.6 33.2 %collective-permute-start.1 = (bf16[16,768,128]{2,1,0:T(8,128)(2,1)}, bf16[16,768,128]{2,1,0:T(8,128)(2,1)S(1)}, u32[]{:S(2)}, u32[]{:S(2)}) collective-permute-start(bf16[16,768,128]{2,1,0:T(8,128)(2,1)} %dynamic-slice_bitcast_fusion), channel_id=1, source_target_pairs={{0,8},{8,0},{16,24},{24,16},{32,40},{40,32},{48,56},{56,48},{64,72... | collective-permute-start | bytes 9437192 | tf_op jit(solution)/shard_map/ppermute | solution.py:566
  5.3 5.1 %collective-permute-start = (s32[2,16]{1,0:T(2,128)S(1)}, s32[2,16]{1,0:T(2,128)S(1)}, u32[]{:S(2)}, u32[]{:S(2)}) collective-permute-start(s32[2,16]{1,0:T(2,128)S(1)} %pad_add_fusion.10), channel_id=1, source_target_pairs={{0,8},{8,0},{16,24},{24,16},{32,40},{40,32},{48,56},{56,48},{64,72... | collective-permute-start | bytes 392 | tf_op jit(solution)/shard_map/ppermute | solution.py:565
  10.5 25.7 %all-to-all-start.1 = ((bf16[16,80,512]{2,1,0:T(8,128)(2,1)}), bf16[16,80,512]{2,1,0:T(8,128)(2,1)}, u32[]{:S(2)}, u32[]{:S(2)}) async-start(bf16[16,80,512]{2,1,0:T(8,128)(2,1)} %norm_rows.1), calls=%async_computation.1 | async-start | bytes 2621440 | tf_op jit(solution)/shard_map/all_to_all | solution.py:575
  48.8 6.4 %collective-permute-start.2 = (bf16[8,64,1280]{2,1,0:T(8,128)(2,1)}, bf16[8,64,1280]{2,1,0:T(8,128)(2,1)}, u32[]{:S(2)}, u32[]{:S(2)}) collective-permute-start(bf16[8,64,1280]{2,1,0:T(8,128)(2,1)} %get-tuple-element.68), channel_id=1, source_target_pairs={{0,8},{8,0},{16,24},{24,16},{32,40},{40,32},{48,56},{56,48},{64,72... | collective-permute-start | bytes 3932168 | tf_op jit(solution)/shard_map/ppermute | solution.py:648
  50.5 38.6 %collective-permute-start.3 = (bf16[38,128,128]{2,1,0:T(8,128)(2,1)}, bf16[38,128,128]{2,1,0:T(8,128)(2,1)}, u32[]{:S(2)}, u32[]{:S(2)}) collective-permute-start(bf16[38,128,128]{2,1,0:T(8,128)(2,1)} %get-tuple-element.66._), channel_id=1, source_target_pairs={{0,32},{8,24},{16,48},{24,8},{32,64},{40,56},{48,80},{56,40},{64,9... | collective-permute-start | bytes 3735560 | tf_op jit(solution)/shard_map/ppermute | solution.py:602
  52.9 36.3 %collective-permute-start.4 = (bf16[38,128,128]{2,1,0:T(8,128)(2,1)}, bf16[38,128,128]{2,1,0:T(8,128)(2,1)}, u32[]{:S(2)}, u32[]{:S(2)}) collective-permute-start(bf16[38,128,128]{2,1,0:T(8,128)(2,1)} %get-tuple-element.69), channel_id=1, source_target_pairs={{0,96},{8,24},{16,112},{24,8},{32,0},{40,56},{48,16},{56,40},{64,3... | collective-permute-start | bytes 3735560 | tf_op jit(solution)/shard_map/ppermute | solution.py:602
  53.6 35.6 %collective-permute-start.5 = (bf16[38,128,128]{2,1,0:T(8,128)(2,1)}, bf16[38,128,128]{2,1,0:T(8,128)(2,1)}, u32[]{:S(2)}, u32[]{:S(2)}) collective-permute-start(bf16[38,128,128]{2,1,0:T(8,128)(2,1)} %get-tuple-element.70), channel_id=1, source_target_pairs={{0,64},{16,80},{32,96},{48,112},{64,0},{80,16},{96,32},{112,48},{1... | collective-permute-start | bytes 3735560 | tf_op jit(solution)/shard_map/ppermute | solution.py:602
  58.3 43.2 %all-to-all-start.2 = ((bf16[8,64,1280]{2,1,0:T(8,128)(2,1)}), bf16[8,64,1280]{2,1,0:T(8,128)(2,1)}, u32[]{:S(2)}, u32[]{:S(2)}) async-start(bf16[8,64,1280]{2,1,0:T(8,128)(2,1)} %add_convert_fusion), calls=%async_computation.2 | async-start | bytes 2621440 | tf_op jit(solution)/shard_map/all_to_all | solution.py:650
  95.1 26.5 %collective-permute-start.7 = (bf16[38,128,128]{2,1,0:T(8,128)(2,1)}, bf16[38,128,128]{2,1,0:T(8,128)(2,1)}, u32[]{:S(2)}, u32[]{:S(2)}) collective-permute-start(bf16[38,128,128]{2,1,0:T(8,128)(2,1)} %get-tuple-element.71), channel_id=1, source_target_pairs={{0,16},{8,40},{16,0},{24,56},{32,48},{40,72},{48,32},{56,88},{64,8... | collective-permute-start | bytes 3735560 | tf_op jit(solution)/shard_map/ppermute | solution.py:641
  95.7 25.9 %collective-permute-start.8 = (bf16[38,128,128]{2,1,0:T(8,128)(2,1)}, bf16[38,128,128]{2,1,0:T(8,128)(2,1)}, u32[]{:S(2)}, u32[]{:S(2)}) collective-permute-start(bf16[38,128,128]{2,1,0:T(8,128)(2,1)} %get-tuple-element.72), channel_id=1, source_target_pairs={{0,16},{8,104},{16,0},{24,120},{32,48},{40,8},{48,32},{56,24},{64,... | collective-permute-start | bytes 3735560 | tf_op jit(solution)/shard_map/ppermute | solution.py:641
  97.8 28.4 %collective-permute-start.9 = (bf16[38,128,128]{2,1,0:T(8,128)(2,1)}, bf16[38,128,128]{2,1,0:T(8,128)(2,1)}, u32[]{:S(2)}, u32[]{:S(2)}) collective-permute-start(bf16[38,128,128]{2,1,0:T(8,128)(2,1)} %get-tuple-element.73), channel_id=1, source_target_pairs={{8,72},{24,88},{40,104},{56,120},{72,8},{88,24},{104,40},{120,56},... | collective-permute-start | bytes 3735560 | tf_op jit(solution)/shard_map/ppermute | solution.py:641
  112.7 1.3 collective-permute-start.6
  115.1 22.0 %all-to-all-start.3 = ((bf16[8,2,64,512]{3,2,1,0:T(8,128)(2,1)}), bf16[8,2,64,512]{3,2,1,0:T(8,128)(2,1)}, u32[]{:S(2)}, u32[]{:S(2)}) async-start(bf16[8,2,64,512]{3,2,1,0:T(8,128)(2,1)} %broadcast_in_dim.319), calls=%async_computation.3 | async-start | bytes 2097152 | tf_op jit(solution)/shard_map/all_to_all | solution.py:661
  137.1 8.1 %collective-permute-start.10 = (bf16[16,64,512]{2,1,0:T(8,128)(2,1)}, bf16[16,64,512]{2,1,0:T(8,128)(2,1)}, u32[]{:S(2)}, u32[]{:S(2)}) collective-permute-start(bf16[16,64,512]{2,1,0:T(8,128)(2,1)} %bitcast.17.near), channel_id=1, source_target_pairs={{0,8},{8,0},{16,24},{24,16},{32,40},{40,32},{48,56},{56,48},{64,72... | collective-permute-start | bytes 3145736 | tf_op jit(solution)/shard_map/ppermute | solution.py:670
  150.6 21.5 %all-to-all-start.4 = ((bf16[8,128,512]{2,1,0:T(8,128)(2,1)}), bf16[8,128,512]{2,1,0:T(8,128)(2,1)}, u32[]{:S(2)}, u32[]{:S(2)}) async-start(bf16[8,128,512]{2,1,0:T(8,128)(2,1)} %bitcast.68), calls=%async_computation.4 | async-start | bytes 2097152 | tf_op jit(solution)/shard_map/all_to_all | solution.py:673
  172.1 18.7 %collective-permute-start.13 = (bf16[16,768,128]{2,1,0:T(8,128)(2,1)}, bf16[16,768,128]{2,1,0:T(8,128)(2,1)S(1)}, u32[]{:S(2)}, u32[]{:S(2)}) collective-permute-start(bf16[16,768,128]{2,1,0:T(8,128)(2,1)} %get-tuple-element.79), channel_id=1, source_target_pairs={{0,8},{8,0},{16,24},{24,16},{32,40},{40,32},{48,56},{56,48},{64,72... | collective-permute-start | bytes 9437192 | tf_op jit(solution)/shard_map/ppermute | solution.py:736
  174.6 7.1 %collective-permute-start.11 = (bf16[64,512]{1,0:T(8,128)(2,1)S(1)}, bf16[64,512]{1,0:T(8,128)(2,1)S(1)}, u32[]{:S(2)}, u32[]{:S(2)}) collective-permute-start(bf16[64,512]{1,0:T(8,128)(2,1)S(1)} %get-tuple-element.137), channel_id=1, source_target_pairs={{0,0},{1,16},{2,32},{3,48},{4,64},{5,80},{6,96},{7,112},{8,8},{9,2... | collective-permute-start | bytes 196616 | tf_op jit(solution)/shard_map/ppermute | solution.py:689
  176.5 13.6 %collective-permute-start.12 = (bf16[64,512]{1,0:T(8,128)(2,1)S(1)}, bf16[64,512]{1,0:T(8,128)(2,1)S(1)}, u32[]{:S(2)}, u32[]{:S(2)}) collective-permute-start(bf16[64,512]{1,0:T(8,128)(2,1)S(1)} %get-tuple-element.138), channel_id=1, source_target_pairs={{0,8},{1,24},{2,40},{3,56},{4,72},{5,88},{6,104},{7,120},{8,0},{9,... | collective-permute-start | bytes 196616 | tf_op jit(solution)/shard_map/ppermute | solution.py:692
  190.8 1.7 copy-start

commit v5 on v4

--- a/solution.py
+++ b/solution.py
@@ -1,3 +1,5 @@
+import functools
+
 import jax
 import jax.numpy as jnp
 from jax import lax
@@ -10,6 +12,7 @@
 ROOM = 38
 LATER = 4
 VMEM_LIMIT = 56 << 20
+VMEM_COMPUTE = 24 << 20
 
 
 def line_pairs(reps, line, along_first):
@@ -79,7 +82,7 @@
                 pltpu.make_async_copy(source(block), put(block), sem).start()
 
     fetch(place == 1, lambda block: blocks_of(cache, at, block, core))
-    fetch(place == 2, lambda block: blocks_of(lent, at, block))
+    fetch(place == 2, lambda block: blocks_of(lent, at, block, core))
     for number, lines in enumerate(legs, 3):
 
         @pl.when(place == number)
@@ -104,8 +107,8 @@
         pltpu.make_async_copy(example, example, sem).wait()
 
 
-def pack_body(core, table, cache, lent, *rest):
-    lines, (out, held, sem, out_sem) = rest[:-6], (rest[-6:-3],) + rest[-3:]
+def pack_body(legs, core, table, cache, lent, *rest):
+    lines, (out, held, sem, out_sem) = rest[:legs], (rest[-6:-3],) + rest[-3:]
 
     def send(at, total):
         to = table[2, at]
@@ -138,10 +141,10 @@
     return pl.CostEstimate(flops=0, bytes_accessed=size, transcendentals=0)
 
 
-def pack_kernel(core, table, cache, lent, lines):
+def pack_kernel(core, table, cache, lent, lines, cost):
     line = jax.ShapeDtypeStruct((ROOM, BLOCK, HEADDIM), jnp.bfloat16)
     return pl.pallas_call(
-        pack_body,
+        functools.partial(pack_body, len(lines)),
         out_shape=[line] * 3,
         in_specs=smem_space(2) + any_space(2 + len(lines)),
         out_specs=any_space(3),
@@ -151,7 +154,7 @@
             pltpu.SemaphoreType.DMA((3,)),
         ],
         compiler_params=pltpu.CompilerParams(vmem_limit_bytes=VMEM_LIMIT),
-        cost_estimate=moved_cost(8 << 20),
+        cost_estimate=moved_cost(cost),
         name="pack_blocks",
     )(core[None].astype(jnp.int32), table, cache, lent, *lines)
 
@@ -231,7 +234,7 @@
 
         row = at % half
         fetch(at // half == core, lambda block: blocks_of(cache, row, block, core))
-        fetch(at // half != core, lambda block: blocks_of(lent, row, block))
+        fetch(at // half != core, lambda block: blocks_of(lent, row, block, core))
         return total + count
 
     total = lax.fori_loop(0, requests, send, jnp.int32(0))
@@ -340,7 +343,7 @@
     )(core[None].astype(jnp.int32), returned, moved)
 
 
-def norm_body(tokens, gain, table, out):
+def norm_body(slots, counts, tokens, gain, out):
     rows, width = tokens.shape
     reps, _, depth = out.shape
     chunk = 1024
@@ -349,31 +352,47 @@
         part = tokens[:, at : at + chunk].astype(jnp.float32)
         total = total + jnp.sum(part * part, axis=-1, keepdims=True)
     inverse = lax.rsqrt(total * (1.0 / width) + 1e-05)
+    shape = (slots.shape[0], depth)
+    row = lax.broadcasted_iota(jnp.int32, shape, 0)
+    left = lax.broadcasted_iota(jnp.int32, shape, 1) < depth // 2
+    table = jnp.zeros(shape, jnp.int32)
+    for one in range(slots.shape[0]):
+        table = jnp.where(row == one, jnp.where(left, slots[one], counts[one]), table)
+    table = table.astype(jnp.float32).astype(jnp.bfloat16)
     for rep in range(reps):
         span = slice(rep * depth, (rep + 1) * depth)
-        part = tokens[:, span].astype(jnp.float32) * inverse * gain[:, span].astype(jnp.float32)
+        scale = gain[span].astype(jnp.float32).reshape(1, depth)
+        part = tokens[:, span].astype(jnp.float32) * inverse * scale
         out[rep, :rows] = part.astype(jnp.bfloat16)
-        out[rep, rows:] = table[...]
-
-
-def norm_kernel(tokens, gain, table, reps):
+        out[rep, rows:] = table
+
+
+def norm_kernel(slots, counts, tokens, gain, reps):
     rows, width = tokens.shape
+    vmem = pl.BlockSpec(memory_space=pltpu.VMEM)
     return pl.pallas_call(
         norm_body,
         out_shape=jax.ShapeDtypeStruct((reps, rows + 16, width // reps), jnp.bfloat16),
-        compiler_params=pltpu.CompilerParams(vmem_limit_bytes=VMEM_LIMIT),
+        in_specs=smem_space(2) + [vmem] * 2,
+        out_specs=vmem,
+        compiler_params=pltpu.CompilerParams(vmem_limit_bytes=VMEM_COMPUTE),
         cost_estimate=moved_cost(4 << 20),
         name="norm_rows",
-    )(tokens, gain, table)
-
-
-def project_body(core, slabs, w_query, w_keyval, _, mine, theirs, held):
+    )(slots, counts, tokens, gain)
+
+
+def project_body(pick, core, slabs, w_query, w_keyval, *rest):
+    out = rest[-1]
     reps, rows, depth = slabs.shape
+    chips = reps // 2
     count = 16
     steps = (rows - count) // count
     requests = reps * count
-    owners = slabs[:, rows - count :, :requests].reshape(requests, requests).astype(jnp.float32)
-    number = lax.broadcasted_iota(jnp.int32, (requests, requests), 1).astype(jnp.float32)
+    core = core[0] if pick == 0 else 1 - core[0]
+    owners = slabs[:, rows - count :, :requests].reshape(chips, 2, count, requests)
+    owners = jnp.where(core == 0, owners[:, 0], owners[:, 1])
+    owners = owners.reshape(requests // 2, requests).astype(jnp.float32)
+    number = lax.broadcasted_iota(jnp.int32, owners.shape, 1).astype(jnp.float32)
     shuffle = jnp.where(owners == number, 1.0, 0.0).astype(jnp.bfloat16)
     query_cols = w_query.shape[1]
     for step in range(steps):
@@ -384,35 +403,31 @@
         for weight, at in ((w_query, 0), (w_keyval, query_cols)):
             product = jnp.dot(features, weight[...], preferred_element_type=jnp.float32)
             width = product.shape[1]
-            held[:, :, at : at + width] = product.astype(jnp.bfloat16).reshape(reps, count, width)
-        for one in range(2):
-
-            @pl.when(core[0] == one)
-            def _():
-                for chip in range(reps // 2):
-                    mine[chip, span] = held[2 * chip + one]
-                    theirs[chip, span] = held[2 * chip + 1 - one]
-
-
-def project_kernel(core, slabs, w_query, w_keyval, after):
+            product = product.reshape(chips, count, width)
+            if pick == 0:
+                product = product + rest[0][:, span, at : at + width].astype(jnp.float32)
+            out[:, span, at : at + width] = product.astype(jnp.bfloat16)
+
+
+def project_kernel(pick, core, slabs, w_query, w_keyval, operands):
     reps, rows, _ = slabs.shape
     width = w_query.shape[1] + w_keyval.shape[1]
-    half = jax.ShapeDtypeStruct((reps // 2, rows - 16, width), jnp.bfloat16)
     vmem = pl.BlockSpec(memory_space=pltpu.VMEM)
     return pl.pallas_call(
-        project_body,
-        out_shape=[half, half],
-        in_specs=smem_space(1) + [vmem] * 3 + any_space(1),
-        out_specs=[vmem] * 2,
-        scratch_shapes=[pltpu.VMEM((reps, 16, width), jnp.bfloat16)],
-        compiler_params=pltpu.CompilerParams(vmem_limit_bytes=VMEM_LIMIT),
-        cost_estimate=moved_cost(6 << 20),
+        functools.partial(project_body, pick),
+        out_shape=jax.ShapeDtypeStruct((reps // 2, rows - 16, width), jnp.bfloat16),
+        in_specs=smem_space(1)
+        + [vmem] * 3
+        + ([vmem] if pick == 0 else any_space(len(operands))),
+        out_specs=vmem,
+        compiler_params=pltpu.CompilerParams(vmem_limit_bytes=VMEM_COMPUTE),
+        cost_estimate=moved_cost(4 << 20),
         name="project_rows",
-    )(core[None].astype(jnp.int32), slabs, w_query, w_keyval, after)
-
-
-def attend_body(counts, sums, cache, *rest):
-    out, queries, keys, values, mixed = rest[-5:]
+    )(core[None].astype(jnp.int32), slabs, w_query, w_keyval, *operands)
+
+
+def attend_body(core, counts, sums, cache, *rest):
+    kept, given, queries, keys, values, mixed = rest[-6:]
     at = pl.program_id(0)
     together, _, span, width = cache.shape
     rows = sums.shape[1]
@@ -436,39 +451,64 @@
     many = heads * steps
     flat = (((1,), (1,)), ((), ()))
     factor = 1.0 / width**0.5
-    for one in range(together):
-        request = at * together + one
-        live = counts[request] * BLOCK
-        query = queries[pl.ds(request, many, stride=per_step)].astype(jnp.bfloat16)
-        key = keys[pl.ds(request, steps, stride=per_step)].astype(jnp.bfloat16)
-        value = values[pl.ds(request, steps, stride=per_step)].astype(jnp.bfloat16)
-        old = lax.dot_general(query, cache[one, 0], flat, preferred_element_type=jnp.float32)
-        place = lax.broadcasted_iota(jnp.int32, (many, span), 1)
-        old = jnp.where(place < live, old * factor, -1e30)
-        new = lax.dot_general(query, key, flat, preferred_element_type=jnp.float32)
-        later = lax.broadcasted_iota(jnp.int32, (many, steps), 1)
-        step = lax.broadcasted_iota(jnp.int32, (many, steps), 0) % steps
-        new = jnp.where(later <= step, new * factor, -1e30)
-        peak = jnp.maximum(
-            jnp.max(old, axis=-1, keepdims=True), jnp.max(new, axis=-1, keepdims=True)
-        )
-        old = jnp.exp(old - peak)
-        new = jnp.exp(new - peak)
-        total = jnp.sum(old, axis=-1, keepdims=True) + jnp.sum(new, axis=-1, keepdims=True)
-        old = (old / total).astype(jnp.bfloat16)
-        new = (new / total).astype(jnp.bfloat16)
-        result = jnp.dot(old, cache[one, 1], preferred_element_type=jnp.float32)
-        result = result + jnp.dot(new, value, preferred_element_type=jnp.float32)
-        mixed[pl.ds(request, many, stride=per_step)] = result
+    longest = counts[at * together]
+    for one in range(1, together):
+        longest = jnp.maximum(longest, counts[at * together + one])
+
+    def attend(reach):
+        for one in range(together):
+            request = at * together + one
+            live = counts[request] * BLOCK
+            query = queries[pl.ds(request, many, stride=per_step)].astype(jnp.bfloat16)
+            key = keys[pl.ds(request, steps, stride=per_step)].astype(jnp.bfloat16)
+            value = values[pl.ds(request, steps, stride=per_step)].astype(jnp.bfloat16)
+            old = lax.dot_general(
+                query, cache[one, 0, :reach], flat, preferred_element_type=jnp.float32
+            )
+            place = lax.broadcasted_iota(jnp.int32, (many, reach), 1)
+            old = jnp.where(place < live, old * factor, -1e30)
+            new = lax.dot_general(query, key, flat, preferred_element_type=jnp.float32)
+            later = lax.broadcasted_iota(jnp.int32, (many, steps), 1)
+            step = lax.broadcasted_iota(jnp.int32, (many, steps), 0) % steps
+            new = jnp.where(later <= step, new * factor, -1e30)
+            peak = jnp.maximum(
+                jnp.max(old, axis=-1, keepdims=True), jnp.max(new, axis=-1, keepdims=True)
+            )
+            old = jnp.exp(old - peak)
+            new = jnp.exp(new - peak)
+            total = jnp.sum(old, axis=-1, keepdims=True) + jnp.sum(new, axis=-1, keepdims=True)
+            share = 1.0 / total
+            old = (old * share).astype(jnp.bfloat16)
+            new = (new * share).astype(jnp.bfloat16)
+            result = jnp.dot(old, cache[one, 1, :reach], preferred_element_type=jnp.float32)
+            result = result + jnp.dot(new, value, preferred_element_type=jnp.float32)
+            mixed[pl.ds(request, many, stride=per_step)] = result
+
+    short = span // 2
+
+    @pl.when(longest * BLOCK <= short)
+    def _():
+        attend(short)
+
+    @pl.when(longest * BLOCK > short)
+    def _():
+        attend(span)
 
     @pl.when(at == pl.num_programs(0) - 1)
     def _():
-        for head in range(heads):
-            cols = slice(head * width, (head + 1) * width)
-            out[:, cols] = mixed[head * rows : (head + 1) * rows].astype(jnp.bfloat16)
-
-
-def attend_kernel(counts, sums, cache, after):
+        for one in range(2):
+
+            @pl.when(core[0] == one)
+            def _():
+                for head in range(heads):
+                    out = kept if head // (heads // 2) == one else given
+                    at = head % (heads // 2) * width
+                    out[:, at : at + width] = mixed[head * rows : (head + 1) * rows].astype(
+                        jnp.bfloat16
+                    )
+
+
+def attend_kernel(core, counts, sums, cache, after):
     requests, kinds, span, width = cache.shape
     rows = sums.shape[1]
     cols = sums.shape[2] - 2 * width
@@ -476,25 +516,25 @@
     together = 4
     return pl.pallas_call(
         attend_body,
-        out_shape=jax.ShapeDtypeStruct((rows, cols), jnp.bfloat16),
+        out_shape=[jax.ShapeDtypeStruct((rows, cols // 2), jnp.bfloat16)] * 2,
         grid=(requests // together,),
-        in_specs=smem_space(1)
+        in_specs=smem_space(2)
         + [
             pl.BlockSpec(sums.shape, lambda at: (0, 0, 0)),
             pl.BlockSpec((together, kinds, span, width), lambda at: (at, 0, 0, 0)),
         ]
         + any_space(len(after)),
-        out_specs=pl.BlockSpec((rows, cols), lambda at: (0, 0)),
+        out_specs=[pl.BlockSpec((rows, cols // 2), lambda at: (0, 0))] * 2,
         scratch_shapes=[
             pltpu.VMEM((heads * rows, width), jnp.float32),
             pltpu.VMEM((rows, width), jnp.float32),
             pltpu.VMEM((rows, width), jnp.float32),
             pltpu.VMEM((heads * rows, width), jnp.float32),
         ],
-        compiler_params=pltpu.CompilerParams(vmem_limit_bytes=VMEM_LIMIT),
+        compiler_params=pltpu.CompilerParams(vmem_limit_bytes=VMEM_COMPUTE),
         cost_estimate=moved_cost(16 << 20),
         name="attend_old_place",
-    )(counts, sums, cache, *after)
+    )(core[None].astype(jnp.int32), counts, sums, cache, *after)
 
 
 def output_body(core, slabs, near, far, weight, *rest):
@@ -537,7 +577,7 @@
         out_shape=jax.ShapeDtypeStruct((reps, rows, weight.shape[1]), jnp.bfloat16),
         in_specs=smem_space(1) + [vmem] * 4 + any_space(len(after)),
         out_specs=vmem,
-        compiler_params=pltpu.CompilerParams(vmem_limit_bytes=VMEM_LIMIT),
+        compiler_params=pltpu.CompilerParams(vmem_limit_bytes=VMEM_COMPUTE),
         cost_estimate=moved_cost(6 << 20),
         name="output_rows",
     )(core[None].astype(jnp.int32), slabs, near, far, weight, *after)
@@ -563,19 +603,11 @@
 
     own_table = jnp.stack([new_slot, block_counts])
     other_table = lax.ppermute(own_table, "rep", other_core)
-    lent = lax.ppermute(
-        lax.dynamic_index_in_dim(kv_cache, 1 - core, 1, keepdims=False), "rep", other_core
-    )
-
-    column = lax.broadcasted_iota(jnp.int32, (num_rows, depth), 1)
-    table = jnp.where(column < depth // 2, new_slot[:, None], block_counts[:, None])
     slabs = norm_kernel(
-        new_tokens.reshape(row_total, feat_width), norm_gain[None], table.astype(jnp.bfloat16), reps
-    )
+        new_slot, block_counts, new_tokens.reshape(row_total, feat_width), norm_gain, reps
+    )
+    lent = lax.ppermute(kv_cache, "rep", other_core)
     slabs = lax.all_to_all(slabs, "rep", split_axis=0, concat_axis=0, tiled=True)
-    slot_table = slabs[:, row_total:, 0].astype(jnp.int32).reshape(-1)
-    length_table = slabs[:, row_total:, depth // 2].astype(jnp.int32).reshape(-1)
-
     my_chip = rep_index // 2
     pair_table = jnp.where(
         core == 0,
@@ -597,10 +629,23 @@
             jnp.clip(fits, 0, pair_lengths),
         ]
     ).astype(jnp.int32)
-    sent = pack_kernel(core, pack_table, kv_cache, lent, [])
+    sent = pack_kernel(core, pack_table, kv_cache, lent, [], 1 << 10)
     leg_one = [
         lax.ppermute(piece, "rep", line_pairs(reps, line, 0)) for line, piece in enumerate(sent)
     ]
+
+    w_pair, *_ = lax.optimization_barrier((w_keyval, *sent))
+    w_pair = w_pair.reshape(depth, 2 * pair_cols)
+    theirs = project_kernel(1, core, slabs, w_query, w_pair, [sent[0]])
+    late_slabs, theirs = lax.optimization_barrier((slabs, theirs))
+    theirs = lax.ppermute(theirs, "rep", other_core)
+    pair_sum = project_kernel(0, core, slabs, w_query, w_pair, [theirs])
+    pair_sum = lax.all_to_all(
+        pair_sum, "rep", split_axis=0, concat_axis=0, tiled=True, axis_index_groups=same_core
+    )
+
+    slot_table = late_slabs[:, row_total:, 0].astype(jnp.int32).reshape(-1)
+    length_table = late_slabs[:, row_total:, depth // 2].astype(jnp.int32).reshape(-1)
 
     every = jnp.arange(reps * num_rows, dtype=jnp.int32)
     source, target = every // chip_rows, slot_table // chip_rows
@@ -637,25 +682,35 @@
             done,
         ],
     )
+    arrive_match = slot_table[None, :] == (my_chip * chip_rows + order)[:, None]
+    unpack_table = pick(
+        arrive_match,
+        [
+            jnp.where(moves_two, 4, jnp.where(moves_one, 3, home)),
+            jnp.where(moves_two, spot_two, jnp.where(moves_one, spot_one, from_home)),
+            done,
+        ],
+    )
+    late_fields = [late_place, done, missed]
+    late_pack = pick(
+        every[None, :] == (my_chip * chip_rows + order)[:, None], [target] + late_fields
+    )
+    late_unpack = pick(arrive_match, [source] + late_fields)
+
+    passed = pack_kernel(core, passing_table, kv_cache, lent, leg_one, 8 << 20)
     leg_two = [
-        lax.ppermute(piece, "rep", line_pairs(reps, line, 1))
-        for line, piece in enumerate(pack_kernel(core, passing_table, kv_cache, lent, leg_one))
-    ]
-
-    mine, theirs = project_kernel(
-        core, slabs, w_query, w_keyval.reshape(depth, 2 * pair_cols), sent[0]
-    )
-    theirs = lax.ppermute(theirs, "rep", other_core)
-    pair_sum = (mine.astype(jnp.float32) + theirs.astype(jnp.float32)).astype(jnp.bfloat16)
-    pair_sum = lax.all_to_all(
-        pair_sum, "rep", split_axis=0, concat_axis=0, tiled=True, axis_index_groups=same_core
-    )
-
-    attended = attend_kernel(block_counts, pair_sum, kv_cache, leg_one)
-
-    halves = attended.reshape(row_total, 2, head_cols // 2)
-    kept = lax.dynamic_index_in_dim(halves, core, 1, keepdims=False)
-    given = lax.dynamic_index_in_dim(halves, 1 - core, 1, keepdims=False)
+        lax.ppermute(piece, "rep", line_pairs(reps, line, 1)) for line, piece in enumerate(passed)
+    ]
+
+
+    kept, given = attend_kernel(
+        core,
+        block_counts,
+        pair_sum,
+        kv_cache,
+        [passed[0], unpack_table, late_pack, late_unpack],
+    )
+
     given = lax.ppermute(given, "rep", other_core)
     kept = jnp.where(core == 0, jnp.stack([kept, given]), jnp.stack([given, kept]))
     near = lax.all_to_all(
@@ -698,24 +753,10 @@
         jnp.concatenate([right, left], axis=1),
     ).reshape(num_steps, num_rows, 2 * out_cols)
 
-    arrive_match = slot_table[None, :] == (my_chip * chip_rows + order)[:, None]
-    unpack_table = pick(
-        arrive_match,
-        [
-            jnp.where(moves_two, 4, jnp.where(moves_one, 3, home)),
-            jnp.where(moves_two, spot_two, jnp.where(moves_one, spot_one, from_home)),
-            done,
-        ],
-    )
     cache_moved, held = unpack_kernel(
         core, unpack_table, kv_cache, lent, leg_one, leg_two, partial_out
     )
 
-    late_fields = [late_place, done, missed]
-    late_pack = pick(
-        every[None, :] == (my_chip * chip_rows + order)[:, None], [target] + late_fields
-    )
-    late_unpack = pick(arrive_match, [source] + late_fields)
 
     def more(state):
         start, moved, other = state

time: 197 us -> 179 us (0.909)
  starting transfers between devices: 44.4 us -> 67.2 us
  waiting for transfers between devices: 71 us -> 53.9 us
  other arithmetic: 17 us -> 6.62 us
  Pallas kernels: 45.2 us -> 36.9 us
  local copies, waits for them, and re-layouts: 15.5 us -> 10.6 us
    ppermute x3, waiting for transfers between devices: 22.4 us -> 0.01 us  [per_device(): lax.ppermute(piece, 'rep', line_pairs(reps, line, 0))]
    all_to_all x1, starting transfers between devices: 6.44 us -> 17.6 us  [per_device(): lax.all_to_all(pair_sum, 'rep', split_axis=0, concat_axis=0, tiled=True,...]
    all_to_all x1, starting transfers between devices: 6.46 us -> 16.6 us  [per_device(): lax.all_to_all(jnp.broadcast_to(kept[None], (chips,) + kept.shape), 'rep'...]
    all_to_all x1, waiting for transfers between devices: 17.3 us -> 7.89 us  [per_device(): lax.all_to_all(slabs, 'rep', split_axis=0, concat_axis=0, tiled=True)]
    ppermute x1, waiting for transfers between devices: 3.42 us -> 10.5 us  [per_device(): lax.ppermute(lax.dynamic_index_in_dim(summed, core, 0, keepdims=False), (...]
    ppermute x1, waiting for transfers between devices: 8.49 us -> 1.4 us  [per_device(): lax.ppermute(lax.dynamic_index_in_dim(summed, 1 - core, 0, keepdims=False...]
    all_to_all x1, waiting for transfers between devices: 0.01 us -> 6.35 us  [per_device(): lax.all_to_all(pair_sum, 'rep', split_axis=0, concat_axis=0, tiled=True,...]
    unnamed x13 -> x27, local copies, waits for them, and re-layouts: 2.44 us -> 7.99 us
  transfers between devices with their start and end apart: 18 -> 18, of which waited for: 8 -> 10; matrix products, arithmetic and copies ran while one was open for 14% -> 5% of each run, Pallas kernels for 13% -> 17%
where the time goes in v5:
time: 179 us; the launch traced here: 178 us
  starting transfers between devices  67.2 us (38%)
  waiting for transfers between devices  53.9 us (30%)
  Pallas kernels  36.9 us (21%)
  local copies, waits for them, and re-layouts  10.6 us (6%)
  other arithmetic  6.62 us (4%)
  between operations  2.38 us (1%)
    all_to_all x1, starting transfers between devices, per_device(): lax.all_to_all(pair_sum, 'rep', split_axis=0, concat_axis=0, tiled=True,...  17.6 us
    all_to_all x1, starting transfers between devices, per_device(): lax.all_to_all(jnp.broadcast_to(kept[None], (chips,) + kept.shape), 'rep'...  16.6 us
    all_to_all x1, waiting for transfers between devices, per_device(): lax.all_to_all(jnp.broadcast_to(kept[None], (chips,) + kept.shape), 'rep'...  14.4 us
    ppermute x1, waiting for transfers between devices, per_device(): lax.ppermute(lax.dynamic_index_in_dim(summed, core, 0, keepdims=False), (...  10.5 us
    pallas_call x2, Pallas kernels, pack_kernel(): pl.pallas_call(functools.partial(pack_body, len(lines)), out_shape=[line]...  9.8 us
    pallas_call x1, Pallas kernels, attend_kernel(): pl.pallas_call(attend_body, out_shape=[jax.ShapeDtypeStruct((rows, cols /...  8.12 us
    unnamed x27, local copies, waits for them, and re-layouts  7.99 us
    all_to_all x1, waiting for transfers between devices, per_device(): lax.all_to_all(slabs, 'rep', split_axis=0, concat_axis=0, tiled=True)  7.89 us
  transfers between devices with their start and end apart: 18, of which 10 were waited for; matrix products, arithmetic and copies ran while one was open for 5% of the time, Pallas kernels for 17%

profile of v5, /device:TPU:17, one launch (start us, length us, event | category | flops | bytes accessed | tf_op | source)
XLA Modules:
  0.0 177.7 jit_solution(11489358332533342085)
XLA Ops:
  5.4 2.1 %norm_rows.1 = bf16[16,80,512]{2,1,0:T(8,128)(2,1)} custom-call(s32[16]{0:T(128)S(1)} %copy-done.11, s32[16]{0:T(128)S(1)} %copy-done.9, bf16[64,8192]{1,0:T(8,128)(2,1)S(1)} %bitcast.65, bf16[8192]{0:T(1024)(128)(2,1)S(1)} %copy-done.8), custom_call_target="tpu_custom_call" | custom-call | bytes 4194304 | tf_op jit(solution)/shard_map/norm_rows/pallas_call | solution.py:373
  7.6 3.5 %collective-permute-done = s32[2,16]{1,0:T(2,128)S(1)} collective-permute-done((s32[2,16]{1,0:T(2,128)S(1)}, s32[2,16]{1,0:T(2,128)S(1)}, u32[]{:S(2)}, u32[]{:S(2)}) %collective-permute-start) | collective-permute-done | bytes 160 | tf_op jit(solution)/shard_map/ppermute | solution.py:605
  11.2 7.1 %all-to-all-start.1 = ((bf16[16,80,512]{2,1,0:T(8,128)(2,1)}), bf16[16,80,512]{2,1,0:T(8,128)(2,1)S(1)}, u32[]{:S(2)}, u32[]{:S(2)}) async-start(bf16[16,80,512]{2,1,0:T(8,128)(2,1)} %norm_rows.1), calls=%async_computation.1 | async-start | bytes 2621440 | tf_op jit(solution)/shard_map/all_to_all | solution.py:610
  19.3 4.5 %pack_blocks.2 = (bf16[38,128,128]{2,1,0:T(8,128)(2,1)}, bf16[38,128,128]{2,1,0:T(8,128)(2,1)}, bf16[38,128,128]{2,1,0:T(8,128)(2,1)}) custom-call(s32[1]{0:T(128)} %bitcast.2.core.scalars, s32[4,32]{1,0:T(4,128)} %pad_add_fusion.9.table, bf16[16,2,768,128]{3,2,1,0:T(8,128)(2,1)} %cache.7, bf16[16,2,768,128]{3,2,1,0:T(8,128)(2,1)} %collective-permute-done.1.lent), custom_call_target="tpu_custom_call" | custom-call | bytes 1024 | tf_op jit(solution)/shard_map/pack_blocks/pallas_call | solution.py:146
  23.8 1.8 collective-permute-start.5
  25.6 2.9 %collective-permute-start.3 = (bf16[38,128,128]{2,1,0:T(8,128)(2,1)}, bf16[38,128,128]{2,1,0:T(8,128)(2,1)}, u32[]{:S(2)}, u32[]{:S(2)}) collective-permute-start(bf16[38,128,128]{2,1,0:T(8,128)(2,1)} %get-tuple-element.69.rest_0_), channel_id=1, source_target_pairs={{0,32},{8,24},{16,48},{24,8},{32,64},{40,56},{48,80},{56,40},{64,9... | collective-permute-start | bytes 3735560 | tf_op jit(solution)/shard_map/ppermute | solution.py:634
  28.6 7.9 %all-to-all-done.1.slabs = bf16[16,80,512]{2,1,0:T(8,128)(2,1)S(1)} async-done(((bf16[16,80,512]{2,1,0:T(8,128)(2,1)}), bf16[16,80,512]{2,1,0:T(8,128)(2,1)S(1)}, u32[]{:S(2)}, u32[]{:S(2)}) %all-to-all-start.1) | async-done | bytes 1310752 | tf_op jit(solution)/shard_map/all_to_all | solution.py:610
  36.5 1.3 copy-done.3
  37.8 1.4 project_rows.2
  42.3 2.1 %collective-permute-done.2.rest_0_ = bf16[8,64,1280]{2,1,0:T(8,128)(2,1)} collective-permute-done((bf16[8,64,1280]{2,1,0:T(8,128)(2,1)}, bf16[8,64,1280]{2,1,0:T(8,128)(2,1)}, u32[]{:S(2)}, u32[]{:S(2)}) %collective-permute-start.2) | collective-permute-done | bytes 1310752 | tf_op jit(solution)/shard_map/ppermute | solution.py:641
  44.5 2.7 %project_rows.3 = bf16[8,64,1280]{2,1,0:T(8,128)(2,1)S(1)} custom-call(s32[1]{0:T(128)} %bitcast.2.core.scalars, bf16[16,80,512]{2,1,0:T(8,128)(2,1)S(1)} %all-to-all-done.1.slabs, bf16[512,1024]{1,0:T(8,128)(2,1)S(1)} %copy-done.1, bf16[512,256]{1,0:T(8,128)(2,1)S(1)} %bitcast.64, bf16[8,64,1280]{2,1,0:T(8,128)(2,1)} %collective-permute-done.2.rest_0_), custom_call_target="tpu_custom_call" | custom-call | bytes 4194304 | tf_op jit(solution)/shard_map/project_rows/pallas_call | solution.py:416
  48.2 17.6 %all-to-all-start.2 = ((bf16[8,64,1280]{2,1,0:T(8,128)(2,1)}), bf16[8,64,1280]{2,1,0:T(8,128)(2,1)S(1)}, u32[]{:S(2)}, u32[]{:S(2)}) async-start(bf16[8,64,1280]{2,1,0:T(8,128)(2,1)} %copy-done), calls=%async_computation.2 | async-start | bytes 2621440 | tf_op jit(solution)/shard_map/all_to_all | solution.py:643
  66.9 5.3 %pack_blocks.3 = (bf16[38,128,128]{2,1,0:T(8,128)(2,1)}, bf16[38,128,128]{2,1,0:T(8,128)(2,1)}, bf16[38,128,128]{2,1,0:T(8,128)(2,1)}) custom-call(s32[1]{0:T(128)} %bitcast.2.core.scalars, s32[4,64]{1,0:T(4,128)} %select_reduce_fusion.2.table, bf16[16,2,768,128]{3,2,1,0:T(8,128)(2,1)} %cache.7, bf16[16,2,768,128]{3,2,1,0:T(8,128)(2,1)} %collective-permute-done.1.lent, ...), custom_call_target="tpu_custom_call" | custom-call | bytes 8388608 | tf_op jit(solution)/shard_map/pack_blocks/pallas_call | solution.py:146
  72.2 2.6 %collective-permute-start.8 = (bf16[38,128,128]{2,1,0:T(8,128)(2,1)}, bf16[38,128,128]{2,1,0:T(8,128)(2,1)}, u32[]{:S(2)}, u32[]{:S(2)}) collective-permute-start(bf16[38,128,128]{2,1,0:T(8,128)(2,1)} %get-tuple-element.78), channel_id=1, source_target_pairs={{0,16},{8,104},{16,0},{24,120},{32,48},{40,8},{48,32},{56,24},{64,... | collective-permute-start | bytes 3735560 | tf_op jit(solution)/shard_map/ppermute | solution.py:702
  74.8 2.6 %collective-permute-start.9 = (bf16[38,128,128]{2,1,0:T(8,128)(2,1)}, bf16[38,128,128]{2,1,0:T(8,128)(2,1)}, u32[]{:S(2)}, u32[]{:S(2)}) collective-permute-start(bf16[38,128,128]{2,1,0:T(8,128)(2,1)} %get-tuple-element.79), channel_id=1, source_target_pairs={{8,72},{24,88},{40,104},{56,120},{72,8},{88,24},{104,40},{120,56},... | collective-permute-start | bytes 3735560 | tf_op jit(solution)/shard_map/ppermute | solution.py:702
  78.2 6.4 %all-to-all-done.2.sums = bf16[8,64,1280]{2,1,0:T(8,128)(2,1)S(1)} async-done(((bf16[8,64,1280]{2,1,0:T(8,128)(2,1)}), bf16[8,64,1280]{2,1,0:T(8,128)(2,1)S(1)}, u32[]{:S(2)}, u32[]{:S(2)}) %all-to-all-start.2) | async-done | bytes 1310752 | tf_op jit(solution)/shard_map/all_to_all | solution.py:643
  85.9 8.1 %attend_old_place.1 = (bf16[64,512]{1,0:T(8,128)(2,1)S(1)}, bf16[64,512]{1,0:T(8,128)(2,1)S(1)}) custom-call(s32[1]{0:T(128)} %bitcast.2.core.scalars, s32[16]{0:T(128)S(1)} %copy-done.10, bf16[8,64,1280]{2,1,0:T(8,128)(2,1)S(1)} %all-to-all-done.2.sums, bf16[16,2,768,128]{3,2,1,0:T(8,128)(2,1)} %cache.7, bf16[38,128,128]{2,1,0:T(8,128)(2,1)S(1)} %copy-done.4, ...), custom_call_target="tpu_custom_call" | custom-call | bytes 16777216 | tf_op jit(solution)/shard_map/attend_old_place/pallas_call | solution.py:517
  94.0 2.0 %collective-permute-start.6 = (bf16[64,512]{1,0:T(8,128)(2,1)S(1)}, bf16[64,512]{1,0:T(8,128)(2,1)S(1)}, u32[]{:S(2)}, u32[]{:S(2)}) collective-permute-start(bf16[64,512]{1,0:T(8,128)(2,1)S(1)} %get-tuple-element.77), channel_id=1, source_target_pairs={{0,8},{8,0},{16,24},{24,16},{32,40},{40,32},{48,56},{56,48},{64,72... | collective-permute-start | bytes 196616 | tf_op jit(solution)/shard_map/ppermute | solution.py:714
  98.0 16.6 %all-to-all-start.3 = ((bf16[8,2,64,512]{3,2,1,0:T(8,128)(2,1)}), bf16[8,2,64,512]{3,2,1,0:T(8,128)(2,1)S(1)}, u32[]{:S(2)}, u32[]{:S(2)}) async-start(bf16[8,2,64,512]{3,2,1,0:T(8,128)(2,1)} %broadcast_in_dim.313), calls=%async_computation.3 | async-start | bytes 2097152 | tf_op jit(solution)/shard_map/all_to_all | solution.py:716
  114.7 14.4 %all-to-all-done.3 = bf16[8,2,64,512]{3,2,1,0:T(8,128)(2,1)S(1)} async-done(((bf16[8,2,64,512]{3,2,1,0:T(8,128)(2,1)}), bf16[8,2,64,512]{3,2,1,0:T(8,128)(2,1)S(1)}, u32[]{:S(2)}, u32[]{:S(2)}) %all-to-all-start.3) | async-done | bytes 1048608 | tf_op jit(solution)/shard_map/all_to_all | solution.py:716
  129.0 1.4 collective-permute-start.10
  130.5 2.3 %collective-permute-done.10.far = bf16[16,64,512]{2,1,0:T(8,128)(2,1)S(1)} collective-permute-done((bf16[16,64,512]{2,1,0:T(8,128)(2,1)S(1)}, bf16[16,64,512]{2,1,0:T(8,128)(2,1)S(1)}, u32[]{:S(2)}, u32[]{:S(2)}) %collective-permute-start.10) | collective-permute-done | bytes 1048608 | tf_op jit(solution)/shard_map/ppermute | solution.py:725
  132.7 3.0 %output_rows.1.rest_6_ = bf16[16,64,512]{2,1,0:T(8,128)(2,1)} custom-call(s32[1]{0:T(128)} %bitcast.2.core.scalars, bf16[16,80,512]{2,1,0:T(8,128)(2,1)S(1)} %all-to-all-done.1.slabs, bf16[16,64,512]{2,1,0:T(8,128)(2,1)S(1)} %bitcast.62, bf16[16,64,512]{2,1,0:T(8,128)(2,1)S(1)} %collective-permute-done.10.far, bf16[1024,512]{1,0:T(8,128)(2,1)S(1)} %copy-done.6), custom_call_target="tpu_custom_call" | custom-call | bytes 6291456 | tf_op jit(solution)/shard_map/output_rows/pallas_call | solution.py:575
  135.8 5.7 %all-to-all-start.4 = ((bf16[8,128,512]{2,1,0:T(8,128)(2,1)}), bf16[8,128,512]{2,1,0:T(8,128)(2,1)S(1)}, u32[]{:S(2)}, u32[]{:S(2)}) async-start(bf16[8,128,512]{2,1,0:T(8,128)(2,1)} %bitcast.21), calls=%async_computation.4 | async-start | bytes 2097152 | tf_op jit(solution)/shard_map/all_to_all | solution.py:728
  145.1 7.0 %unpack_blocks.1 = (bf16[16,2,768,128]{3,2,1,0:T(8,128)(2,1)}, bf16[16,768,128]{2,1,0:T(8,128)(2,1)}) custom-call(s32[1]{0:T(128)} %bitcast.2.core.scalars, s32[3,32]{1,0:T(4,128)} %copy-done.7, bf16[16,2,768,128]{3,2,1,0:T(8,128)(2,1)} %cache.7, bf16[16,2,768,128]{3,2,1,0:T(8,128)(2,1)} %collective-permute-done.1.lent, ...), custom_call_target="tpu_custom_call" | custom-call | bytes 10485760 | tf_op jit(solution)/shard_map/unpack_blocks/pallas_call | solution.py:196
  152.1 4.6 %all-to-all-done.4 = bf16[8,128,512]{2,1,0:T(8,128)(2,1)S(1)} async-done(((bf16[8,128,512]{2,1,0:T(8,128)(2,1)}), bf16[8,128,512]{2,1,0:T(8,128)(2,1)S(1)}, u32[]{:S(2)}, u32[]{:S(2)}) %all-to-all-start.4) | async-done | bytes 1048608 | tf_op jit(solution)/shard_map/all_to_all | solution.py:728
  156.7 1.5 collective-permute-start.13
  158.4 2.1 %collective-permute-start.11 = (bf16[64,512]{1,0:T(8,128)(2,1)S(1)}, bf16[64,512]{1,0:T(8,128)(2,1)S(1)}, u32[]{:S(2)}, u32[]{:S(2)}) collective-permute-start(bf16[64,512]{1,0:T(8,128)(2,1)S(1)} %get-tuple-element.143), channel_id=1, source_target_pairs={{0,0},{1,16},{2,32},{3,48},{4,64},{5,80},{6,96},{7,112},{8,8},{9,2... | collective-permute-start | bytes 196616 | tf_op jit(solution)/shard_map/ppermute | solution.py:744
  160.5 1.6 collective-permute-start.12
  162.0 10.5 %collective-permute-done.11 = bf16[64,512]{1,0:T(8,128)(2,1)S(1)} collective-permute-done((bf16[64,512]{1,0:T(8,128)(2,1)S(1)}, bf16[64,512]{1,0:T(8,128)(2,1)S(1)}, u32[]{:S(2)}, u32[]{:S(2)}) %collective-permute-start.11) | collective-permute-done | bytes 65568 | tf_op jit(solution)/shard_map/ppermute | solution.py:744
  172.6 1.4 collective-permute-done.12
  174.7 2.9 %put_other_kind.1 = bf16[16,2,768,128]{3,2,1,0:T(8,128)(2,1)} custom-call(s32[1]{0:T(128)} %bitcast.2.core.scalars, bf16[16,768,128]{2,1,0:T(8,128)(2,1)} %collective-permute-done.13.returned, bf16[16,2,768,128]{3,2,1,0:T(8,128)(2,1)} %get-tuple-element.86._), custom_call_target="tpu_custom_call", output_to_operand_aliasing={{}: (2, {})} | custom-call | bytes 6291456 | tf_op jit(solution)/shard_map/put_other_kind/pallas_call | solution.py:329
  (93 shorter events, 18.5 us)
Async XLA Ops:
  0.6 18.6 %collective-permute-start.1 = (bf16[16,2,768,128]{3,2,1,0:T(8,128)(2,1)}, bf16[16,2,768,128]{3,2,1,0:T(8,128)(2,1)}, u32[]{:S(2)}, u32[]{:S(2)}) collective-permute-start(bf16[16,2,768,128]{3,2,1,0:T(8,128)(2,1)} %cache.7), channel_id=1, source_target_pairs={{0,8},{8,0},{16,24},{24,16},{32,40},{40,32},{48,56},{56,48},{64,72... | collective-permute-start | bytes 18874376 | tf_op jit(solution)/shard_map/ppermute | solution.py:609
  2.1 9.0 %collective-permute-start = (s32[2,16]{1,0:T(2,128)S(1)}, s32[2,16]{1,0:T(2,128)S(1)}, u32[]{:S(2)}, u32[]{:S(2)}) collective-permute-start(s32[2,16]{1,0:T(2,128)S(1)} %pad_add_fusion.10), channel_id=1, source_target_pairs={{0,8},{8,0},{16,24},{24,16},{32,40},{40,32},{48,56},{56,48},{64,72... | collective-permute-start | bytes 392 | tf_op jit(solution)/shard_map/ppermute | solution.py:605
  2.2 1.2 copy-start.5
  3.4 0.7 copy-start.8
  4.1 0.7 copy-start.9
  4.8 0.7 copy-start.11
  11.2 25.3 %all-to-all-start.1 = ((bf16[16,80,512]{2,1,0:T(8,128)(2,1)}), bf16[16,80,512]{2,1,0:T(8,128)(2,1)S(1)}, u32[]{:S(2)}, u32[]{:S(2)}) async-start(bf16[16,80,512]{2,1,0:T(8,128)(2,1)} %norm_rows.1), calls=%async_computation.1 | async-start | bytes 2621440 | tf_op jit(solution)/shard_map/all_to_all | solution.py:610
  19.3 9.3 %copy-start.13 = (bf16[512,2,128]{2,1,0:T(2,128)(2,1)S(1)}, bf16[512,2,128]{2,1,0:T(2,128)(2,1)}, u32[]{:S(2)}) copy-start(bf16[512,2,128]{2,1,0:T(2,128)(2,1)} %param.13) | copy-start | bytes 786436
  19.3 17.2 %copy-start.1 = (bf16[512,1024]{1,0:T(8,128)(2,1)S(1)}, bf16[512,1024]{1,0:T(8,128)(2,1)}, u32[]{:S(2)}) copy-start(bf16[512,1024]{1,0:T(8,128)(2,1)} %w_query.3) | copy-start | bytes 3145732
  23.7 43.2 %collective-permute-start.4 = (bf16[38,128,128]{2,1,0:T(8,128)(2,1)}, bf16[38,128,128]{2,1,0:T(8,128)(2,1)}, u32[]{:S(2)}, u32[]{:S(2)}) collective-permute-start(bf16[38,128,128]{2,1,0:T(8,128)(2,1)} %get-tuple-element.70), channel_id=1, source_target_pairs={{0,96},{8,24},{16,112},{24,8},{32,0},{40,56},{48,16},{56,40},{64,3... | collective-permute-start | bytes 3735560 | tf_op jit(solution)/shard_map/ppermute | solution.py:634
  23.8 43.1 %collective-permute-start.5 = (bf16[38,128,128]{2,1,0:T(8,128)(2,1)}, bf16[38,128,128]{2,1,0:T(8,128)(2,1)}, u32[]{:S(2)}, u32[]{:S(2)}) collective-permute-start(bf16[38,128,128]{2,1,0:T(8,128)(2,1)} %get-tuple-element.71), channel_id=1, source_target_pairs={{0,64},{16,80},{32,96},{48,112},{64,0},{80,16},{96,32},{112,48},{1... | collective-permute-start | bytes 3735560 | tf_op jit(solution)/shard_map/ppermute | solution.py:634
  25.6 41.3 %collective-permute-start.3 = (bf16[38,128,128]{2,1,0:T(8,128)(2,1)}, bf16[38,128,128]{2,1,0:T(8,128)(2,1)}, u32[]{:S(2)}, u32[]{:S(2)}) collective-permute-start(bf16[38,128,128]{2,1,0:T(8,128)(2,1)} %get-tuple-element.69.rest_0_), channel_id=1, source_target_pairs={{0,32},{8,24},{16,48},{24,8},{32,64},{40,56},{48,80},{56,40},{64,9... | collective-permute-start | bytes 3735560 | tf_op jit(solution)/shard_map/ppermute | solution.py:634
  36.5 1.3 copy-start.3
  39.1 1.1 copy-start.2
  41.0 3.5 %collective-permute-start.2 = (bf16[8,64,1280]{2,1,0:T(8,128)(2,1)}, bf16[8,64,1280]{2,1,0:T(8,128)(2,1)}, u32[]{:S(2)}, u32[]{:S(2)}) collective-permute-start(bf16[8,64,1280]{2,1,0:T(8,128)(2,1)} %copy-done.2), channel_id=1, source_target_pairs={{0,8},{8,0},{16,24},{24,16},{32,40},{40,32},{48,56},{56,48},{64,72... | collective-permute-start | bytes 3932168 | tf_op jit(solution)/shard_map/ppermute | solution.py:641
  47.1 1.1 copy-start
  48.2 36.4 %all-to-all-start.2 = ((bf16[8,64,1280]{2,1,0:T(8,128)(2,1)}), bf16[8,64,1280]{2,1,0:T(8,128)(2,1)S(1)}, u32[]{:S(2)}, u32[]{:S(2)}) async-start(bf16[8,64,1280]{2,1,0:T(8,128)(2,1)} %copy-done), calls=%async_computation.2 | async-start | bytes 2621440 | tf_op jit(solution)/shard_map/all_to_all | solution.py:643
  66.9 17.7 %copy-start.10 = (s32[16]{0:T(128)S(1)}, s32[16]{0:T(128)}, u32[]{:S(2)}) copy-start(s32[16]{0:T(128)} %counts.3) | copy-start | bytes 196
  72.2 42.4 %collective-permute-start.8 = (bf16[38,128,128]{2,1,0:T(8,128)(2,1)}, bf16[38,128,128]{2,1,0:T(8,128)(2,1)}, u32[]{:S(2)}, u32[]{:S(2)}) collective-permute-start(bf16[38,128,128]{2,1,0:T(8,128)(2,1)} %get-tuple-element.78), channel_id=1, source_target_pairs={{0,16},{8,104},{16,0},{24,120},{32,48},{40,8},{48,32},{56,24},{64,... | collective-permute-start | bytes 3735560 | tf_op jit(solution)/shard_map/ppermute | solution.py:702
  74.8 39.8 %collective-permute-start.9 = (bf16[38,128,128]{2,1,0:T(8,128)(2,1)}, bf16[38,128,128]{2,1,0:T(8,128)(2,1)}, u32[]{:S(2)}, u32[]{:S(2)}) collective-permute-start(bf16[38,128,128]{2,1,0:T(8,128)(2,1)} %get-tuple-element.79), channel_id=1, source_target_pairs={{8,72},{24,88},{40,104},{56,120},{72,8},{88,24},{104,40},{120,56},... | collective-permute-start | bytes 3735560 | tf_op jit(solution)/shard_map/ppermute | solution.py:702
  77.4 37.2 %collective-permute-start.7 = (bf16[38,128,128]{2,1,0:T(8,128)(2,1)}, bf16[38,128,128]{2,1,0:T(8,128)(2,1)}, u32[]{:S(2)}, u32[]{:S(2)}) collective-permute-start(bf16[38,128,128]{2,1,0:T(8,128)(2,1)} %get-tuple-element.75.rest_0_), channel_id=1, source_target_pairs={{0,16},{8,40},{16,0},{24,56},{32,48},{40,72},{48,32},{56,88},{64,8... | collective-permute-start | bytes 3735560 | tf_op jit(solution)/shard_map/ppermute | solution.py:702
  78.1 15.9 %copy-start.7 = (s32[3,32]{1,0:T(4,128)}, s32[3,32]{1,0:T(4,128)S(1)}, u32[]{:S(2)}) copy-start(s32[3,32]{1,0:T(4,128)S(1)} %select_reduce_fusion.11.rest_1_.table) | copy-start | bytes 1156
  84.6 1.3 copy-start.4
  94.0 2.9 %collective-permute-start.6 = (bf16[64,512]{1,0:T(8,128)(2,1)S(1)}, bf16[64,512]{1,0:T(8,128)(2,1)S(1)}, u32[]{:S(2)}, u32[]{:S(2)}) collective-permute-start(bf16[64,512]{1,0:T(8,128)(2,1)S(1)} %get-tuple-element.77), channel_id=1, source_target_pairs={{0,8},{8,0},{16,24},{24,16},{32,40},{40,32},{48,56},{56,48},{64,72... | collective-permute-start | bytes 196616 | tf_op jit(solution)/shard_map/ppermute | solution.py:714
  98.0 34.7 %copy-start.6 = (bf16[1024,512]{1,0:T(8,128)(2,1)S(1)}, bf16[1024,512]{1,0:T(8,128)(2,1)}, u32[]{:S(2)}) copy-start(bf16[1024,512]{1,0:T(8,128)(2,1)} %weight.1) | copy-start | bytes 3145732
  98.0 31.0 %all-to-all-start.3 = ((bf16[8,2,64,512]{3,2,1,0:T(8,128)(2,1)}), bf16[8,2,64,512]{3,2,1,0:T(8,128)(2,1)S(1)}, u32[]{:S(2)}, u32[]{:S(2)}) async-start(bf16[8,2,64,512]{3,2,1,0:T(8,128)(2,1)} %broadcast_in_dim.313), calls=%async_computation.3 | async-start | bytes 2097152 | tf_op jit(solution)/shard_map/all_to_all | solution.py:716
  129.0 3.7 %collective-permute-start.10 = (bf16[16,64,512]{2,1,0:T(8,128)(2,1)S(1)}, bf16[16,64,512]{2,1,0:T(8,128)(2,1)S(1)}, u32[]{:S(2)}, u32[]{:S(2)}) collective-permute-start(bf16[16,64,512]{2,1,0:T(8,128)(2,1)S(1)} %bitcast.61), channel_id=1, source_target_pairs={{0,8},{8,0},{16,24},{24,16},{32,40},{40,32},{48,56},{56,48},{64,72... | collective-permute-start | bytes 3145736 | tf_op jit(solution)/shard_map/ppermute | solution.py:725
  135.8 20.9 %all-to-all-start.4 = ((bf16[8,128,512]{2,1,0:T(8,128)(2,1)}), bf16[8,128,512]{2,1,0:T(8,128)(2,1)S(1)}, u32[]{:S(2)}, u32[]{:S(2)}) async-start(bf16[8,128,512]{2,1,0:T(8,128)(2,1)} %bitcast.21), calls=%async_computation.4 | async-start | bytes 2097152 | tf_op jit(solution)/shard_map/all_to_all | solution.py:728
  156.7 18.0 %collective-permute-start.13 = (bf16[16,768,128]{2,1,0:T(8,128)(2,1)}, bf16[16,768,128]{2,1,0:T(8,128)(2,1)}, u32[]{:S(2)}, u32[]{:S(2)}) collective-permute-start(bf16[16,768,128]{2,1,0:T(8,128)(2,1)} %get-tuple-element.85), channel_id=1, source_target_pairs={{0,8},{8,0},{16,24},{24,16},{32,40},{40,32},{48,56},{56,48},{64,72... | collective-permute-start | bytes 9437192 | tf_op jit(solution)/shard_map/ppermute | solution.py:777
  158.4 14.2 %collective-permute-start.11 = (bf16[64,512]{1,0:T(8,128)(2,1)S(1)}, bf16[64,512]{1,0:T(8,128)(2,1)S(1)}, u32[]{:S(2)}, u32[]{:S(2)}) collective-permute-start(bf16[64,512]{1,0:T(8,128)(2,1)S(1)} %get-tuple-element.143), channel_id=1, source_target_pairs={{0,0},{1,16},{2,32},{3,48},{4,64},{5,80},{6,96},{7,112},{8,8},{9,2... | collective-permute-start | bytes 196616 | tf_op jit(solution)/shard_map/ppermute | solution.py:744
  160.5 13.5 %collective-permute-start.12 = (bf16[64,512]{1,0:T(8,128)(2,1)S(1)}, bf16[64,512]{1,0:T(8,128)(2,1)S(1)}, u32[]{:S(2)}, u32[]{:S(2)}) collective-permute-start(bf16[64,512]{1,0:T(8,128)(2,1)S(1)} %get-tuple-element.144), channel_id=1, source_target_pairs={{0,8},{1,24},{2,40},{3,56},{4,72},{5,88},{6,104},{7,120},{8,0},{9,... | collective-permute-start | bytes 196616 | tf_op jit(solution)/shard_map/ppermute | solution.py:747

commit v6 on v5

--- a/solution.py
+++ b/solution.py
@@ -449,40 +449,59 @@
                 values[...] = total
 
     many = heads * steps
+    lanes = together * many
+    factor = 1.0 / width**0.5
+    first = at * together
+    longest = counts[first]
+    for one in range(1, together):
+        longest = jnp.maximum(longest, counts[first + one])
     flat = (((1,), (1,)), ((), ()))
-    factor = 1.0 / width**0.5
-    longest = counts[at * together]
-    for one in range(1, together):
-        longest = jnp.maximum(longest, counts[at * together + one])
+    turned = (((0,), (0,)), ((), ()))
+
+    def gather(ref, number):
+        rows_of = [ref[pl.ds(first + one, number, stride=per_step)] for one in range(together)]
+        return jnp.concatenate(rows_of, axis=0).astype(jnp.bfloat16)
 
     def attend(reach):
+        query = gather(queries, many)
+        lane = lax.broadcasted_iota(jnp.int32, (1, lanes), 1)
+        live = jnp.zeros((1, lanes), jnp.int32)
+        old = jnp.zeros((reach, lanes), jnp.float32)
         for one in range(together):
-            request = at * together + one
-            live = counts[request] * BLOCK
-            query = queries[pl.ds(request, many, stride=per_step)].astype(jnp.bfloat16)
-            key = keys[pl.ds(request, steps, stride=per_step)].astype(jnp.bfloat16)
-            value = values[pl.ds(request, steps, stride=per_step)].astype(jnp.bfloat16)
-            old = lax.dot_general(
-                query, cache[one, 0, :reach], flat, preferred_element_type=jnp.float32
+            here = lane // many == one
+            live = jnp.where(here, counts[first + one] * BLOCK, live)
+            product = lax.dot_general(
+                cache[one, 0, :reach], query, flat, preferred_element_type=jnp.float32
             )
-            place = lax.broadcasted_iota(jnp.int32, (many, reach), 1)
-            old = jnp.where(place < live, old * factor, -1e30)
-            new = lax.dot_general(query, key, flat, preferred_element_type=jnp.float32)
-            later = lax.broadcasted_iota(jnp.int32, (many, steps), 1)
-            step = lax.broadcasted_iota(jnp.int32, (many, steps), 0) % steps
-            new = jnp.where(later <= step, new * factor, -1e30)
-            peak = jnp.maximum(
-                jnp.max(old, axis=-1, keepdims=True), jnp.max(new, axis=-1, keepdims=True)
+            old = jnp.where(here, product, old)
+        place = lax.broadcasted_iota(jnp.int32, (reach, lanes), 0)
+        old = jnp.where(place < live, old * factor, -1e30)
+        new = lax.dot_general(
+            gather(keys, steps), query, flat, preferred_element_type=jnp.float32
+        )
+        row = lax.broadcasted_iota(jnp.int32, new.shape, 0)
+        column = lax.broadcasted_iota(jnp.int32, new.shape, 1)
+        seen = (row // steps == column // many) & (row % steps <= column % steps)
+        new = jnp.where(seen, new * factor, -1e30)
+        peak = jnp.maximum(
+            jnp.max(old, axis=0, keepdims=True), jnp.max(new, axis=0, keepdims=True)
+        )
+        old = jnp.exp(old - peak)
+        new = jnp.exp(new - peak)
+        total = jnp.sum(old, axis=0, keepdims=True) + jnp.sum(new, axis=0, keepdims=True)
+        share = 1.0 / total
+        old = (old * share).astype(jnp.bfloat16)
+        new = (new * share).astype(jnp.bfloat16)
+        fresh = lax.dot_general(
+            new, gather(values, steps), turned, preferred_element_type=jnp.float32
+        )
+        turned_old = jnp.transpose(old)
+        for one in range(together):
+            span_of = slice(one * many, (one + 1) * many)
+            result = jnp.dot(
+                turned_old[span_of], cache[one, 1, :reach], preferred_element_type=jnp.float32
             )
-            old = jnp.exp(old - peak)
-            new = jnp.exp(new - peak)
-            total = jnp.sum(old, axis=-1, keepdims=True) + jnp.sum(new, axis=-1, keepdims=True)
-            share = 1.0 / total
-            old = (old * share).astype(jnp.bfloat16)
-            new = (new * share).astype(jnp.bfloat16)
-            result = jnp.dot(old, cache[one, 1, :reach], preferred_element_type=jnp.float32)
-            result = result + jnp.dot(new, value, preferred_element_type=jnp.float32)
-            mixed[pl.ds(request, many, stride=per_step)] = result
+            mixed[pl.ds(first + one, many, stride=per_step)] = result + fresh[span_of]
 
     short = span // 2
 
@@ -697,6 +716,9 @@
     )
     late_unpack = pick(arrive_match, [source] + late_fields)
 
+    late_pack, late_unpack, most = lax.optimization_barrier((late_pack, late_unpack, most))
+    most_row = jnp.broadcast_to(most, (1, late_pack.shape[1]))
+    late_pack = jnp.concatenate([late_pack, most_row.astype(jnp.int32)])
     passed = pack_kernel(core, passing_table, kv_cache, lent, leg_one, 8 << 20)
     leg_two = [
         lax.ppermute(piece, "rep", line_pairs(reps, line, 1)) for line, piece in enumerate(passed)
@@ -725,6 +747,9 @@
     far = lax.ppermute(near, "rep", other_core)
 
     partial_out = output_kernel(core, slabs, near, far, w_output, [])
+    cache_moved, held = unpack_kernel(
+        core, unpack_table, kv_cache, lent, leg_one, leg_two, partial_out
+    )
     exchanged = lax.all_to_all(
         partial_out.reshape(tps, all_rows // tps, out_cols),
         "tp",
@@ -733,30 +758,6 @@
         tiled=True,
     )
     first, exchanged = lax.optimization_barrier((jnp.int32(0), exchanged))
-    summed = jnp.sum(exchanged.astype(jnp.float32), axis=0).astype(jnp.bfloat16)
-    summed = summed.reshape(2, row_total, out_cols)
-    straight = [
-        (r * tps + t, (2 * t + r % 2) * tps + r // 2) for r in range(reps) for t in range(tps)
-    ]
-    crossed = [
-        (r * tps + t, (2 * t + 1 - r % 2) * tps + r // 2) for r in range(reps) for t in range(tps)
-    ]
-    left = lax.ppermute(
-        lax.dynamic_index_in_dim(summed, core, 0, keepdims=False), ("rep", "tp"), straight
-    )
-    right = lax.ppermute(
-        lax.dynamic_index_in_dim(summed, 1 - core, 0, keepdims=False), ("rep", "tp"), crossed
-    )
-    layer_out = jnp.where(
-        core == 0,
-        jnp.concatenate([left, right], axis=1),
-        jnp.concatenate([right, left], axis=1),
-    ).reshape(num_steps, num_rows, 2 * out_cols)
-
-    cache_moved, held = unpack_kernel(
-        core, unpack_table, kv_cache, lent, leg_one, leg_two, partial_out
-    )
-
 
     def more(state):
         start, moved, other = state
@@ -772,10 +773,31 @@
         return start + LATER, moved, other
 
     _, cache_moved, held = lax.while_loop(
-        lambda state: state[0] < most, more, (first, cache_moved, held)
+        lambda state: state[0] < late_pack[4, 0], more, (first, cache_moved, held)
     )
     returned = lax.ppermute(held, "rep", other_core)
     cache_moved = finish_kernel(core, returned, cache_moved)
+    summed = jnp.sum(exchanged.astype(jnp.float32), axis=0).astype(jnp.bfloat16)
+    summed = summed.reshape(2, row_total, out_cols)
+    straight = [
+        (r * tps + t, (2 * t + r % 2) * tps + r // 2) for r in range(reps) for t in range(tps)
+    ]
+    crossed = [
+        (r * tps + t, (2 * t + 1 - r % 2) * tps + r // 2) for r in range(reps) for t in range(tps)
+    ]
+    left = lax.ppermute(
+        lax.dynamic_index_in_dim(summed, core, 0, keepdims=False), ("rep", "tp"), straight
+    )
+    right = lax.ppermute(
+        lax.dynamic_index_in_dim(summed, 1 - core, 0, keepdims=False), ("rep", "tp"), crossed
+    )
+    left, right, cache_moved = lax.optimization_barrier((left, right, cache_moved))
+    layer_out = jnp.where(
+        core == 0,
+        jnp.concatenate([left, right], axis=1),
+        jnp.concatenate([right, left], axis=1),
+    ).reshape(num_steps, num_rows, 2 * out_cols)
+
     return (layer_out, cache_moved)
 
 

time: 179 us -> 176 us (0.983)
  starting transfers between devices: 67.2 us -> 42.8 us
  waiting for transfers between devices: 53.9 us -> 76.5 us
  Pallas kernels: 36.9 us -> 35.1 us
    ppermute x3, waiting for transfers between devices: 0.01 us -> 17.5 us  [per_device(): lax.ppermute(piece, 'rep', line_pairs(reps, line, 0))]
    ppermute x3, waiting for transfers between devices: 0.01 us -> 12.7 us  [per_device(): lax.ppermute(piece, 'rep', line_pairs(reps, line, 1))]
    all_to_all x1, starting transfers between devices: 17.6 us -> 6.29 us  [per_device(): lax.all_to_all(pair_sum, 'rep', split_axis=0, concat_axis=0, tiled=True,...]
    all_to_all x1, starting transfers between devices: 16.6 us -> 5.56 us  [per_device(): lax.all_to_all(jnp.broadcast_to(kept[None], (chips,) + kept.shape), 'rep'...]
    ppermute x1, waiting for transfers between devices: 10.5 us -> 0.01 us  [per_device(): lax.ppermute(lax.dynamic_index_in_dim(summed, core, 0, keepdims=False), (...]
    all_to_all x1, waiting for transfers between devices: 14.4 us -> 7.54 us  [per_device(): lax.all_to_all(jnp.broadcast_to(kept[None], (chips,) + kept.shape), 'rep'...]
    ppermute x1, waiting for transfers between devices: 1.4 us -> 7.77 us  [per_device(): lax.ppermute(lax.dynamic_index_in_dim(summed, 1 - core, 0, keepdims=False...]
    all_to_all x1, waiting for transfers between devices: 6.35 us -> 0.01 us  [per_device(): lax.all_to_all(pair_sum, 'rep', split_axis=0, concat_axis=0, tiled=True,...]
  transfers between devices with their start and end apart: 18 -> 18, of which waited for: 10 -> 12; matrix products, arithmetic and copies ran while one was open for 5% -> 4% of each run, Pallas kernels for 17% -> 18%
where the time goes in v6:
time: 176 us; the launch traced here: 174 us
  waiting for transfers between devices  76.5 us (43%)
  starting transfers between devices  42.8 us (24%)
  Pallas kernels  35.1 us (20%)
  local copies, waits for them, and re-layouts  10.1 us (6%)
  other arithmetic  6.61 us (4%)
  between operations  2.17 us (1%)
    ppermute x3, waiting for transfers between devices, per_device(): lax.ppermute(piece, 'rep', line_pairs(reps, line, 0))  17.5 us
    all_to_all x1, waiting for transfers between devices, per_device(): lax.all_to_all(slabs, 'rep', split_axis=0, concat_axis=0, tiled=True)  12.7 us
    ppermute x3, waiting for transfers between devices, per_device(): lax.ppermute(piece, 'rep', line_pairs(reps, line, 1))  12.7 us
    pallas_call x2, Pallas kernels, pack_kernel(): pl.pallas_call(functools.partial(pack_body, len(lines)), out_shape=[line]...  9.69 us
    all_to_all x1, waiting for transfers between devices, per_device(): lax.all_to_all(partial_out.reshape(tps, all_rows // tps, out_cols), 'tp',...  8.41 us
    ppermute x1, waiting for transfers between devices, per_device(): lax.ppermute(lax.dynamic_index_in_dim(summed, 1 - core, 0, keepdims=False...  7.77 us
    all_to_all x1, waiting for transfers between devices, per_device(): lax.all_to_all(jnp.broadcast_to(kept[None], (chips,) + kept.shape), 'rep'...  7.54 us
    all_to_all x1, starting transfers between devices, per_device(): lax.all_to_all(slabs, 'rep', split_axis=0, concat_axis=0, tiled=True)  7.09 us
  transfers between devices with their start and end apart: 18, of which 12 were waited for; matrix products, arithmetic and copies ran while one was open for 4% of the time, Pallas kernels for 18%

profile of v6, /device:TPU:17, one launch (start us, length us, event | category | flops | bytes accessed | tf_op | source)
XLA Modules:
  0.0 174.0 jit_solution(14526089536163260860)
XLA Ops:
  5.4 2.1 %norm_rows.1 = bf16[16,80,512]{2,1,0:T(8,128)(2,1)} custom-call(s32[16]{0:T(128)S(1)} %copy-done.10, s32[16]{0:T(128)S(1)} %copy-done.8, bf16[64,8192]{1,0:T(8,128)(2,1)S(1)} %bitcast.69, bf16[8192]{0:T(1024)(128)(2,1)S(1)} %copy-done.7), custom_call_target="tpu_custom_call" | custom-call | bytes 4194304 | tf_op jit(solution)/shard_map/norm_rows/pallas_call | solution.py:373
  7.6 3.5 %collective-permute-done = s32[2,16]{1,0:T(2,128)S(1)} collective-permute-done((s32[2,16]{1,0:T(2,128)S(1)}, s32[2,16]{1,0:T(2,128)S(1)}, u32[]{:S(2)}, u32[]{:S(2)}) %collective-permute-start) | collective-permute-done | bytes 160 | tf_op jit(solution)/shard_map/ppermute | solution.py:624
  11.2 7.1 %all-to-all-start.1 = ((bf16[16,80,512]{2,1,0:T(8,128)(2,1)}), bf16[16,80,512]{2,1,0:T(8,128)(2,1)S(1)}, u32[]{:S(2)}, u32[]{:S(2)}) async-start(bf16[16,80,512]{2,1,0:T(8,128)(2,1)} %norm_rows.1), calls=%async_computation.1 | async-start | bytes 2621440 | tf_op jit(solution)/shard_map/all_to_all | solution.py:629
  19.3 4.4 %pack_blocks.2 = (bf16[38,128,128]{2,1,0:T(8,128)(2,1)}, bf16[38,128,128]{2,1,0:T(8,128)(2,1)}, bf16[38,128,128]{2,1,0:T(8,128)(2,1)}) custom-call(s32[1]{0:T(128)} %bitcast.3.core.scalars, s32[4,32]{1,0:T(4,128)} %pad_add_fusion.9.table, bf16[16,2,768,128]{3,2,1,0:T(8,128)(2,1)} %cache.7, bf16[16,2,768,128]{3,2,1,0:T(8,128)(2,1)} %collective-permute-done.1.lent), custom_call_target="tpu_custom_call" | custom-call | bytes 1024 | tf_op jit(solution)/shard_map/pack_blocks/pallas_call | solution.py:146
  23.7 12.7 %all-to-all-done.1.slabs = bf16[16,80,512]{2,1,0:T(8,128)(2,1)S(1)} async-done(((bf16[16,80,512]{2,1,0:T(8,128)(2,1)}), bf16[16,80,512]{2,1,0:T(8,128)(2,1)S(1)}, u32[]{:S(2)}, u32[]{:S(2)}) %all-to-all-start.1) | async-done | bytes 1310752 | tf_op jit(solution)/shard_map/all_to_all | solution.py:629
  36.5 1.3 copy-done.2
  37.8 1.4 project_rows.2
  41.1 1.9 %collective-permute-start.3 = (bf16[38,128,128]{2,1,0:T(8,128)(2,1)}, bf16[38,128,128]{2,1,0:T(8,128)(2,1)}, u32[]{:S(2)}, u32[]{:S(2)}) collective-permute-start(bf16[38,128,128]{2,1,0:T(8,128)(2,1)} %get-tuple-element.75.rest_0_), channel_id=1, source_target_pairs={{0,32},{8,24},{16,48},{24,8},{32,64},{40,56},{48,80},{56,40},{64,9... | collective-permute-start | bytes 3735560 | tf_op jit(solution)/shard_map/ppermute | solution.py:653
  44.1 1.8 %collective-permute-start.5 = (bf16[38,128,128]{2,1,0:T(8,128)(2,1)}, bf16[38,128,128]{2,1,0:T(8,128)(2,1)}, u32[]{:S(2)}, u32[]{:S(2)}) collective-permute-start(bf16[38,128,128]{2,1,0:T(8,128)(2,1)} %get-tuple-element.77), channel_id=1, source_target_pairs={{0,64},{16,80},{32,96},{48,112},{64,0},{80,16},{96,32},{112,48},{1... | collective-permute-start | bytes 3735560 | tf_op jit(solution)/shard_map/ppermute | solution.py:653
  45.9 1.6 collective-permute-start.2
  50.5 3.7 %project_rows.3 = bf16[8,64,1280]{2,1,0:T(8,128)(2,1)} custom-call(s32[1]{0:T(128)} %bitcast.3.core.scalars, bf16[16,80,512]{2,1,0:T(8,128)(2,1)S(1)} %all-to-all-done.1.slabs, bf16[512,1024]{1,0:T(8,128)(2,1)S(1)} %copy-done, bf16[512,256]{1,0:T(8,128)(2,1)S(1)} %bitcast.68, bf16[8,64,1280]{2,1,0:T(8,128)(2,1)} %collective-permute-done.2.rest_0_), custom_call_target="tpu_custom_call" | custom-call | bytes 4194304 | tf_op jit(solution)/shard_map/project_rows/pallas_call | solution.py:416
  54.2 6.3 %all-to-all-start.2 = ((bf16[8,64,1280]{2,1,0:T(8,128)(2,1)}), bf16[8,64,1280]{2,1,0:T(8,128)(2,1)S(1)}, u32[]{:S(2)}, u32[]{:S(2)}) async-start(bf16[8,64,1280]{2,1,0:T(8,128)(2,1)} %project_rows.3), calls=%async_computation.2 | async-start | bytes 2621440 | tf_op jit(solution)/shard_map/all_to_all | solution.py:662
  62.7 17.5 %collective-permute-done.4.rest_1_ = bf16[38,128,128]{2,1,0:T(8,128)(2,1)} collective-permute-done((bf16[38,128,128]{2,1,0:T(8,128)(2,1)}, bf16[38,128,128]{2,1,0:T(8,128)(2,1)}, u32[]{:S(2)}, u32[]{:S(2)}) %collective-permute-start.4) | collective-permute-done | bytes 1245216 | tf_op jit(solution)/shard_map/ppermute | solution.py:653
  80.3 5.3 %pack_blocks.3 = (bf16[38,128,128]{2,1,0:T(8,128)(2,1)}, bf16[38,128,128]{2,1,0:T(8,128)(2,1)}, bf16[38,128,128]{2,1,0:T(8,128)(2,1)}) custom-call(s32[1]{0:T(128)} %bitcast.3.core.scalars, s32[4,64]{1,0:T(4,128)} %select_reduce_fusion.2.table, bf16[16,2,768,128]{3,2,1,0:T(8,128)(2,1)} %cache.7, bf16[16,2,768,128]{3,2,1,0:T(8,128)(2,1)} %collective-permute-done.1.lent, ...), custom_call_target="tpu_custom_call" | custom-call | bytes 8388608 | tf_op jit(solution)/shard_map/pack_blocks/pallas_call | solution.py:146
  85.9 2.4 %collective-permute-start.8 = (bf16[38,128,128]{2,1,0:T(8,128)(2,1)}, bf16[38,128,128]{2,1,0:T(8,128)(2,1)}, u32[]{:S(2)}, u32[]{:S(2)}) collective-permute-start(bf16[38,128,128]{2,1,0:T(8,128)(2,1)} %get-tuple-element.87), channel_id=1, source_target_pairs={{0,16},{8,104},{16,0},{24,120},{32,48},{40,8},{48,32},{56,24},{64,... | collective-permute-start | bytes 3735560 | tf_op jit(solution)/shard_map/ppermute | solution.py:724
  88.3 3.2 %collective-permute-start.9 = (bf16[38,128,128]{2,1,0:T(8,128)(2,1)}, bf16[38,128,128]{2,1,0:T(8,128)(2,1)}, u32[]{:S(2)}, u32[]{:S(2)}) collective-permute-start(bf16[38,128,128]{2,1,0:T(8,128)(2,1)} %get-tuple-element.88), channel_id=1, source_target_pairs={{8,72},{24,88},{40,104},{56,120},{72,8},{88,24},{104,40},{120,56},... | collective-permute-start | bytes 3735560 | tf_op jit(solution)/shard_map/ppermute | solution.py:724
  92.8 1.3 copy-done.3
  94.0 5.3 %attend_old_place.1 = (bf16[64,512]{1,0:T(8,128)(2,1)S(1)}, bf16[64,512]{1,0:T(8,128)(2,1)S(1)}) custom-call(s32[1]{0:T(128)} %bitcast.3.core.scalars, s32[16]{0:T(128)S(1)} %copy-done.9, bf16[8,64,1280]{2,1,0:T(8,128)(2,1)S(1)} %all-to-all-done.2.sums, bf16[16,2,768,128]{3,2,1,0:T(8,128)(2,1)} %cache.7, bf16[38,128,128]{2,1,0:T(8,128)(2,1)S(1)} %copy-done.3, ...), custom_call_target="tpu_custom_call" | custom-call | bytes 16777216 | tf_op jit(solution)/shard_map/attend_old_place/pallas_call | solution.py:536
  101.8 5.6 %all-to-all-start.3 = ((bf16[8,2,64,512]{3,2,1,0:T(8,128)(2,1)}), bf16[8,2,64,512]{3,2,1,0:T(8,128)(2,1)S(1)}, u32[]{:S(2)}, u32[]{:S(2)}) async-start(bf16[8,2,64,512]{3,2,1,0:T(8,128)(2,1)} %broadcast_in_dim.316), calls=%async_computation.3 | async-start | bytes 2097152 | tf_op jit(solution)/shard_map/all_to_all | solution.py:738
  107.4 8.3 %collective-permute-done.7.rest_3_ = bf16[38,128,128]{2,1,0:T(8,128)(2,1)} collective-permute-done((bf16[38,128,128]{2,1,0:T(8,128)(2,1)}, bf16[38,128,128]{2,1,0:T(8,128)(2,1)}, u32[]{:S(2)}, u32[]{:S(2)}) %collective-permute-start.7) | collective-permute-done | bytes 1245216 | tf_op jit(solution)/shard_map/ppermute | solution.py:724
  115.6 4.4 %collective-permute-done.9.rest_5_ = bf16[38,128,128]{2,1,0:T(8,128)(2,1)} collective-permute-done((bf16[38,128,128]{2,1,0:T(8,128)(2,1)}, bf16[38,128,128]{2,1,0:T(8,128)(2,1)}, u32[]{:S(2)}, u32[]{:S(2)}) %collective-permute-start.9) | collective-permute-done | bytes 1245216 | tf_op jit(solution)/shard_map/ppermute | solution.py:724
  120.0 7.5 %all-to-all-done.3 = bf16[8,2,64,512]{3,2,1,0:T(8,128)(2,1)S(1)} async-done(((bf16[8,2,64,512]{3,2,1,0:T(8,128)(2,1)}), bf16[8,2,64,512]{3,2,1,0:T(8,128)(2,1)S(1)}, u32[]{:S(2)}, u32[]{:S(2)}) %all-to-all-start.3) | async-done | bytes 1048608 | tf_op jit(solution)/shard_map/all_to_all | solution.py:738
  127.6 2.7 %collective-permute-done.10.far = bf16[16,64,512]{2,1,0:T(8,128)(2,1)S(1)} collective-permute-done((bf16[16,64,512]{2,1,0:T(8,128)(2,1)S(1)}, bf16[16,64,512]{2,1,0:T(8,128)(2,1)S(1)}, u32[]{:S(2)}, u32[]{:S(2)}) %collective-permute-start.10) | collective-permute-done | bytes 1048608 | tf_op jit(solution)/shard_map/ppermute | solution.py:747
  130.2 3.0 %output_rows.1.rest_6_ = bf16[16,64,512]{2,1,0:T(8,128)(2,1)} custom-call(s32[1]{0:T(128)} %bitcast.3.core.scalars, bf16[16,80,512]{2,1,0:T(8,128)(2,1)S(1)} %all-to-all-done.1.slabs, bf16[16,64,512]{2,1,0:T(8,128)(2,1)S(1)} %bitcast.66, bf16[16,64,512]{2,1,0:T(8,128)(2,1)S(1)} %collective-permute-done.10.far, bf16[1024,512]{1,0:T(8,128)(2,1)S(1)} %copy-done.5), custom_call_target="tpu_custom_call" | custom-call | bytes 6291456 | tf_op jit(solution)/shard_map/output_rows/pallas_call | solution.py:594
  133.3 5.8 %all-to-all-start.4 = ((bf16[8,128,512]{2,1,0:T(8,128)(2,1)}), bf16[8,128,512]{2,1,0:T(8,128)(2,1)S(1)}, u32[]{:S(2)}, u32[]{:S(2)}) async-start(bf16[8,128,512]{2,1,0:T(8,128)(2,1)} %bitcast.22), calls=%async_computation.4 | async-start | bytes 2097152 | tf_op jit(solution)/shard_map/all_to_all | solution.py:753
  139.0 7.0 %unpack_blocks.1 = (bf16[16,2,768,128]{3,2,1,0:T(8,128)(2,1)}, bf16[16,768,128]{2,1,0:T(8,128)(2,1)}) custom-call(s32[1]{0:T(128)} %bitcast.3.core.scalars, s32[3,32]{1,0:T(4,128)} %copy-done.6, bf16[16,2,768,128]{3,2,1,0:T(8,128)(2,1)} %cache.7, bf16[16,2,768,128]{3,2,1,0:T(8,128)(2,1)} %collective-permute-done.1.lent, ...), custom_call_target="tpu_custom_call" | custom-call | bytes 10485760 | tf_op jit(solution)/shard_map/unpack_blocks/pallas_call | solution.py:196
  146.0 8.4 %all-to-all-done.4 = bf16[8,128,512]{2,1,0:T(8,128)(2,1)S(1)} async-done(((bf16[8,128,512]{2,1,0:T(8,128)(2,1)}), bf16[8,128,512]{2,1,0:T(8,128)(2,1)S(1)}, u32[]{:S(2)}, u32[]{:S(2)}) %all-to-all-start.4) | async-done | bytes 1048608 | tf_op jit(solution)/shard_map/all_to_all | solution.py:753
  155.7 1.4 collective-permute-start.13
  157.2 3.4 %collective-permute-start.11 = (bf16[64,512]{1,0:T(8,128)(2,1)S(1)}, bf16[64,512]{1,0:T(8,128)(2,1)S(1)}, u32[]{:S(2)}, u32[]{:S(2)}) collective-permute-start(bf16[64,512]{1,0:T(8,128)(2,1)S(1)} %get-tuple-element.159), channel_id=1, source_target_pairs={{0,0},{1,16},{2,32},{3,48},{4,64},{5,80},{6,96},{7,112},{8,8},{9,2... | collective-permute-start | bytes 196616 | tf_op jit(solution)/shard_map/ppermute | solution.py:788
  160.8 1.8 %collective-permute-done.13.returned = bf16[16,768,128]{2,1,0:T(8,128)(2,1)} collective-permute-done((bf16[16,768,128]{2,1,0:T(8,128)(2,1)}, bf16[16,768,128]{2,1,0:T(8,128)(2,1)}, u32[]{:S(2)}, u32[]{:S(2)}) %collective-permute-start.13) | collective-permute-done | bytes 3145760 | tf_op jit(solution)/shard_map/ppermute | solution.py:778
  162.6 2.9 %put_other_kind.1 = bf16[16,2,768,128]{3,2,1,0:T(8,128)(2,1)} custom-call(s32[1]{0:T(128)} %bitcast.3.core.scalars, bf16[16,768,128]{2,1,0:T(8,128)(2,1)} %collective-permute-done.13.returned, bf16[16,2,768,128]{3,2,1,0:T(8,128)(2,1)} %get-tuple-element.95._), custom_call_target="tpu_custom_call", output_to_operand_aliasing={{}: (2, {})} | custom-call | bytes 6291456 | tf_op jit(solution)/shard_map/put_other_kind/pallas_call | solution.py:329
  165.5 7.8 %collective-permute-done.12 = bf16[64,512]{1,0:T(8,128)(2,1)S(1)} collective-permute-done((bf16[64,512]{1,0:T(8,128)(2,1)S(1)}, bf16[64,512]{1,0:T(8,128)(2,1)S(1)}, u32[]{:S(2)}, u32[]{:S(2)}) %collective-permute-start.12) | collective-permute-done | bytes 65568 | tf_op jit(solution)/shard_map/ppermute | solution.py:791
  (93 shorter events, 19.4 us)
Async XLA Ops:
  0.6 18.6 %collective-permute-start.1 = (bf16[16,2,768,128]{3,2,1,0:T(8,128)(2,1)}, bf16[16,2,768,128]{3,2,1,0:T(8,128)(2,1)}, u32[]{:S(2)}, u32[]{:S(2)}) collective-permute-start(bf16[16,2,768,128]{3,2,1,0:T(8,128)(2,1)} %cache.7), channel_id=1, source_target_pairs={{0,8},{8,0},{16,24},{24,16},{32,40},{40,32},{48,56},{56,48},{64,72... | collective-permute-start | bytes 18874376 | tf_op jit(solution)/shard_map/ppermute | solution.py:628
  2.1 9.0 %collective-permute-start = (s32[2,16]{1,0:T(2,128)S(1)}, s32[2,16]{1,0:T(2,128)S(1)}, u32[]{:S(2)}, u32[]{:S(2)}) collective-permute-start(s32[2,16]{1,0:T(2,128)S(1)} %pad_add_fusion.10), channel_id=1, source_target_pairs={{0,8},{8,0},{16,24},{24,16},{32,40},{40,32},{48,56},{56,48},{64,72... | collective-permute-start | bytes 392 | tf_op jit(solution)/shard_map/ppermute | solution.py:624
  2.2 1.2 copy-start.4
  3.4 0.7 copy-start.7
  4.1 0.7 copy-start.8
  4.8 0.7 copy-start.10
  11.2 25.3 %all-to-all-start.1 = ((bf16[16,80,512]{2,1,0:T(8,128)(2,1)}), bf16[16,80,512]{2,1,0:T(8,128)(2,1)S(1)}, u32[]{:S(2)}, u32[]{:S(2)}) async-start(bf16[16,80,512]{2,1,0:T(8,128)(2,1)} %norm_rows.1), calls=%async_computation.1 | async-start | bytes 2621440 | tf_op jit(solution)/shard_map/all_to_all | solution.py:629
  19.2 4.4 %copy-start.12 = (bf16[512,2,128]{2,1,0:T(2,128)(2,1)S(1)}, bf16[512,2,128]{2,1,0:T(2,128)(2,1)}, u32[]{:S(2)}) copy-start(bf16[512,2,128]{2,1,0:T(2,128)(2,1)} %param.13) | copy-start | bytes 786436
  19.3 17.2 %copy-start = (bf16[512,1024]{1,0:T(8,128)(2,1)S(1)}, bf16[512,1024]{1,0:T(8,128)(2,1)}, u32[]{:S(2)}) copy-start(bf16[512,1024]{1,0:T(8,128)(2,1)} %w_query.3) | copy-start | bytes 3145732
  36.5 1.3 copy-start.2
  39.1 1.1 copy-start.1
  41.1 21.6 %collective-permute-start.3 = (bf16[38,128,128]{2,1,0:T(8,128)(2,1)}, bf16[38,128,128]{2,1,0:T(8,128)(2,1)}, u32[]{:S(2)}, u32[]{:S(2)}) collective-permute-start(bf16[38,128,128]{2,1,0:T(8,128)(2,1)} %get-tuple-element.75.rest_0_), channel_id=1, source_target_pairs={{0,32},{8,24},{16,48},{24,8},{32,64},{40,56},{48,80},{56,40},{64,9... | collective-permute-start | bytes 3735560 | tf_op jit(solution)/shard_map/ppermute | solution.py:653
  43.0 37.2 %collective-permute-start.4 = (bf16[38,128,128]{2,1,0:T(8,128)(2,1)}, bf16[38,128,128]{2,1,0:T(8,128)(2,1)}, u32[]{:S(2)}, u32[]{:S(2)}) collective-permute-start(bf16[38,128,128]{2,1,0:T(8,128)(2,1)} %get-tuple-element.76), channel_id=1, source_target_pairs={{0,96},{8,24},{16,112},{24,8},{32,0},{40,56},{48,16},{56,40},{64,3... | collective-permute-start | bytes 3735560 | tf_op jit(solution)/shard_map/ppermute | solution.py:653
  44.1 36.1 %collective-permute-start.5 = (bf16[38,128,128]{2,1,0:T(8,128)(2,1)}, bf16[38,128,128]{2,1,0:T(8,128)(2,1)}, u32[]{:S(2)}, u32[]{:S(2)}) collective-permute-start(bf16[38,128,128]{2,1,0:T(8,128)(2,1)} %get-tuple-element.77), channel_id=1, source_target_pairs={{0,64},{16,80},{32,96},{48,112},{64,0},{80,16},{96,32},{112,48},{1... | collective-permute-start | bytes 3735560 | tf_op jit(solution)/shard_map/ppermute | solution.py:653
  45.9 4.6 %collective-permute-start.2 = (bf16[8,64,1280]{2,1,0:T(8,128)(2,1)}, bf16[8,64,1280]{2,1,0:T(8,128)(2,1)}, u32[]{:S(2)}, u32[]{:S(2)}) collective-permute-start(bf16[8,64,1280]{2,1,0:T(8,128)(2,1)} %copy-done.1), channel_id=1, source_target_pairs={{0,8},{8,0},{16,24},{24,16},{32,40},{40,32},{48,56},{56,48},{64,72... | collective-permute-start | bytes 3932168 | tf_op jit(solution)/shard_map/ppermute | solution.py:660
  54.2 38.5 %all-to-all-start.2 = ((bf16[8,64,1280]{2,1,0:T(8,128)(2,1)}), bf16[8,64,1280]{2,1,0:T(8,128)(2,1)S(1)}, u32[]{:S(2)}, u32[]{:S(2)}) async-start(bf16[8,64,1280]{2,1,0:T(8,128)(2,1)} %project_rows.3), calls=%async_computation.2 | async-start | bytes 2621440 | tf_op jit(solution)/shard_map/all_to_all | solution.py:662
  62.7 30.0 %copy-start.9 = (s32[16]{0:T(128)S(1)}, s32[16]{0:T(128)}, u32[]{:S(2)}) copy-start(s32[16]{0:T(128)} %counts.3) | copy-start | bytes 196
  85.5 30.1 %collective-permute-start.7 = (bf16[38,128,128]{2,1,0:T(8,128)(2,1)}, bf16[38,128,128]{2,1,0:T(8,128)(2,1)}, u32[]{:S(2)}, u32[]{:S(2)}) collective-permute-start(bf16[38,128,128]{2,1,0:T(8,128)(2,1)} %get-tuple-element.81.rest_0_), channel_id=1, source_target_pairs={{0,16},{8,40},{16,0},{24,56},{32,48},{40,72},{48,32},{56,88},{64,8... | collective-permute-start | bytes 3735560 | tf_op jit(solution)/shard_map/ppermute | solution.py:724
  85.9 29.7 %collective-permute-start.8 = (bf16[38,128,128]{2,1,0:T(8,128)(2,1)}, bf16[38,128,128]{2,1,0:T(8,128)(2,1)}, u32[]{:S(2)}, u32[]{:S(2)}) collective-permute-start(bf16[38,128,128]{2,1,0:T(8,128)(2,1)} %get-tuple-element.87), channel_id=1, source_target_pairs={{0,16},{8,104},{16,0},{24,120},{32,48},{40,8},{48,32},{56,24},{64,... | collective-permute-start | bytes 3735560 | tf_op jit(solution)/shard_map/ppermute | solution.py:724
  88.3 31.8 %collective-permute-start.9 = (bf16[38,128,128]{2,1,0:T(8,128)(2,1)}, bf16[38,128,128]{2,1,0:T(8,128)(2,1)}, u32[]{:S(2)}, u32[]{:S(2)}) collective-permute-start(bf16[38,128,128]{2,1,0:T(8,128)(2,1)} %get-tuple-element.88), channel_id=1, source_target_pairs={{8,72},{24,88},{40,104},{56,120},{72,8},{88,24},{104,40},{120,56},... | collective-permute-start | bytes 3735560 | tf_op jit(solution)/shard_map/ppermute | solution.py:724
  92.7 6.7 %copy-start.6 = (s32[3,32]{1,0:T(4,128)}, s32[3,32]{1,0:T(4,128)S(1)}, u32[]{:S(2)}) copy-start(s32[3,32]{1,0:T(4,128)S(1)} %select_reduce_fusion.11.rest_1_.table) | copy-start | bytes 1156
  92.7 1.3 copy-start.3
  99.4 1.3 collective-permute-start.6
  101.8 28.4 %copy-start.5 = (bf16[1024,512]{1,0:T(8,128)(2,1)S(1)}, bf16[1024,512]{1,0:T(8,128)(2,1)}, u32[]{:S(2)}) copy-start(bf16[1024,512]{1,0:T(8,128)(2,1)} %weight.1) | copy-start | bytes 3145732
  101.8 25.8 %all-to-all-start.3 = ((bf16[8,2,64,512]{3,2,1,0:T(8,128)(2,1)}), bf16[8,2,64,512]{3,2,1,0:T(8,128)(2,1)S(1)}, u32[]{:S(2)}, u32[]{:S(2)}) async-start(bf16[8,2,64,512]{3,2,1,0:T(8,128)(2,1)} %broadcast_in_dim.316), calls=%async_computation.3 | async-start | bytes 2097152 | tf_op jit(solution)/shard_map/all_to_all | solution.py:738
  127.6 2.7 %collective-permute-start.10 = (bf16[16,64,512]{2,1,0:T(8,128)(2,1)S(1)}, bf16[16,64,512]{2,1,0:T(8,128)(2,1)S(1)}, u32[]{:S(2)}, u32[]{:S(2)}) collective-permute-start(bf16[16,64,512]{2,1,0:T(8,128)(2,1)S(1)} %bitcast.65), channel_id=1, source_target_pairs={{0,8},{8,0},{16,24},{24,16},{32,40},{40,32},{48,56},{56,48},{64,72... | collective-permute-start | bytes 3145736 | tf_op jit(solution)/shard_map/ppermute | solution.py:747
  133.3 21.2 %all-to-all-start.4 = ((bf16[8,128,512]{2,1,0:T(8,128)(2,1)}), bf16[8,128,512]{2,1,0:T(8,128)(2,1)S(1)}, u32[]{:S(2)}, u32[]{:S(2)}) async-start(bf16[8,128,512]{2,1,0:T(8,128)(2,1)} %bitcast.22), calls=%async_computation.4 | async-start | bytes 2097152 | tf_op jit(solution)/shard_map/all_to_all | solution.py:753
  155.7 7.0 %collective-permute-start.13 = (bf16[16,768,128]{2,1,0:T(8,128)(2,1)}, bf16[16,768,128]{2,1,0:T(8,128)(2,1)}, u32[]{:S(2)}, u32[]{:S(2)}) collective-permute-start(bf16[16,768,128]{2,1,0:T(8,128)(2,1)} %get-tuple-element.94), channel_id=1, source_target_pairs={{0,8},{8,0},{16,24},{24,16},{32,40},{40,32},{48,56},{56,48},{64,72... | collective-permute-start | bytes 9437192 | tf_op jit(solution)/shard_map/ppermute | solution.py:778
  157.2 8.3 %collective-permute-start.11 = (bf16[64,512]{1,0:T(8,128)(2,1)S(1)}, bf16[64,512]{1,0:T(8,128)(2,1)S(1)}, u32[]{:S(2)}, u32[]{:S(2)}) collective-permute-start(bf16[64,512]{1,0:T(8,128)(2,1)S(1)} %get-tuple-element.159), channel_id=1, source_target_pairs={{0,0},{1,16},{2,32},{3,48},{4,64},{5,80},{6,96},{7,112},{8,8},{9,2... | collective-permute-start | bytes 196616 | tf_op jit(solution)/shard_map/ppermute | solution.py:788
  160.6 12.7 %collective-permute-start.12 = (bf16[64,512]{1,0:T(8,128)(2,1)S(1)}, bf16[64,512]{1,0:T(8,128)(2,1)S(1)}, u32[]{:S(2)}, u32[]{:S(2)}) collective-permute-start(bf16[64,512]{1,0:T(8,128)(2,1)S(1)} %get-tuple-element.158), channel_id=1, source_target_pairs={{0,8},{1,24},{2,40},{3,56},{4,72},{5,88},{6,104},{7,120},{8,0},{9,... | collective-permute-start | bytes 196616 | tf_op jit(solution)/shard_map/ppermute | solution.py:791
